TPU v7x, 512 devices: a whole 4x8x8 slice. The times are simulated.
512 devices in a mesh: seg: 16 (over y, core), vid: 16 (over z, x_hi), tp: 2 (over x_lo).
Axes of the slice: x: 4 (x_hi: 2, x_lo: 2; x = x_hi * 2 + x_lo), y: 8, z: 8, core: 2. Of those that a mesh axis runs over, the one named last changes fastest.
Arguments:
- tokens: bfloat16 [16, 8192, 2048], P('vid', 'seg', 'tp'), may hold values from -400 to 400
- key_weight: bfloat16 [2048, 2048], P('vid', 'tp'), may hold values from -0.125 to 0.125
- query_weight: bfloat16 [2048, 2048], P('vid', 'tp'), may hold values from -0.125 to 0.125
- latent_queries: bfloat16 [128, 2048], P(None, 'tp'), may hold values from -400 to 400
- init_memory: float32 [16, 128, 2048], P('vid', None, 'tp'), may hold values from -6 to 6
- forget: float32 [16, 16, 2048], P('vid', 'seg', 'tp'), may hold values from 0 to 1
Outputs:
- mixed: bfloat16 [16, 8192, 2048], P('vid', 'seg', 'tp')
- memory: float32 [16, 2048, 2048], P('vid', 'seg', 'tp')
All inputs are finite; a program needn't handle non-finite values.
Results may differ from a plain program's by a relative error of at most 0.015.
The roundings to bfloat16 on the way count: a program that leaves them out, or rounds other values in their place, can miss the bound.
Values may be sent and summed in bfloat16 or wider, within the bound.
No kernel may reach another device: no remote copies, remote signals or barrier semaphores. Data moves between devices by JAX's collectives and lax.ppermute only.
A program may use at most 64 MiB of HBM per device.

v0:
```python
import jax
import jax.numpy as jnp
from jax import lax
from jax.sharding import PartitionSpec as P

HEAD = 128


def in_order(blocks, dim):
    blocks = jnp.moveaxis(blocks, 0, dim)
    lengths = blocks.shape
    return blocks.reshape(*lengths[:dim], lengths[dim] * lengths[dim + 1], *lengths[dim + 2 :])


def sent_to_all(shard, axis):
    copies = jnp.broadcast_to(shard, (lax.axis_size(axis), *shard.shape))
    return lax.all_to_all(copies, axis, split_axis=0, concat_axis=0, tiled=True)


def gather_directly(shard, axis, dim):
    return in_order(sent_to_all(shard, axis), dim)


def in_one_piece(arrays, axis, dim, along):
    ends, at = ([], 0)
    for a in arrays[:-1]:
        at += a.shape[along]
        ends.append(at)
    both = jnp.concatenate(arrays, axis=along)
    return tuple(jnp.split(lax.all_gather(both, axis, axis=dim, tiled=True), ends, axis=along))


def entering(shard, axis, combine, identity):
    length, place = (lax.axis_size(axis), lax.axis_index(axis))
    everything = jax.tree.map(lambda part: lax.all_gather(part, axis), shard)
    start = jax.tree.map(
        lambda part, zero: jnp.broadcast_to(jnp.asarray(zero, part.dtype), part.shape),
        shard,
        identity,
    )

    def lap(k, before):
        reached = k < place
        new = combine(before, jax.tree.map(lambda part: part[k], everything))
        return jax.tree.map(lambda a, b: jnp.where(reached, a, b), new, before)

    return lax.fori_loop(0, length, lap, start)


def trailing_softmax(scores):
    top = jnp.max(scores, axis=-1, keepdims=True)
    expo = jnp.exp(scores - top)
    return expo / jnp.sum(expo, axis=-1, keepdims=True)


def add_rows(left, piece):
    return jnp.dot(left, piece, preferred_element_type=jnp.float32)


def shards(tokens, key_weight, query_weight, latent_queries, init_memory, forget):
    local = tokens[0]
    width = local.shape[1]
    heads = width // HEAD
    latents = latent_queries.shape[0]
    whole = gather_directly(local, "tp", 1)
    pieces = in_one_piece((key_weight, query_weight), "vid", 0, 1)
    keys_full = add_rows(whole, pieces[0])
    queries_full = add_rows(whole, pieces[1])
    scale = 1.0 / jnp.sqrt(jnp.float32(HEAD))
    keys = keys_full.astype(jnp.bfloat16).reshape(-1, heads, HEAD)
    queries = queries_full.astype(jnp.bfloat16).reshape(-1, heads, HEAD)
    values = local.reshape(-1, heads, HEAD)
    latent = latent_queries.reshape(latents, heads, HEAD)
    scores = jnp.einsum("mhe,the->hmt", latent, keys, preferred_element_type=jnp.float32) * scale
    weight_params = trailing_softmax(scores).astype(jnp.bfloat16)
    update = jnp.einsum(
        "hmt,the->mhe", weight_params, values, preferred_element_type=jnp.float32
    ).reshape(latents, width)
    retain = forget[0]
    initial_memory = init_memory[0]

    def combine(earlier, later):
        return (earlier[0] * later[0], later[0] * earlier[1] + later[1])

    prior_retain, prior_update = entering(
        (retain, update), "seg", combine, (jnp.ones_like(retain), jnp.zeros_like(update))
    )
    memory_in = prior_retain * initial_memory + prior_update
    memory_out = retain * memory_in + update
    grouped = memory_in.reshape(latents, heads, HEAD)
    normed = grouped * lax.rsqrt(jnp.mean(grouped * grouped, axis=-1, keepdims=True) + 1e-06)
    read_scores = (
        jnp.einsum(
            "the,mhe->htm", queries, normed.astype(jnp.bfloat16), preferred_element_type=jnp.float32
        )
        * scale
    )
    read_weights = trailing_softmax(read_scores).astype(jnp.bfloat16)
    read = jnp.einsum(
        "htm,mhe->the",
        read_weights,
        grouped.astype(jnp.bfloat16),
        preferred_element_type=jnp.float32,
    )
    mixed = (local.astype(jnp.float32) + read.reshape(-1, width)).astype(jnp.bfloat16)
    return (mixed[None], memory_out[None])


def solution(mesh):
    placed = (
        P("vid", "seg", "tp"),
        P("vid", "tp"),
        P("vid", "tp"),
        P(None, "tp"),
        P("vid", None, "tp"),
        P("vid", "seg", "tp"),
    )
    return jax.shard_map(
        shards,
        mesh=mesh,
        in_specs=placed,
        out_specs=(P("vid", "seg", "tp"), P("vid", "seg", "tp")),
        check_vma=False,
    )
```

profile of v0, /device:TPU:1, one launch (start us, length us, event | category | flops | bytes accessed | tf_op | source)
XLA Modules:
  0.0 283.6 jit_solution(8829787111092926543)
XLA Ops:
  7.2 2.0 pad_maximum_fusion
  9.8 1.5 broadcast_in_dim.20
  11.3 3.8 %all-to-all-start = ((bf16[2,512,1024]{1,2,0:T(8,128)(2,1)}), bf16[2,512,1024]{1,2,0:T(8,128)(2,1)S(1)}, u32[]{:S(2)}, u32[]{:S(2)}) async-start(bf16[2,512,1024]{1,2,0:T(8,128)(2,1)} %broadcast_in_dim.20), calls=%async_computation | async-start | bytes 4194304 | tf_op jit(solution)/shard_map/all_to_all | solution.py:17
  16.4 17.8 %all-to-all-done = bf16[2,512,1024]{1,2,0:T(8,128)(2,1)S(1)} async-done(((bf16[2,512,1024]{1,2,0:T(8,128)(2,1)}), bf16[2,512,1024]{1,2,0:T(8,128)(2,1)S(1)}, u32[]{:S(2)}, u32[]{:S(2)}) %all-to-all-start) | async-done | bytes 2097184 | tf_op jit(solution)/shard_map/all_to_all | solution.py:17
  34.2 130.9 %all-gather.3.cloned.1.call-done = bf16[2048,2048]{1,0:T(8,128)(2,1)} async-done(((bf16[128,2048]{1,0:T(8,128)(2,1)}), bf16[2048,2048]{1,0:T(8,128)(2,1)}) %all-gather.3.cloned.1.call-update) | async-done | bytes 8388624 | tf_op jit(solution)/shard_map/all_gather | solution.py:30
  165.1 4.5 %fusion.13 = bf16[1024,512]{1,0:T(8,128)(2,1)S(1)} fusion(bf16[512,2048]{0,1:T(8,128)(2,1)S(1)} %bitcast.83, bf16[2048,2048]{1,0:T(8,128)(2,1)} %all-gather.3.cloned.1.call-done), kind=kOutput, calls=%fused_computation.22 | convolution fusion | flops 2148007936 | bytes 7340032 | tf_op jit(solution)/shard_map/dot_general | solution.py:57
  172.2 3.2 %fusion.22 = f32[8,128,128]{1,2,0:T(8,128)S(1)} fusion(bf16[512,8,128]{0,2,1:T(8,128)(2,1)S(1)} %bitcast.90, f32[8,128]{1,0:T(8,128)S(1)} %fusion.51, f32[8,512,128]{2,1,0:T(8,128)} %copy-done.3), kind=kOutput, calls=%fused_computation.27 | convolution fusion | flops 136840704 | bytes 3674112 | tf_op jit(solution)/shard_map/hmt,the->mhe/dot_general | solution.py:76
  176.4 18.3 %all_gather.9 = f32[16,1,1024]{2,1,0:T(1,128)S(1)} all-gather(f32[1,1,1024]{2,1,0:T(1,128)S(1)} %copy-done.7), channel_id=1, replica_groups=mesh['seg'=16,'vid'=16,'tp'=2] {'seg'}, dimensions={0}, use_global_device_ids=true | all-gather | bytes 69632 | tf_op jit(solution)/shard_map/all_gather | solution.py:35
  194.9 5.4 %fusion.16 = bf16[1024,512]{1,0:T(8,128)(2,1)S(1)} fusion(bf16[512,2048]{0,1:T(8,128)(2,1)} %bitcast.84, bf16[2048,2048]{1,0:T(8,128)(2,1)} %all-gather.3.cloned.1.call-done), kind=kOutput, calls=%fused_computation.23 | convolution fusion | flops 2148007936 | bytes 7340032 | tf_op jit(solution)/shard_map/dot_general | solution.py:57
  200.3 31.6 %all-gather.5.cloned.1.call-done = f32[16,128,1024]{2,1,0:T(8,128)} async-done(((f32[1,128,1024]{2,1,0:T(8,128)}), f32[16,128,1024]{2,1,0:T(8,128)}) %all-gather.5.cloned.1.call-update) | async-done | bytes 8388624 | tf_op jit(solution)/shard_map/all_gather | solution.py:35
  232.0 24.4 %while.16 = (s32[]{:T(128)}, f32[1,1024]{1,0:T(1,128)S(1)}, f32[128,1024]{1,0:T(8,128)S(1)}, s32[]{:T(128)}, f32[16,1,1024]{2,1,0:T(1,128)S(1)}, /*index=5*/f32[16,128,1024]{2,1,0:T(8,128)}, s32[]{:T(128)}, s32[]{:T(128)}) while((s32[]{:T(128)}, f32[1,1024]{1,0:T(1,128)S(1)}, f32[128,1024]{1,0:T(8,128)S(1)}, s32[]{:T(128)}, ...), condition=%wide.region_3.4_spmd.clone, body=%wide.region_2.3_spmd.clone.sunk | while | flops 527364 | bytes 1593467 | solution.py:47
  232.0 1.5 fusion.63
  233.5 1.5 fusion.63
  235.0 1.5 fusion.63
  236.6 1.5 fusion.63
  238.1 1.5 fusion.63
  239.6 1.5 fusion.63
  241.1 1.5 fusion.63
  242.7 1.5 fusion.63
  244.2 1.5 fusion.63
  245.7 1.5 fusion.63
  247.3 1.5 fusion.63
  248.8 1.5 fusion.63
  250.3 1.5 fusion.63
  251.8 1.5 fusion.63
  253.4 1.5 fusion.63
  254.9 1.5 fusion.63
  256.4 2.0 add_bitcast_fusion
  260.5 1.5 fusion.52
  262.0 1.8 fusion.28
  263.8 9.8 %fusion.21 = f32[8,128,512]{2,1,0:T(8,128)} fusion(f32[8,512]{1,0:T(8,128)S(1)} %fusion.52, bf16[128,8,128]{2,1,0:T(8,128)(2,1)} %bitcast_convert_fusion, f32[8,512,128]{2,1,0:T(8,128)S(1)} %fusion.28), kind=kOutput, calls=%fused_computation.26 | convolution fusion | flops 136319104 | bytes 4472832 | tf_op jit(solution)/shard_map/htm,mhe->the/dot_general | solution.py:99
  273.5 1.9 copy.55
  (52 shorter events, 9.4 us)
Async XLA Ops:
  7.2 162.5 %copy-start = (bf16[128,1024]{1,0:T(8,128)(2,1)S(1)}, bf16[128,1024]{1,0:T(8,128)(2,1)}, u32[]{:S(2)}) copy-start(bf16[128,1024]{1,0:T(8,128)(2,1)} %param.11) | copy-start | bytes 786436
  7.2 2.0 copy-start.1
  7.2 157.9 %all-gather.3.cloned.1.call-start = ((), (), s32[]{:S(2)}) async-start(), calls=%async_computation.1 | async-start | bytes 8912896 | tf_op jit(solution)/shard_map/all_gather | solution.py:30
  11.3 22.9 %all-to-all-start = ((bf16[2,512,1024]{1,2,0:T(8,128)(2,1)}), bf16[2,512,1024]{1,2,0:T(8,128)(2,1)S(1)}, u32[]{:S(2)}, u32[]{:S(2)}) async-start(bf16[2,512,1024]{1,2,0:T(8,128)(2,1)} %broadcast_in_dim.20), calls=%async_computation | async-start | bytes 4194304 | tf_op jit(solution)/shard_map/all_to_all | solution.py:17
  15.0 216.9 %all-gather.5.cloned.1.call-start = ((), (), s32[]{:S(2)}) async-start(), calls=%async_computation.2 | async-start | bytes 8912896 | tf_op jit(solution)/shard_map/all_gather | solution.py:35
  34.2 135.5 %copy-start.2 = (bf16[2,512,1024]{1,2,0:T(8,128)(2,1)}, bf16[2,512,1024]{1,2,0:T(8,128)(2,1)S(1)}, u32[]{:S(2)}) copy-start(bf16[2,512,1024]{1,2,0:T(8,128)(2,1)S(1)} %all-to-all-done) | copy-start | bytes 6291460
  170.2 1.4 copy-start.3
  170.2 2.0 copy-start.5
  172.2 4.3 %copy-start.7 = (f32[1,1,1024]{2,1,0:T(1,128)S(1)}, f32[1,1,1024]{2,1,0:T(1,128)}, u32[]{:S(2)}) copy-start(f32[1,1,1024]{2,1,0:T(1,128)} %param.13) | copy-start | bytes 12292
  200.3 59.5 %copy-start.4 = (bf16[1024,512]{1,0:T(8,128)(2,1)}, bf16[1024,512]{1,0:T(8,128)(2,1)S(1)}, u32[]{:S(2)}) copy-start(bf16[1024,512]{1,0:T(8,128)(2,1)S(1)} %fusion.16) | copy-start | bytes 3145732
  259.8 0.7 copy-start.6
Sparse Core Ops, SparseCore 0:
  11.8 153.2 all-gather.2
  176.5 55.3 all-gather.4
where the time goes:
time: 285 us; the launch traced here: 284 us
  waiting for transfers between devices  180 us (63%)
  other arithmetic  31.1 us (11%)
  matrix products  26.6 us (9%)
  blocking collectives  18.3 us (6%)
  between operations  14.3 us (5%)
  local copies, waits for them, and re-layouts  8.82 us (3%)
  starting transfers between devices  3.84 us (1%)
    all_gather x1, waiting for transfers between devices, in_one_piece(): lax.all_gather(both, axis, axis=dim, tiled=True)  131 us
    all_gather x1, waiting for transfers between devices, entering(): everything = jax.tree.map(lambda part: lax.all_gather(part, axis), shard)  31.6 us
    select_n x32, other arithmetic, lap(): return jax.tree.map(lambda a, b: jnp.where(reached, a, b), new, before)  24 us
    all_gather x1, blocking collectives, entering(): everything = jax.tree.map(lambda part: lax.all_gather(part, axis), shard)  18.3 us
    all_to_all x1, waiting for transfers between devices, sent_to_all(): return lax.all_to_all(copies, axis, split_axis=0, concat_axis=0, tiled=True)  17.8 us
    dot_general x2, matrix products, add_rows(): return jnp.dot(left, piece, preferred_element_type=jnp.float32)  9.92 us
    dot_general x1, matrix products, shards(): jnp.einsum('htm,mhe->the', read_weights, grouped.astype(jnp.bfloat16), pr...  9.75 us
  transfers between devices with their start and end apart: 3, of which 3 were waited for; matrix products, arithmetic and copies ran while one was open for 3% of the time, Pallas kernels for 0%

commit v1 on v0

v1 whole, which is shorter than its diff:
```python
import jax
import jax.numpy as jnp
from jax import lax
from jax.experimental import pallas as pl
from jax.experimental.pallas import tpu as pltpu
from jax.sharding import Mesh, PartitionSpec as P

HEAD = 128
M = 128
TOK = 512
HALF = 1024
QUART = 512
Y, C, Z, H, L = 8, 2, 8, 2, 2
AXES = ("y", "c", "z", "h", "l")
BF = jnp.bfloat16
F32 = jnp.float32
SCALE = 128.0**-0.5
VMEM = pl.BlockSpec(memory_space=pltpu.VMEM)
PARAMS = pltpu.CompilerParams(vmem_limit_bytes=40 * 1024 * 1024)


def rank(y, c, z, h, l):
    return (((y * C + c) * Z + z) * H + h) * L + l


def sent(x, move):
    pairs = []
    for y in range(Y):
        for c in range(C):
            for z in range(Z):
                for h in range(H):
                    for l in range(L):
                        pairs.append((rank(y, c, z, h, l), rank(*move(y, c, z, h, l))))
    return lax.ppermute(x, AXES, pairs)


def to_core(x):
    return sent(x, lambda y, c, z, h, l: (y, 1 - c, z, h, l))


def to_tp(x):
    return sent(x, lambda y, c, z, h, l: (y, c, z, h, 1 - l))


def to_h(x):
    return sent(x, lambda y, c, z, h, l: (y, c, z, 1 - h, l))


def to_y(x, d):
    return sent(x, lambda y, c, z, h, l: ((y + d) % Y, c, z, h, l))


def to_z(x, d):
    return sent(x, lambda y, c, z, h, l: (y, c, (z + d) % Z, h, l))


def softmax(s):
    top = jnp.max(s, axis=-1, keepdims=True)
    e = jnp.exp(s - top)
    return (e / jnp.sum(e, axis=-1, keepdims=True)).astype(BF)


def dot(a, b):
    return jnp.dot(a, b, preferred_element_type=F32)


def dot_t(a, b):
    return lax.dot_general(a, b, (((1,), (1,)), ((), ())), preferred_element_type=F32)


def lanes(block, width):
    return pl.ds(pl.multiple_of(block * width, width), width)


def update_kernel(ml, mr, ol, orr, s0, s1, s2a, s2b, s3, lat, fm, fo, u_ref, p_ref, w):
    y, c, z, l = (lax.axis_index(a) for a in ("y", "c", "z", "l"))
    k = lax.rem(y + 2 * z, 4)
    w[:, lanes(k, HEAD)] = s0[...]
    w[:, lanes(lax.rem(k + 1, 4), HEAD)] = s1[...]
    w[0:HALF, lanes(lax.rem(k + 2, 4), HEAD)] = s2a[...]
    w[HALF:, lanes(lax.rem(k + 2, 4), HEAD)] = s2b[...]
    w[:, lanes(lax.rem(k + 3, 4), HEAD)] = s3[...]
    for j, (a, b) in enumerate(((ml, mr), (ol, orr))):
        keys = (
            dot(a[...], w[lanes(l, HALF), :]) + dot(b[...], w[lanes(1 - l, HALF), :])
        ).astype(BF)
        for h in range(4):
            cols = pl.ds(pl.multiple_of(c * QUART + h * HEAD, HEAD), HEAD)
            wts = softmax(dot_t(lat[:, cols], keys[:, h * HEAD : (h + 1) * HEAD]) * SCALE)
            u_ref[j, :, h * HEAD : (h + 1) * HEAD] = dot(wts, a[:, cols])
    mine, other = fm[:, lanes(c, QUART)], fo[:, lanes(c, QUART)]
    first = c == 0
    f1 = jnp.where(first, other, mine)
    u0 = jnp.where(first, u_ref[0], u_ref[1])
    u1 = jnp.where(first, u_ref[1], u_ref[0])
    p_ref[:, 0:16, :] = (f1 * u0 + u1).astype(BF).reshape(Y, 16, QUART)
    f = mine * other
    hi = f.astype(BF)
    rest = f - hi.astype(F32)
    mid = rest.astype(BF)
    low = (rest - mid.astype(F32)).astype(BF)
    row = lax.broadcasted_iota(jnp.int32, (16, QUART), 0)
    rows = jnp.where(
        row == 0,
        hi.astype(F32),
        jnp.where(row == 1, mid.astype(F32), jnp.where(row == 2, low.astype(F32), 0.0)),
    ).astype(BF)
    p_ref[:, 16:32, :] = jnp.broadcast_to(rows[None], (Y, 16, QUART))


def scan_kernel(p, init, e_ref):
    y, c = lax.axis_index("y"), lax.axis_index("c")
    e = init[pl.ds(pl.multiple_of(y * 16, 16), 16), lanes(c, QUART)]
    for s in range(Y):
        e_ref[s] = e.astype(BF)
        rows = p[s, 16:32, :].astype(F32)
        f = rows[0:1] + rows[1:2] + rows[2:3]
        e = f * e + p[s, 0:16, :].astype(F32)


def query_kernel(ml, mr, ol, orr, w, q_ref):
    l = lax.axis_index("l")
    for j, (a, b) in enumerate(((ml, mr), (ol, orr))):
        q_ref[j] = (
            dot(a[...], w[lanes(l, HALF), :]) + dot(b[...], w[lanes(1 - l, HALF), :])
        ).astype(BF)


def read_kernel(tok, qm, qo, em, eo, um, uo, fm, fo, mixed, mem):
    c = lax.axis_index("c")
    first = c == 0
    f0 = jnp.where(first, fm[...], fo[...])
    for half, (q, e, u) in enumerate(((qm, em, um), (qo, eo, uo))):
        part = c if half == 0 else 1 - c
        at = lanes(part, QUART)
        g = jnp.where(first, fm[:, at], fo[:, at])
        mine = fm[:, at]
        own, oth = (u[0], u[1]) if half == 0 else (u[1], u[0])
        e0 = e[...].astype(F32)
        entering = jnp.where(first, e0, g * e0 + oth)
        mem[:, at] = mine * entering + own
        for h in range(4):
            lo = h * HEAD
            x = entering[:, lo : lo + HEAD]
            keys = (x * lax.rsqrt(jnp.mean(x * x, axis=-1, keepdims=True) + 1e-6)).astype(BF)
            wts = softmax(dot_t(q[:, lo : lo + HEAD], keys) * SCALE)
            r = dot(wts, x.astype(BF))
            cols = pl.ds(pl.multiple_of(part * QUART + lo, HEAD), HEAD)
            mixed[:, cols] = (tok[:, cols].astype(F32) + r).astype(BF)


def shards(tokens, key_weight, query_weight, latent_queries, init_memory, forget):
    y, c, z, h = (lax.axis_index(a) for a in ("y", "c", "z", "h"))
    mine_l = tokens[0]
    fm = forget[0]
    mine_r = to_tp(mine_l)
    qw = lax.dynamic_slice(query_weight, (0, c * QUART), (128, QUART))
    qw2 = to_h(qw)
    both = jnp.stack([jnp.where(h == 0, qw, qw2), jnp.where(h == 0, qw2, qw)])
    wq = lax.all_gather(both[None], "z", tiled=True).reshape(2048, QUART)
    even = lax.dynamic_slice(key_weight, (0, c * QUART + (y % 4) * HEAD), (128, HEAD))
    odd = lax.dynamic_slice(key_weight, (0, c * QUART + ((y + 2) % 4) * HEAD), (128, HEAD))
    out = jnp.stack([even, even, odd, odd] * 4)
    s0 = lax.all_to_all(out, ("z", "h"), 0, 0, tiled=True).reshape(2048, HEAD)
    s1 = to_y(s0, -1)
    s3 = to_y(s0, 1)
    s2a = to_z(s0[:HALF], 1)
    s2b = to_z(s0[HALF:], -1)
    other_l = to_core(mine_l)
    fo = to_core(fm)
    other_r = to_core(mine_r)
    u, packed = pl.pallas_call(
        update_kernel,
        out_shape=(
            jax.ShapeDtypeStruct((2, M, QUART), F32),
            jax.ShapeDtypeStruct((Y, 32, QUART), BF),
        ),
        in_specs=[VMEM] * 12,
        out_specs=(VMEM, VMEM),
        scratch_shapes=[pltpu.VMEM((2048, QUART), BF)],
        compiler_params=PARAMS,
        cost_estimate=pl.CostEstimate(
            flops=2 * 1024 * 2048 * 512, bytes_accessed=7 << 20, transcendentals=1 << 19
        ),
        name="update",
    )(mine_l, mine_r, other_l, other_r, s0, s1, s2a, s2b, s3, latent_queries, fm, fo)
    arrived = lax.all_to_all(packed, "y", 0, 0, tiled=True)
    u_other = to_core(u)
    queries = pl.pallas_call(
        query_kernel,
        out_shape=jax.ShapeDtypeStruct((2, TOK, QUART), BF),
        in_specs=[VMEM] * 5,
        out_specs=VMEM,
        compiler_params=PARAMS,
        cost_estimate=pl.CostEstimate(
            flops=2 * 1024 * 2048 * 512, bytes_accessed=7 << 20, transcendentals=0
        ),
        name="query",
    )(mine_l, mine_r, other_l, other_r, wq)
    q_other = to_core(queries[1])
    entered = pl.pallas_call(
        scan_kernel,
        out_shape=jax.ShapeDtypeStruct((Y, 16, QUART), BF),
        in_specs=[VMEM] * 2,
        out_specs=VMEM,
        compiler_params=PARAMS,
        name="scan",
    )(arrived, init_memory[0])
    e = lax.all_to_all(entered, "y", 0, 0, tiled=True).reshape(M, QUART)
    e_other = to_core(e)
    mixed, mem = pl.pallas_call(
        read_kernel,
        out_shape=(
            jax.ShapeDtypeStruct((TOK, HALF), BF),
            jax.ShapeDtypeStruct((M, HALF), F32),
        ),
        in_specs=[VMEM] * 9,
        out_specs=(VMEM, VMEM),
        compiler_params=PARAMS,
        name="read",
    )(mine_l, queries[0], q_other, e, e_other, u, u_other, fm, fo)
    return mixed[None], mem[None]


def solution(mesh):
    fine = Mesh(mesh.devices.reshape(Y, C, Z, H, L), AXES)
    seg, vid = ("y", "c"), ("z", "h")
    return jax.shard_map(
        shards,
        mesh=fine,
        in_specs=(
            P(vid, seg, "l"),
            P(vid, "l"),
            P(vid, "l"),
            P(None, "l"),
            P(vid, None, "l"),
            P(vid, seg, "l"),
        ),
        out_specs=(P(vid, seg, "l"), P(vid, seg, "l")),
        check_vma=False,
    )
```

time: 285 us -> 157 us (0.55)
  waiting for transfers between devices: 180 us -> 26 us
  starting transfers between devices: 3.84 us -> 61.9 us
  other arithmetic: 31.1 us -> 1.69 us
  matrix products: 26.6 us -> 0 us
  Pallas kernels: 0 us -> 15.8 us
  local copies, waits for them, and re-layouts: 8.82 us -> 21.2 us
  blocking collectives: 18.3 us -> 14.5 us
    all_gather x2 -> x1, waiting for transfers between devices: 163 us -> 0.02 us  [shards(): wq = lax.all_gather(both[None], 'z', tiled=True).reshape(2048, QUART)]
    ppermute x0 -> x12, starting transfers between devices: none -> 44.4 us  [sent(): return lax.ppermute(x, AXES, pairs)]
    dot_general x6 -> x0, matrix products: 25.2 us -> none  [the longest x2 9.92 us: add_rows(): return jnp.dot(left, piece, preferred_element_type=jnp.float32)]
    select_n x32 -> x0, other arithmetic: 24 us -> none  [lap(): return jax.tree.map(lambda a, b: jnp.where(reached, a, b), new, before)]
    all_gather x1 -> x0, blocking collectives: 18.3 us -> none  [entering(): everything = jax.tree.map(lambda part: lax.all_gather(part, axis), shard)]
    unnamed x17 -> x33, local copies, waits for them, and re-layouts: 2.19 us -> 18.7 us
    pallas_call x0 -> x4, Pallas kernels: none -> 15.8 us  [the longest x1 8.05 us: shards(): pl.pallas_call(update_kernel, out_shape=(jax.ShapeDtypeStruct((2, M, QUAR...]
    all_to_all x0 -> x1, blocking collectives: none -> 14.5 us  [shards(): e = lax.all_to_all(entered, 'y', 0, 0, tiled=True).reshape(M, QUART)]
  transfers between devices with their start and end apart: 3 -> 15, of which waited for: 3 -> 6; matrix products, arithmetic and copies ran while one was open for 3% -> 10% of each run, Pallas kernels for 0% -> 8%
where the time goes in v1:
time: 157 us; the launch traced here: 155 us
  starting transfers between devices  61.9 us (39%)
  waiting for transfers between devices  26 us (17%)
  local copies, waits for them, and re-layouts  21.2 us (14%)
  Pallas kernels  15.8 us (10%)
  blocking collectives  14.5 us (9%)
  between operations  14.4 us (9%)
  other arithmetic  1.69 us (1%)
    ppermute x12, starting transfers between devices, sent(): return lax.ppermute(x, AXES, pairs)  44.4 us
    unnamed x33, local copies, waits for them, and re-layouts  18.7 us
    all_to_all x1, waiting for transfers between devices, shards(): s0 = lax.all_to_all(out, ('z', 'h'), 0, 0, tiled=True).reshape(2048, HEAD)  16.8 us
    all_to_all x1, blocking collectives, shards(): e = lax.all_to_all(entered, 'y', 0, 0, tiled=True).reshape(M, QUART)  14.5 us
    all_to_all x1, starting transfers between devices, shards(): s0 = lax.all_to_all(out, ('z', 'h'), 0, 0, tiled=True).reshape(2048, HEAD)  12.3 us
    ppermute x12, waiting for transfers between devices, sent(): return lax.ppermute(x, AXES, pairs)  9.07 us
    pallas_call x1, Pallas kernels, shards(): pl.pallas_call(update_kernel, out_shape=(jax.ShapeDtypeStruct((2, M, QUAR...  8.05 us
    all_to_all x1, starting transfers between devices, shards(): arrived = lax.all_to_all(packed, 'y', 0, 0, tiled=True)  5.21 us
  transfers between devices with their start and end apart: 15, of which 6 were waited for; matrix products, arithmetic and copies ran while one was open for 10% of the time, Pallas kernels for 8%

profile of v1, /device:TPU:1, one launch (start us, length us, event | category | flops | bytes accessed | tf_op | source)
XLA Modules:
  0.0 155.4 jit_solution(3014628518473031195)
XLA Ops:
  7.2 1.0 constant_dynamic-slice_fusion
  8.3 5.5 %collective-permute-start.3 = (bf16[128,512]{1,0:T(8,128)(2,1)S(1)}, bf16[128,512]{1,0:T(8,128)(2,1)S(1)}, u32[]{:S(2)}, u32[]{:S(2)}) collective-permute-start(bf16[128,512]{1,0:T(8,128)(2,1)S(1)} %constant_dynamic-slice_fusion), channel_id=1, source_target_pairs={{0,2},{1,3},{2,0},{3,1},{4,6},{5,7},{6,4},{7,5},{8,10},{9,11},{10,... | collective-permute-start | bytes 393224 | tf_op jit(solution)/shard_map/ppermute | solution.py:34
  13.8 2.3 %collective-permute-done.3 = bf16[128,512]{1,0:T(8,128)(2,1)S(1)} collective-permute-done((bf16[128,512]{1,0:T(8,128)(2,1)S(1)}, bf16[128,512]{1,0:T(8,128)(2,1)S(1)}, u32[]{:S(2)}, u32[]{:S(2)}) %collective-permute-start.3) | collective-permute-done | bytes 131104 | tf_op jit(solution)/shard_map/ppermute | solution.py:34
  17.8 3.9 %collective-permute-start = (bf16[512,1024]{1,0:T(8,128)(2,1)}, bf16[512,1024]{1,0:T(8,128)(2,1)S(1)}, u32[]{:S(2)}, u32[]{:S(2)}) collective-permute-start(bf16[512,1024]{1,0:T(8,128)(2,1)} %bitcast.39), channel_id=1, source_target_pairs={{0,1},{1,0},{2,3},{3,2},{4,5},{5,4},{6,7},{7,6},{8,9},{9,8},{10,11... | collective-permute-start | bytes 3145736 | tf_op jit(solution)/shard_map/ppermute | solution.py:34
  21.7 1.4 constant_dynamic-update-slice_fusion.15
  23.1 1.4 constant_dynamic-update-slice_fusion.14
  24.5 1.4 constant_dynamic-update-slice_fusion.13
  25.9 1.4 constant_dynamic-update-slice_fusion.12
  27.2 1.4 constant_dynamic-update-slice_fusion.11
  28.6 1.4 constant_dynamic-update-slice_fusion.10
  30.0 1.4 constant_dynamic-update-slice_fusion.9
  37.0 12.3 %all-to-all-start = ((bf16[16,128,128]{2,1,0:T(8,128)(2,1)}), bf16[16,128,128]{2,1,0:T(8,128)(2,1)S(1)}, u32[]{:S(2)}, u32[]{:S(2)}) async-start(bf16[16,128,128]{2,1,0:T(8,128)(2,1)} %constant_dynamic-update-slice_fusion), calls=%async_computation | async-start | bytes 1048576 | tf_op jit(solution)/shard_map/all_to_all | solution.py:164
  49.3 4.0 %collective-permute-start.1 = (bf16[512,1024]{1,0:T(8,128)(2,1)S(1)}, bf16[512,1024]{1,0:T(8,128)(2,1)}, u32[]{:S(2)}, u32[]{:S(2)}) collective-permute-start(bf16[512,1024]{1,0:T(8,128)(2,1)S(1)} %bitcast.40), channel_id=1, source_target_pairs={{0,32},{1,33},{2,34},{3,35},{4,36},{5,37},{6,38},{7,39},{8,40},{9,... | collective-permute-start | bytes 3145736 | tf_op jit(solution)/shard_map/ppermute | solution.py:34
  53.4 1.9 %collective-permute-start.2 = (bf16[512,1024]{1,0:T(8,128)(2,1)S(1)}, bf16[512,1024]{1,0:T(8,128)(2,1)}, u32[]{:S(2)}, u32[]{:S(2)}) collective-permute-start(bf16[512,1024]{1,0:T(8,128)(2,1)S(1)} %collective-permute-done.mr), channel_id=1, source_target_pairs={{0,32},{1,33},{2,34},{3,35},{4,36},{5,37},{6,38},{7,39},{8,40},{9,... | collective-permute-start | bytes 3145736 | tf_op jit(solution)/shard_map/ppermute | solution.py:34
  55.3 16.8 %all-to-all-done = bf16[16,128,128]{2,1,0:T(8,128)(2,1)S(1)} async-done(((bf16[16,128,128]{2,1,0:T(8,128)(2,1)}), bf16[16,128,128]{2,1,0:T(8,128)(2,1)S(1)}, u32[]{:S(2)}, u32[]{:S(2)}) %all-to-all-start) | async-done | bytes 524320 | tf_op jit(solution)/shard_map/all_to_all | solution.py:164
  72.1 5.2 %collective-permute-start.5 = (bf16[2048,128]{1,0:T(8,128)(2,1)S(1)}, bf16[2048,128]{1,0:T(8,128)(2,1)S(1)}, u32[]{:S(2)}, u32[]{:S(2)}) collective-permute-start(bf16[2048,128]{1,0:T(8,128)(2,1)S(1)} %bitcast.36), channel_id=1, source_target_pairs={{0,448},{1,449},{2,450},{3,451},{4,452},{5,453},{6,454},{7,455},{8... | collective-permute-start | bytes 1572872 | tf_op jit(solution)/shard_map/ppermute | solution.py:34
  77.4 1.9 %collective-permute-start.8 = (bf16[2048,128]{1,0:T(8,128)(2,1)S(1)}, bf16[2048,128]{1,0:T(8,128)(2,1)S(1)}, u32[]{:S(2)}, u32[]{:S(2)}) collective-permute-start(bf16[2048,128]{1,0:T(8,128)(2,1)S(1)} %bitcast.37), channel_id=1, source_target_pairs={{0,64},{1,65},{2,66},{3,67},{4,68},{5,69},{6,70},{7,71},{8,72},{9,... | collective-permute-start | bytes 1572872 | tf_op jit(solution)/shard_map/ppermute | solution.py:34
  79.3 5.7 %collective-permute-start.9 = (f32[1,1024]{1,0:T(1,128)S(1)}, f32[1,1024]{1,0:T(1,128)S(1)}, u32[]{:S(2)}, u32[]{:S(2)}) collective-permute-start(f32[1,1024]{1,0:T(1,128)S(1)} %bitcast.47), channel_id=1, source_target_pairs={{0,32},{1,33},{2,34},{3,35},{4,36},{5,37},{6,38},{7,39},{8,40},{9,... | collective-permute-start | bytes 12296 | tf_op jit(solution)/shard_map/ppermute | solution.py:34
  85.8 1.9 %collective-permute-start.6 = (bf16[1024,128]{1,0:T(8,128)(2,1)S(1)}, bf16[1024,128]{1,0:T(8,128)(2,1)S(1)}, u32[]{:S(2)}, u32[]{:S(2)}) collective-permute-start(bf16[1024,128]{1,0:T(8,128)(2,1)S(1)} %bitcast.52), channel_id=1, source_target_pairs={{0,4},{1,5},{2,6},{3,7},{4,8},{5,9},{6,10},{7,11},{8,12},{9,13},{1... | collective-permute-start | bytes 786440 | tf_op jit(solution)/shard_map/ppermute | solution.py:34
  87.8 4.6 %collective-permute-start.7 = (bf16[1024,128]{1,0:T(8,128)(2,1)S(1)}, bf16[1024,128]{1,0:T(8,128)(2,1)S(1)}, u32[]{:S(2)}, u32[]{:S(2)}) collective-permute-start(bf16[1024,128]{1,0:T(8,128)(2,1)S(1)} %bitcast.51), channel_id=1, source_target_pairs={{0,28},{1,29},{2,30},{3,31},{4,0},{5,1},{6,2},{7,3},{8,4},{9,5},{1... | collective-permute-start | bytes 786440 | tf_op jit(solution)/shard_map/ppermute | solution.py:34
  92.4 4.1 %collective-permute-done.6.s2a = bf16[1024,128]{1,0:T(8,128)(2,1)S(1)} collective-permute-done((bf16[1024,128]{1,0:T(8,128)(2,1)S(1)}, bf16[1024,128]{1,0:T(8,128)(2,1)S(1)}, u32[]{:S(2)}, u32[]{:S(2)}) %collective-permute-start.6) | collective-permute-done | bytes 262176 | tf_op jit(solution)/shard_map/ppermute | solution.py:34
  97.4 1.2 copy-done.5
  98.6 8.0 %update.1 = (f32[2,128,512]{2,1,0:T(8,128)S(1)}, bf16[8,32,512]{2,1,0:T(8,128)(2,1)}) custom-call(bf16[512,1024]{1,0:T(8,128)(2,1)S(1)} %bitcast.41, bf16[512,1024]{1,0:T(8,128)(2,1)S(1)} %copy-done.5, bf16[512,1024]{1,0:T(8,128)(2,1)} %collective-permute-done.1.ol, bf16[512,1024]{1,0:T(8,128)(2,1)} %collective-permute-done.2.orr, ...), custom_call_target="tpu_custom_call" | custom-call | flops 2147483648 | bytes 7340032 | tf_op jit(solution)/shard_map/update/pallas_call | solution.py:172
  106.7 5.2 %all-to-all-start.1 = ((bf16[8,32,512]{2,1,0:T(8,128)(2,1)}), bf16[8,32,512]{2,1,0:T(8,128)(2,1)S(1)}, u32[]{:S(2)}, u32[]{:S(2)}) async-start(bf16[8,32,512]{2,1,0:T(8,128)(2,1)} %get-tuple-element.6), calls=%async_computation.1 | async-start | bytes 524288 | tf_op jit(solution)/shard_map/all_to_all | solution.py:187
  111.9 3.7 %collective-permute-start.11 = (f32[2,128,512]{2,1,0:T(8,128)S(1)}, f32[2,128,512]{2,1,0:T(8,128)S(1)}, u32[]{:S(2)}, u32[]{:S(2)}) collective-permute-start(f32[2,128,512]{2,1,0:T(8,128)S(1)} %get-tuple-element.7.um), channel_id=1, source_target_pairs={{0,32},{1,33},{2,34},{3,35},{4,36},{5,37},{6,38},{7,39},{8,40},{9,... | collective-permute-start | bytes 1572872 | tf_op jit(solution)/shard_map/ppermute | solution.py:34
  115.6 1.6 %copy-done.3 = bf16[16,128,512]{2,1,0:T(8,128)(2,1)S(1)} copy-done((bf16[16,128,512]{2,1,0:T(8,128)(2,1)S(1)}, bf16[16,128,512]{2,1,0:T(8,128)(2,1)}, u32[]{:S(2)}) %copy-start.3) | copy-done | bytes 2097176
  117.2 1.2 copy-done.6
  118.4 3.9 %query.1 = bf16[2,512,512]{2,1,0:T(8,128)(2,1)S(1)} custom-call(bf16[512,1024]{1,0:T(8,128)(2,1)S(1)} %bitcast.42, bf16[512,1024]{1,0:T(8,128)(2,1)S(1)} %copy-done.6, bf16[512,1024]{1,0:T(8,128)(2,1)} %collective-permute-done.1.ol, bf16[512,1024]{1,0:T(8,128)(2,1)} %collective-permute-done.2.orr, bf16[2048,512]{1,0:T(8,128)(2,1)S(1)} %bitcast.50), custom_call_target="tpu_custom_call" | custom-call | flops 2147483648 | bytes 7340032 | tf_op jit(solution)/shard_map/query/pallas_call | solution.py:189
  123.1 1.9 %collective-permute-start.4 = (bf16[512,512]{1,0:T(8,128)(2,1)}, bf16[512,512]{1,0:T(8,128)(2,1)}, u32[]{:S(2)}, u32[]{:S(2)}) collective-permute-start(bf16[512,512]{1,0:T(8,128)(2,1)} %get-tuple-element.10), channel_id=1, source_target_pairs={{0,32},{1,33},{2,34},{3,35},{4,36},{5,37},{6,38},{7,39},{8,40},{9,... | collective-permute-start | bytes 1572872 | tf_op jit(solution)/shard_map/ppermute | solution.py:34
  125.1 14.5 %all_to_all.15 = bf16[8,16,512]{2,1,0:T(8,128)(2,1)S(1)} all-to-all(bf16[8,16,512]{2,1,0:T(8,128)(2,1)S(1)} %scan.1), channel_id=1, replica_groups=mesh['y'=8,'c'=2,'z'=8,'h'=2,'l'=2] {'y'}, dimensions={0} | all-to-all | bytes 262144 | tf_op jit(solution)/shard_map/all_to_all | solution.py:209
  139.6 4.2 %collective-permute-start.10 = (bf16[128,512]{1,0:T(8,128)(2,1)S(1)}, bf16[128,512]{1,0:T(8,128)(2,1)S(1)}, u32[]{:S(2)}, u32[]{:S(2)}) collective-permute-start(bf16[128,512]{1,0:T(8,128)(2,1)S(1)} %bitcast.45), channel_id=1, source_target_pairs={{0,32},{1,33},{2,34},{3,35},{4,36},{5,37},{6,38},{7,39},{8,40},{9,... | collective-permute-start | bytes 393224 | tf_op jit(solution)/shard_map/ppermute | solution.py:34
  144.8 3.8 %read.1 = (bf16[512,1024]{1,0:T(8,128)(2,1)}, f32[128,1024]{1,0:T(8,128)}) custom-call(bf16[512,1024]{1,0:T(8,128)(2,1)S(1)} %bitcast.43, bf16[512,512]{1,0:T(8,128)(2,1)S(1)} %get-tuple-element.11.qm, bf16[512,512]{1,0:T(8,128)(2,1)} %collective-permute-done.4.qo, bf16[128,512]{1,0:T(8,128)(2,1)S(1)} %bitcast.46, ...), custom_call_target="tpu_custom_call" | custom-call | tf_op jit(solution)/shard_map/read/pallas_call | solution.py:211
  (43 shorter events, 11.0 us)
Async XLA Ops:
  7.2 42.1 %copy-start = (bf16[1,512,1024]{2,1,0:T(8,128)(2,1)S(1)}, bf16[1,512,1024]{2,1,0:T(8,128)(2,1)}, u32[]{:S(2)}) copy-start(bf16[1,512,1024]{2,1,0:T(8,128)(2,1)} %param.6) | copy-start | bytes 3145732
  7.2 24.2 %copy-start.8 = (bf16[128,1024]{1,0:T(8,128)(2,1)S(1)}, bf16[128,1024]{1,0:T(8,128)(2,1)}, u32[]{:S(2)}) copy-start(bf16[128,1024]{1,0:T(8,128)(2,1)} %param.7) | copy-start | bytes 786436
  7.2 72.1 %copy-start.2 = (f32[1,1,1024]{2,1,0:T(1,128)S(1)}, f32[1,1,1024]{2,1,0:T(1,128)}, u32[]{:S(2)}) copy-start(f32[1,1,1024]{2,1,0:T(1,128)} %param.11) | copy-start | bytes 12292
  7.2 108.4 %all-gather.3.cloned.1.call-start = ((), (), s32[]{:S(2)}) async-start(), calls=%async_computation.3 | async-start | bytes 2359296 | tf_op jit(solution)/shard_map/all_gather | solution.py:160
  8.3 7.8 %collective-permute-start.3 = (bf16[128,512]{1,0:T(8,128)(2,1)S(1)}, bf16[128,512]{1,0:T(8,128)(2,1)S(1)}, u32[]{:S(2)}, u32[]{:S(2)}) collective-permute-start(bf16[128,512]{1,0:T(8,128)(2,1)S(1)} %constant_dynamic-slice_fusion), channel_id=1, source_target_pairs={{0,2},{1,3},{2,0},{3,1},{4,6},{5,7},{6,4},{7,5},{8,10},{9,11},{10,... | collective-permute-start | bytes 393224 | tf_op jit(solution)/shard_map/ppermute | solution.py:34
  17.0 80.3 %copy-start.7 = (bf16[128,1024]{1,0:T(8,128)(2,1)S(1)}, bf16[128,1024]{1,0:T(8,128)(2,1)}, u32[]{:S(2)}) copy-start(bf16[128,1024]{1,0:T(8,128)(2,1)} %lat.1) | copy-start | bytes 786436
  17.8 35.5 %collective-permute-start = (bf16[512,1024]{1,0:T(8,128)(2,1)}, bf16[512,1024]{1,0:T(8,128)(2,1)S(1)}, u32[]{:S(2)}, u32[]{:S(2)}) collective-permute-start(bf16[512,1024]{1,0:T(8,128)(2,1)} %bitcast.39), channel_id=1, source_target_pairs={{0,1},{1,0},{2,3},{3,2},{4,5},{5,4},{6,7},{7,6},{8,9},{9,8},{10,11... | collective-permute-start | bytes 3145736 | tf_op jit(solution)/shard_map/ppermute | solution.py:34
  37.0 35.1 %all-to-all-start = ((bf16[16,128,128]{2,1,0:T(8,128)(2,1)}), bf16[16,128,128]{2,1,0:T(8,128)(2,1)S(1)}, u32[]{:S(2)}, u32[]{:S(2)}) async-start(bf16[16,128,128]{2,1,0:T(8,128)(2,1)} %constant_dynamic-update-slice_fusion), calls=%async_computation | async-start | bytes 1048576 | tf_op jit(solution)/shard_map/all_to_all | solution.py:164
  49.3 38.4 %collective-permute-start.1 = (bf16[512,1024]{1,0:T(8,128)(2,1)S(1)}, bf16[512,1024]{1,0:T(8,128)(2,1)}, u32[]{:S(2)}, u32[]{:S(2)}) collective-permute-start(bf16[512,1024]{1,0:T(8,128)(2,1)S(1)} %bitcast.40), channel_id=1, source_target_pairs={{0,32},{1,33},{2,34},{3,35},{4,36},{5,37},{6,38},{7,39},{8,40},{9,... | collective-permute-start | bytes 3145736 | tf_op jit(solution)/shard_map/ppermute | solution.py:34
  53.4 44.0 %copy-start.4 = (bf16[512,1024]{1,0:T(8,128)(2,1)}, bf16[512,1024]{1,0:T(8,128)(2,1)S(1)}, u32[]{:S(2)}) copy-start(bf16[512,1024]{1,0:T(8,128)(2,1)S(1)} %collective-permute-done.mr) | copy-start | bytes 3145732
  53.4 44.0 %collective-permute-start.2 = (bf16[512,1024]{1,0:T(8,128)(2,1)S(1)}, bf16[512,1024]{1,0:T(8,128)(2,1)}, u32[]{:S(2)}, u32[]{:S(2)}) collective-permute-start(bf16[512,1024]{1,0:T(8,128)(2,1)S(1)} %collective-permute-done.mr), channel_id=1, source_target_pairs={{0,32},{1,33},{2,34},{3,35},{4,36},{5,37},{6,38},{7,39},{8,40},{9,... | collective-permute-start | bytes 3145736 | tf_op jit(solution)/shard_map/ppermute | solution.py:34
  72.1 25.2 %collective-permute-start.5 = (bf16[2048,128]{1,0:T(8,128)(2,1)S(1)}, bf16[2048,128]{1,0:T(8,128)(2,1)S(1)}, u32[]{:S(2)}, u32[]{:S(2)}) collective-permute-start(bf16[2048,128]{1,0:T(8,128)(2,1)S(1)} %bitcast.36), channel_id=1, source_target_pairs={{0,448},{1,449},{2,450},{3,451},{4,452},{5,453},{6,454},{7,455},{8... | collective-permute-start | bytes 1572872 | tf_op jit(solution)/shard_map/ppermute | solution.py:34
  77.4 20.0 %collective-permute-start.8 = (bf16[2048,128]{1,0:T(8,128)(2,1)S(1)}, bf16[2048,128]{1,0:T(8,128)(2,1)S(1)}, u32[]{:S(2)}, u32[]{:S(2)}) collective-permute-start(bf16[2048,128]{1,0:T(8,128)(2,1)S(1)} %bitcast.37), channel_id=1, source_target_pairs={{0,64},{1,65},{2,66},{3,67},{4,68},{5,69},{6,70},{7,71},{8,72},{9,... | collective-permute-start | bytes 1572872 | tf_op jit(solution)/shard_map/ppermute | solution.py:34
  79.3 6.6 %collective-permute-start.9 = (f32[1,1024]{1,0:T(1,128)S(1)}, f32[1,1024]{1,0:T(1,128)S(1)}, u32[]{:S(2)}, u32[]{:S(2)}) collective-permute-start(f32[1,1024]{1,0:T(1,128)S(1)} %bitcast.47), channel_id=1, source_target_pairs={{0,32},{1,33},{2,34},{3,35},{4,36},{5,37},{6,38},{7,39},{8,40},{9,... | collective-permute-start | bytes 12296 | tf_op jit(solution)/shard_map/ppermute | solution.py:34
  85.8 10.6 %collective-permute-start.6 = (bf16[1024,128]{1,0:T(8,128)(2,1)S(1)}, bf16[1024,128]{1,0:T(8,128)(2,1)S(1)}, u32[]{:S(2)}, u32[]{:S(2)}) collective-permute-start(bf16[1024,128]{1,0:T(8,128)(2,1)S(1)} %bitcast.52), channel_id=1, source_target_pairs={{0,4},{1,5},{2,6},{3,7},{4,8},{5,9},{6,10},{7,11},{8,12},{9,13},{1... | collective-permute-start | bytes 786440 | tf_op jit(solution)/shard_map/ppermute | solution.py:34
  87.8 9.6 %collective-permute-start.7 = (bf16[1024,128]{1,0:T(8,128)(2,1)S(1)}, bf16[1024,128]{1,0:T(8,128)(2,1)S(1)}, u32[]{:S(2)}, u32[]{:S(2)}) collective-permute-start(bf16[1024,128]{1,0:T(8,128)(2,1)S(1)} %bitcast.51), channel_id=1, source_target_pairs={{0,28},{1,29},{2,30},{3,31},{4,0},{5,1},{6,2},{7,3},{8,4},{9,5},{1... | collective-permute-start | bytes 786440 | tf_op jit(solution)/shard_map/ppermute | solution.py:34
  97.4 1.2 copy-start.5
  106.7 18.4 %all-to-all-start.1 = ((bf16[8,32,512]{2,1,0:T(8,128)(2,1)}), bf16[8,32,512]{2,1,0:T(8,128)(2,1)S(1)}, u32[]{:S(2)}, u32[]{:S(2)}) async-start(bf16[8,32,512]{2,1,0:T(8,128)(2,1)} %get-tuple-element.6), calls=%async_computation.1 | async-start | bytes 524288 | tf_op jit(solution)/shard_map/all_to_all | solution.py:187
  111.9 31.9 %collective-permute-start.11 = (f32[2,128,512]{2,1,0:T(8,128)S(1)}, f32[2,128,512]{2,1,0:T(8,128)S(1)}, u32[]{:S(2)}, u32[]{:S(2)}) collective-permute-start(f32[2,128,512]{2,1,0:T(8,128)S(1)} %get-tuple-element.7.um), channel_id=1, source_target_pairs={{0,32},{1,33},{2,34},{3,35},{4,36},{5,37},{6,38},{7,39},{8,40},{9,... | collective-permute-start | bytes 1572872 | tf_op jit(solution)/shard_map/ppermute | solution.py:34
  115.6 1.6 %copy-start.3 = (bf16[16,128,512]{2,1,0:T(8,128)(2,1)S(1)}, bf16[16,128,512]{2,1,0:T(8,128)(2,1)}, u32[]{:S(2)}) copy-start(bf16[16,128,512]{2,1,0:T(8,128)(2,1)} %all-gather.3.cloned.1.call-done) | copy-start | bytes 6291460
  117.2 1.2 copy-start.6
  122.3 2.8 %copy-start.1 = (f32[1,128,1024]{2,1,0:T(8,128)S(1)}, f32[1,128,1024]{2,1,0:T(8,128)}, u32[]{:S(2)}) copy-start(f32[1,128,1024]{2,1,0:T(8,128)} %param.10) | copy-start | bytes 1572868
  123.1 21.6 %collective-permute-start.4 = (bf16[512,512]{1,0:T(8,128)(2,1)}, bf16[512,512]{1,0:T(8,128)(2,1)}, u32[]{:S(2)}, u32[]{:S(2)}) collective-permute-start(bf16[512,512]{1,0:T(8,128)(2,1)} %get-tuple-element.10), channel_id=1, source_target_pairs={{0,32},{1,33},{2,34},{3,35},{4,36},{5,37},{6,38},{7,39},{8,40},{9,... | collective-permute-start | bytes 1572872 | tf_op jit(solution)/shard_map/ppermute | solution.py:34
  139.6 5.1 %collective-permute-start.10 = (bf16[128,512]{1,0:T(8,128)(2,1)S(1)}, bf16[128,512]{1,0:T(8,128)(2,1)S(1)}, u32[]{:S(2)}, u32[]{:S(2)}) collective-permute-start(bf16[128,512]{1,0:T(8,128)(2,1)S(1)} %bitcast.45), channel_id=1, source_target_pairs={{0,32},{1,33},{2,34},{3,35},{4,36},{5,37},{6,38},{7,39},{8,40},{9,... | collective-permute-start | bytes 393224 | tf_op jit(solution)/shard_map/ppermute | solution.py:34
Sparse Core Ops, SparseCore 0:
  17.9 57.3 all-gather.2

commit v2 on v1

v2 whole, which is shorter than its diff:
```python
import jax
import jax.numpy as jnp
from jax import lax
from jax.experimental import pallas as pl
from jax.experimental.pallas import tpu as pltpu
from jax.sharding import Mesh, PartitionSpec as P

HEAD = 128
M = 128
TOK = 512
HALF = 1024
QUART = 512
Y, C, Z, H, L = 8, 2, 8, 2, 2
AXES = ("y", "c", "z", "h", "l")
BF = jnp.bfloat16
F32 = jnp.float32
SCALE = 128.0**-0.5
VMEM = pl.BlockSpec(memory_space=pltpu.VMEM)
PARAMS = pltpu.CompilerParams(vmem_limit_bytes=24 * 1024 * 1024)


def rank(y, c, z, h, l):
    return (((y * C + c) * Z + z) * H + h) * L + l


def sent(x, move):
    pairs = []
    for y in range(Y):
        for c in range(C):
            for z in range(Z):
                for h in range(H):
                    for l in range(L):
                        pairs.append((rank(y, c, z, h, l), rank(*move(y, c, z, h, l))))
    return lax.ppermute(x, AXES, pairs)


def to_core(x):
    return sent(x, lambda y, c, z, h, l: (y, 1 - c, z, h, l))


def to_tp(x):
    return sent(x, lambda y, c, z, h, l: (y, c, z, h, 1 - l))


def to_h(x):
    return sent(x, lambda y, c, z, h, l: (y, c, z, 1 - h, l))


def to_y(x, d):
    return sent(x, lambda y, c, z, h, l: ((y + d) % Y, c, z, h, l))


def to_z(x, d):
    return sent(x, lambda y, c, z, h, l: (y, c, (z + d) % Z, h, l))


def softmax(s):
    top = jnp.max(s, axis=-1, keepdims=True)
    e = jnp.exp(s - top)
    return (e / jnp.sum(e, axis=-1, keepdims=True)).astype(BF)


def dot(a, b):
    return jnp.dot(a, b, preferred_element_type=F32)


def dot_t(a, b):
    return lax.dot_general(a, b, (((1,), (1,)), ((), ())), preferred_element_type=F32)


def lanes(block, width):
    return pl.ds(pl.multiple_of(block * width, width), width)


def resample(a, b, w, lat, u_ref):
    c, l = lax.axis_index("c"), lax.axis_index("l")
    keys = (
        dot(a[...], w[lanes(l, HALF), :]) + dot(b[...], w[lanes(1 - l, HALF), :])
    ).astype(BF)
    for h in range(4):
        cols = pl.ds(pl.multiple_of(c * QUART + h * HEAD, HEAD), HEAD)
        wts = softmax(dot_t(lat[:, cols], keys[:, h * HEAD : (h + 1) * HEAD]) * SCALE)
        u_ref[:, h * HEAD : (h + 1) * HEAD] = dot(wts, a[:, cols])


def first_kernel(a, b, s0, s1, s2a, s2b, s3, lat, u_ref, w):
    y, z = lax.axis_index("y"), lax.axis_index("z")
    k = lax.rem(y + 2 * z, 4)
    w[:, lanes(k, HEAD)] = s0[...]
    w[:, lanes(lax.rem(k + 1, 4), HEAD)] = s1[...]
    w[0:HALF, lanes(lax.rem(k + 2, 4), HEAD)] = s2a[...]
    w[HALF:, lanes(lax.rem(k + 2, 4), HEAD)] = s2b[...]
    w[:, lanes(lax.rem(k + 3, 4), HEAD)] = s3[...]
    resample(a, b, w, lat, u_ref)


def second_kernel(a, b, w, lat, um, fm, fo, u_ref, p_ref):
    c = lax.axis_index("c")
    u_ref[0] = um[...]
    resample(a, b, w, lat, u_ref.at[1])
    mine, other = fm[:, lanes(c, QUART)], fo[:, lanes(c, QUART)]
    first = c == 0
    f1 = jnp.where(first, other, mine)
    u0 = jnp.where(first, u_ref[0], u_ref[1])
    u1 = jnp.where(first, u_ref[1], u_ref[0])
    p_ref[:, :, 0:QUART] = (f1 * u0 + u1).astype(BF).reshape(Y, 16, QUART)
    f = mine * other
    hi = f.astype(BF)
    rest = f - hi.astype(F32)
    mid = rest.astype(BF)
    low = (rest - mid.astype(F32)).astype(BF)
    terms = [
        t.astype(F32)[:, i * HEAD : (i + 1) * HEAD] for t in (hi, mid, low) for i in range(4)
    ]
    rows = jnp.concatenate(terms + [jnp.zeros((4, HEAD), F32)], axis=0).astype(BF)
    p_ref[:, :, QUART:] = jnp.broadcast_to(rows[None], (Y, 16, HEAD))


def scan_kernel(p, init, e_ref):
    y, c = lax.axis_index("y"), lax.axis_index("c")
    e = init[pl.ds(pl.multiple_of(y * 16, 16), 16), lanes(c, QUART)]
    for s in range(Y):
        e_ref[s] = e.astype(BF)
        rows = p[s, :, QUART:].astype(F32)
        rows = rows[0:4] + rows[4:8] + rows[8:12]
        f = jnp.concatenate([rows[i : i + 1] for i in range(4)], axis=1)
        e = f * e + p[s, :, 0:QUART].astype(F32)


def query_kernel(ml, mr, ol, orr, t0, t1a, t1b, qm_ref, qo_ref, w):
    l, z = lax.axis_index("l"), lax.axis_index("z")
    k = lax.rem(z, 2)
    w[:, lanes(k, 256)] = t0[...]
    w[0:HALF, lanes(1 - k, 256)] = t1a[...]
    w[HALF:, lanes(1 - k, 256)] = t1b[...]
    for q_ref, a, b in ((qm_ref, ml, mr), (qo_ref, ol, orr)):
        q_ref[...] = (
            dot(a[...], w[lanes(l, HALF), :]) + dot(b[...], w[lanes(1 - l, HALF), :])
        ).astype(BF)


def read_kernel(tok, qm, qo, em, eo, um, uo, fm, fo, mixed, mem):
    c = lax.axis_index("c")
    first = c == 0
    f0 = jnp.where(first, fm[...], fo[...])
    for half, (q, e, u) in enumerate(((qm, em, um), (qo, eo, uo))):
        part = c if half == 0 else 1 - c
        at = lanes(part, QUART)
        g = jnp.where(first, fm[:, at], fo[:, at])
        mine = fm[:, at]
        own, oth = (u[0], u[1]) if half == 0 else (u[1], u[0])
        e0 = e[...].astype(F32)
        entering = jnp.where(first, e0, g * e0 + oth)
        mem[:, at] = mine * entering + own
        for h in range(4):
            lo = h * HEAD
            x = entering[:, lo : lo + HEAD]
            keys = (x * lax.rsqrt(jnp.mean(x * x, axis=-1, keepdims=True) + 1e-6)).astype(BF)
            wts = softmax(dot_t(q[:, lo : lo + HEAD], keys) * SCALE)
            r = dot(wts, x.astype(BF))
            cols = pl.ds(pl.multiple_of(part * QUART + lo, HEAD), HEAD)
            mixed[:, cols] = (tok[:, cols].astype(F32) + r).astype(BF)


def spread(pair):
    wide = jnp.stack(pair)[None, :, None]
    return jnp.broadcast_to(wide, (4, 2, 2, *pair[0].shape)).reshape(16, *pair[0].shape)


def shards(tokens, key_weight, query_weight, latent_queries, init_memory, forget):
    y, c, z, h = (lax.axis_index(a) for a in ("y", "c", "z", "h"))
    tie = lax.optimization_barrier
    fm = forget[0]
    even = lax.dynamic_slice(key_weight, (0, c * QUART + (y % 4) * HEAD), (128, HEAD))
    odd = lax.dynamic_slice(key_weight, (0, c * QUART + ((y + 2) % 4) * HEAD), (128, HEAD))
    qeven = lax.dynamic_slice(query_weight, (0, c * QUART), (128, 256))
    qodd = lax.dynamic_slice(query_weight, (0, c * QUART + 256), (128, 256))
    out, mine_l = tie((spread((even, odd)), tokens[0]))
    s0 = lax.all_to_all(out, ("z", "h"), 0, 0, tiled=True).reshape(2048, HEAD)
    mine_r = to_tp(mine_l)
    other_l = to_core(mine_l)
    fo = to_core(fm)
    qout, fo = tie((spread((qeven, qodd)), fo))
    t0 = lax.all_to_all(qout, ("z", "h"), 0, 0, tiled=True).reshape(2048, 256)
    s0, fo, other_l = tie((s0, fo, other_l))
    s1 = to_y(s0, -1)
    s3 = to_y(s0, 1)
    s2a = to_z(s0[:HALF], 1)
    s2b = to_z(s0[HALF:], -1)
    s1, s3, s2a, s2b, mine_r = tie((s1, s3, s2a, s2b, mine_r))
    other_r = to_core(mine_r)
    cost = pl.CostEstimate(
        flops=2 * 512 * 2048 * 512, bytes_accessed=7 << 20, transcendentals=1 << 18
    )
    um, w = pl.pallas_call(
        first_kernel,
        out_shape=(
            jax.ShapeDtypeStruct((M, QUART), F32),
            jax.ShapeDtypeStruct((2048, QUART), BF),
        ),
        in_specs=[VMEM] * 8,
        out_specs=(VMEM, VMEM),
        compiler_params=PARAMS,
        cost_estimate=cost,
        name="first",
    )(mine_l, mine_r, s0, s1, s2a, s2b, s3, latent_queries)
    u, packed = pl.pallas_call(
        second_kernel,
        out_shape=(
            jax.ShapeDtypeStruct((2, M, QUART), F32),
            jax.ShapeDtypeStruct((Y, 16, QUART + HEAD), BF),
        ),
        in_specs=[VMEM] * 7,
        out_specs=(VMEM, VMEM),
        compiler_params=PARAMS,
        cost_estimate=cost,
        name="second",
    )(other_l, other_r, w, latent_queries, um, fm, fo)
    arrived = lax.all_to_all(packed, "y", 0, 0, tiled=True)
    packed, t0 = tie((packed, t0))
    t1a = to_z(t0[:HALF], 1)
    t1b = to_z(t0[HALF:], -1)
    swapped = to_core(u)
    entered = pl.pallas_call(
        scan_kernel,
        out_shape=jax.ShapeDtypeStruct((Y, 16, QUART), BF),
        in_specs=[VMEM] * 2,
        out_specs=VMEM,
        compiler_params=PARAMS,
        name="scan",
    )(arrived, init_memory[0])
    entered, t0 = tie((entered, t0))
    queries = pl.pallas_call(
        query_kernel,
        out_shape=(jax.ShapeDtypeStruct((TOK, QUART), BF),) * 2,
        in_specs=[VMEM] * 7,
        out_specs=(VMEM, VMEM),
        scratch_shapes=[pltpu.VMEM((2048, QUART), BF)],
        compiler_params=PARAMS,
        cost_estimate=pl.CostEstimate(
            flops=2 * 1024 * 2048 * 512, bytes_accessed=7 << 20, transcendentals=0
        ),
        name="query",
    )(mine_l, mine_r, other_l, other_r, t0, t1a, t1b)
    e = lax.all_to_all(entered, "y", 0, 0, tiled=True).reshape(M, QUART)
    e_other = to_core(e)
    q_late, e_late = tie((queries[1], e))
    q_other = to_core(q_late)
    mixed, mem = pl.pallas_call(
        read_kernel,
        out_shape=(
            jax.ShapeDtypeStruct((TOK, HALF), BF),
            jax.ShapeDtypeStruct((M, HALF), F32),
        ),
        in_specs=[VMEM] * 9,
        out_specs=(VMEM, VMEM),
        compiler_params=PARAMS,
        name="read",
    )(mine_l, queries[0], q_other, e, e_other, u, swapped, fm, fo)
    return mixed[None], mem[None]


def solution(mesh):
    fine = Mesh(mesh.devices.reshape(Y, C, Z, H, L), AXES)
    seg, vid = ("y", "c"), ("z", "h")
    return jax.shard_map(
        shards,
        mesh=fine,
        in_specs=(
            P(vid, seg, "l"),
            P(vid, "l"),
            P(vid, "l"),
            P(None, "l"),
            P(vid, None, "l"),
            P(vid, seg, "l"),
        ),
        out_specs=(P(vid, seg, "l"), P(vid, seg, "l")),
        check_vma=False,
    )
```

time: 157 us -> 129 us (0.82)
  between operations: 14.4 us -> 0.97 us
  local copies, waits for them, and re-layouts: 21.2 us -> 10.2 us
  starting transfers between devices: 61.9 us -> 59.6 us
  other arithmetic: 1.69 us -> 0.02 us
    unnamed x33 -> x22, local copies, waits for them, and re-layouts: 18.7 us -> 5.49 us
    ppermute x12 -> x13, waiting for transfers between devices: 9.07 us -> 18.6 us  [sent(): return lax.ppermute(x, AXES, pairs)]
    all_to_all x1, waiting for transfers between devices: 16.8 us -> 7.66 us  [shards(): s0 = lax.all_to_all(out, ('z', 'h'), 0, 0, tiled=True).reshape(2048, HEAD)]
    ppermute x12 -> x13, starting transfers between devices: 44.4 us -> 38 us  [sent(): return lax.ppermute(x, AXES, pairs)]
    all_to_all x1 -> x2, starting transfers between devices: 5.21 us -> 8.16 us  [the longest x1 4.79 us: shards(): t0 = lax.all_to_all(qout, ('z', 'h'), 0, 0, tiled=True).reshape(2048, 256)]
    broadcast_in_dim x0 -> x2, local copies, waits for them, and re-layouts: none -> 1.99 us  [spread(): jnp.broadcast_to(wide, (4, 2, 2, *pair[0].shape))]
    another operation x2, other arithmetic: 1.69 us -> 0.02 us  [spread(): wide = jnp.stack(pair)[None, :, None]]
    pallas_call x2 -> x3, Pallas kernels: 11.9 us -> 12.9 us  [the longest x1 4.46 us: shards(): pl.pallas_call(query_kernel, out_shape=(jax.ShapeDtypeStruct((TOK, QUART)...]
  transfers between devices with their start and end apart: 15 -> 16, of which waited for: 6 -> 5; matrix products, arithmetic and copies ran while one was open for 10% -> 2% of each run, Pallas kernels for 8% -> 11%
where the time goes in v2:
time: 129 us; the launch traced here: 128 us
  starting transfers between devices  59.6 us (46%)
  waiting for transfers between devices  26.3 us (20%)
  Pallas kernels  16.3 us (13%)
  blocking collectives  14.9 us (12%)
  local copies, waits for them, and re-layouts  10.2 us (8%)
    ppermute x13, starting transfers between devices, sent(): return lax.ppermute(x, AXES, pairs)  38 us
    ppermute x13, waiting for transfers between devices, sent(): return lax.ppermute(x, AXES, pairs)  18.6 us
    all_to_all x1, blocking collectives, shards(): arrived = lax.all_to_all(packed, 'y', 0, 0, tiled=True)  14.9 us
    all_to_all x1, starting transfers between devices, shards(): s0 = lax.all_to_all(out, ('z', 'h'), 0, 0, tiled=True).reshape(2048, HEAD)  13.4 us
    all_to_all x1, waiting for transfers between devices, shards(): s0 = lax.all_to_all(out, ('z', 'h'), 0, 0, tiled=True).reshape(2048, HEAD)  7.66 us
    unnamed x22, local copies, waits for them, and re-layouts  5.49 us
    all_to_all x1, starting transfers between devices, shards(): t0 = lax.all_to_all(qout, ('z', 'h'), 0, 0, tiled=True).reshape(2048, 256)  4.79 us
    pallas_call x1, Pallas kernels, shards(): pl.pallas_call(query_kernel, out_shape=(jax.ShapeDtypeStruct((TOK, QUART)...  4.46 us
  transfers between devices with their start and end apart: 16, of which 5 were waited for; matrix products, arithmetic and copies ran while one was open for 2% of the time, Pallas kernels for 11%

profile of v2, /device:TPU:1, one launch (start us, length us, event | category | flops | bytes accessed | tf_op | source)
XLA Modules:
  0.0 128.3 jit_solution(3917697945888108925)
XLA Ops:
  1.5 0.9 broadcast_in_dim.8
  2.4 13.4 %all-to-all-start = ((bf16[16,128,128]{2,1,0:T(8,128)(2,1)}), bf16[16,128,128]{2,1,0:T(8,128)(2,1)S(1)}, u32[]{:S(2)}, u32[]{:S(2)}) async-start(bf16[16,128,128]{2,1,0:T(8,128)(2,1)} %bitcast.2), calls=%async_computation | async-start | bytes 1048576 | tf_op jit(solution)/shard_map/all_to_all | solution.py:179
  15.8 2.9 %collective-permute-start.1 = (bf16[512,1024]{1,0:T(8,128)(2,1)}, bf16[512,1024]{1,0:T(8,128)(2,1)}, u32[]{:S(2)}, u32[]{:S(2)}) collective-permute-start(bf16[512,1024]{1,0:T(8,128)(2,1)} %bitcast.22), channel_id=1, source_target_pairs={{0,32},{1,33},{2,34},{3,35},{4,36},{5,37},{6,38},{7,39},{8,40},{9,... | collective-permute-start | bytes 3145736 | tf_op jit(solution)/shard_map/ppermute | solution.py:34
  18.7 2.2 %collective-permute-start.6 = (bf16[512,1024]{1,0:T(8,128)(2,1)}, bf16[512,1024]{1,0:T(8,128)(2,1)}, u32[]{:S(2)}, u32[]{:S(2)}) collective-permute-start(bf16[512,1024]{1,0:T(8,128)(2,1)} %bitcast.23), channel_id=1, source_target_pairs={{0,1},{1,0},{2,3},{3,2},{4,5},{5,4},{6,7},{7,6},{8,9},{9,8},{10,11... | collective-permute-start | bytes 3145736 | tf_op jit(solution)/shard_map/ppermute | solution.py:34
  20.9 2.2 %collective-permute-start = (f32[1,1024]{1,0:T(1,128)}, f32[1,1024]{1,0:T(1,128)S(1)}, u32[]{:S(2)}, u32[]{:S(2)}) collective-permute-start(f32[1,1024]{1,0:T(1,128)} %bitcast.32), channel_id=1, source_target_pairs={{0,32},{1,33},{2,34},{3,35},{4,36},{5,37},{6,38},{7,39},{8,40},{9,... | collective-permute-start | bytes 12296 | tf_op jit(solution)/shard_map/ppermute | solution.py:34
  23.1 0.9 dynamic-slice_bitcast_fusion.1
  24.2 1.1 broadcast_in_dim.9
  25.3 7.7 %all-to-all-done = bf16[16,128,128]{2,1,0:T(8,128)(2,1)S(1)} async-done(((bf16[16,128,128]{2,1,0:T(8,128)(2,1)}), bf16[16,128,128]{2,1,0:T(8,128)(2,1)S(1)}, u32[]{:S(2)}, u32[]{:S(2)}) %all-to-all-start) | async-done | bytes 524320 | tf_op jit(solution)/shard_map/all_to_all | solution.py:179
  32.9 4.8 %all-to-all-start.2 = ((bf16[16,128,256]{2,1,0:T(8,128)(2,1)}), bf16[16,128,256]{2,1,0:T(8,128)(2,1)S(1)}, u32[]{:S(2)}, u32[]{:S(2)}) async-start(bf16[16,128,256]{2,1,0:T(8,128)(2,1)} %bitcast.35), calls=%async_computation.2 | async-start | bytes 2097152 | tf_op jit(solution)/shard_map/all_to_all | solution.py:184
  37.7 3.2 %collective-permute-start.3 = (bf16[2048,128]{1,0:T(8,128)(2,1)S(1)}, bf16[2048,128]{1,0:T(8,128)(2,1)S(1)}, u32[]{:S(2)}, u32[]{:S(2)}) collective-permute-start(bf16[2048,128]{1,0:T(8,128)(2,1)S(1)} %bitcast.18), channel_id=1, source_target_pairs={{0,64},{1,65},{2,66},{3,67},{4,68},{5,69},{6,70},{7,71},{8,72},{9,... | collective-permute-start | bytes 1572872 | tf_op jit(solution)/shard_map/ppermute | solution.py:34
  41.0 3.8 %collective-permute-start.2 = (bf16[2048,128]{1,0:T(8,128)(2,1)S(1)}, bf16[2048,128]{1,0:T(8,128)(2,1)S(1)}, u32[]{:S(2)}, u32[]{:S(2)}) collective-permute-start(bf16[2048,128]{1,0:T(8,128)(2,1)S(1)} %bitcast.19), channel_id=1, source_target_pairs={{0,448},{1,449},{2,450},{3,451},{4,452},{5,453},{6,454},{7,455},{8... | collective-permute-start | bytes 1572872 | tf_op jit(solution)/shard_map/ppermute | solution.py:34
  44.8 4.5 %collective-permute-start.5 = (bf16[1024,128]{1,0:T(8,128)(2,1)S(1)}, bf16[1024,128]{1,0:T(8,128)(2,1)S(1)}, u32[]{:S(2)}, u32[]{:S(2)}) collective-permute-start(bf16[1024,128]{1,0:T(8,128)(2,1)S(1)} %get-tuple-element.52), channel_id=1, source_target_pairs={{0,28},{1,29},{2,30},{3,31},{4,0},{5,1},{6,2},{7,3},{8,4},{9,5},{1... | collective-permute-start | bytes 786440 | tf_op jit(solution)/shard_map/ppermute | solution.py:34
  49.3 1.9 %collective-permute-start.4 = (bf16[1024,128]{1,0:T(8,128)(2,1)S(1)}, bf16[1024,128]{1,0:T(8,128)(2,1)S(1)}, u32[]{:S(2)}, u32[]{:S(2)}) collective-permute-start(bf16[1024,128]{1,0:T(8,128)(2,1)S(1)} %get-tuple-element.53), channel_id=1, source_target_pairs={{0,4},{1,5},{2,6},{3,7},{4,8},{5,9},{6,10},{7,11},{8,12},{9,13},{1... | collective-permute-start | bytes 786440 | tf_op jit(solution)/shard_map/ppermute | solution.py:34
  51.3 16.3 %collective-permute-done.5.s2b = bf16[1024,128]{1,0:T(8,128)(2,1)S(1)} collective-permute-done((bf16[1024,128]{1,0:T(8,128)(2,1)S(1)}, bf16[1024,128]{1,0:T(8,128)(2,1)S(1)}, u32[]{:S(2)}, u32[]{:S(2)}) %collective-permute-start.5) | collective-permute-done | bytes 262176 | tf_op jit(solution)/shard_map/ppermute | solution.py:34
  67.6 1.2 collective-permute-done.4.s2a
  68.8 3.4 %collective-permute-start.7 = (bf16[512,1024]{1,0:T(8,128)(2,1)}, bf16[512,1024]{1,0:T(8,128)(2,1)S(1)}, u32[]{:S(2)}, u32[]{:S(2)}) collective-permute-start(bf16[512,1024]{1,0:T(8,128)(2,1)} %collective-permute-done.6.b.mr), channel_id=1, source_target_pairs={{0,32},{1,33},{2,34},{3,35},{4,36},{5,37},{6,38},{7,39},{8,40},{9,... | collective-permute-start | bytes 3145736 | tf_op jit(solution)/shard_map/ppermute | solution.py:34
  72.2 4.4 %first.1 = (f32[128,512]{1,0:T(8,128)S(1)}, bf16[2048,512]{1,0:T(8,128)(2,1)S(1)}) custom-call(bf16[512,1024]{1,0:T(8,128)(2,1)S(1)} %bitcast.24, bf16[512,1024]{1,0:T(8,128)(2,1)} %collective-permute-done.6.b.mr, bf16[2048,128]{1,0:T(8,128)(2,1)S(1)} %bitcast.21, bf16[2048,128]{1,0:T(8,128)(2,1)S(1)} %collective-permute-done.2.s1, ...), custom_call_target="tpu_custom_call" | custom-call | flops 1073741824 | bytes 7340032 | tf_op jit(solution)/shard_map/first/pallas_call | solution.py:195
  76.6 4.0 %second.1 = (f32[2,128,512]{2,1,0:T(8,128)S(1)}, bf16[8,16,640]{2,1,0:T(8,128)(2,1)S(1)}) custom-call(bf16[512,1024]{1,0:T(8,128)(2,1)} %collective-permute-done.1.a.ol, bf16[512,1024]{1,0:T(8,128)(2,1)S(1)} %collective-permute-done.7.b.orr, bf16[2048,512]{1,0:T(8,128)(2,1)S(1)} %get-tuple-element.36.w, bf16[128,1024]{1,0:T(8,128)(2,1)S(1)} %copy-done.1, ...), custom_call_target="tpu_custom_call" | custom-call | flops 1073741824 | bytes 7340032 | tf_op jit(solution)/shard_map/second/pallas_call | solution.py:207
  80.6 1.0 copy-done.2
  82.2 1.0 fusion
  83.3 3.1 %collective-permute-start.9 = (bf16[1024,256]{1,0:T(8,128)(2,1)}, bf16[1024,256]{1,0:T(8,128)(2,1)}, u32[]{:S(2)}, u32[]{:S(2)}) collective-permute-start(bf16[1024,256]{1,0:T(8,128)(2,1)} %get-tuple-element.50), channel_id=1, source_target_pairs={{0,28},{1,29},{2,30},{3,31},{4,0},{5,1},{6,2},{7,3},{8,4},{9,5},{1... | collective-permute-start | bytes 1572872 | tf_op jit(solution)/shard_map/ppermute | solution.py:34
  86.4 2.2 %collective-permute-start.8 = (bf16[1024,256]{1,0:T(8,128)(2,1)}, bf16[1024,256]{1,0:T(8,128)(2,1)}, u32[]{:S(2)}, u32[]{:S(2)}) collective-permute-start(bf16[1024,256]{1,0:T(8,128)(2,1)} %get-tuple-element.51), channel_id=1, source_target_pairs={{0,4},{1,5},{2,6},{3,7},{4,8},{5,9},{6,10},{7,11},{8,12},{9,13},{1... | collective-permute-start | bytes 1572872 | tf_op jit(solution)/shard_map/ppermute | solution.py:34
  88.6 14.9 %all_to_all.20.p = bf16[8,16,640]{2,1,0:T(8,128)(2,1)S(1)} all-to-all(bf16[8,16,640]{2,1,0:T(8,128)(2,1)S(1)} %copy-done.8), channel_id=1, replica_groups=mesh['y'=8,'c'=2,'z'=8,'h'=2,'l'=2] {'y'}, dimensions={0} | all-to-all | bytes 327680 | tf_op jit(solution)/shard_map/all_to_all | solution.py:219
  104.2 3.4 %all-to-all-start.3 = ((bf16[8,16,512]{2,1,0:T(8,128)(2,1)}), bf16[8,16,512]{2,1,0:T(8,128)(2,1)S(1)}, u32[]{:S(2)}, u32[]{:S(2)}) async-start(bf16[8,16,512]{2,1,0:T(8,128)(2,1)} %scan.1), calls=%async_computation.3 | async-start | bytes 262144 | tf_op jit(solution)/shard_map/all_to_all | solution.py:245
  107.5 4.3 %collective-permute-start.12 = (f32[2,128,512]{2,1,0:T(8,128)S(1)}, f32[2,128,512]{2,1,0:T(8,128)S(1)}, u32[]{:S(2)}, u32[]{:S(2)}) collective-permute-start(f32[2,128,512]{2,1,0:T(8,128)S(1)} %get-tuple-element.47.um), channel_id=1, source_target_pairs={{0,32},{1,33},{2,34},{3,35},{4,36},{5,37},{6,38},{7,39},{8,40},{9,... | collective-permute-start | bytes 1572872 | tf_op jit(solution)/shard_map/ppermute | solution.py:34
  111.9 1.2 copy-done.3
  113.1 4.5 %query.1 = (bf16[512,512]{1,0:T(8,128)(2,1)S(1)}, bf16[512,512]{1,0:T(8,128)(2,1)S(1)}) custom-call(bf16[512,1024]{1,0:T(8,128)(2,1)S(1)} %bitcast.25, bf16[512,1024]{1,0:T(8,128)(2,1)} %collective-permute-done.6.b.mr, bf16[512,1024]{1,0:T(8,128)(2,1)} %collective-permute-done.1.a.ol, bf16[512,1024]{1,0:T(8,128)(2,1)S(1)} %copy-done.3, ...), custom_call_target="tpu_custom_call" | custom-call | flops 2147483648 | bytes 7340032 | tf_op jit(solution)/shard_map/query/pallas_call | solution.py:233
  119.2 1.9 %collective-permute-start.10 = (bf16[512,512]{1,0:T(8,128)(2,1)}, bf16[512,512]{1,0:T(8,128)(2,1)S(1)}, u32[]{:S(2)}, u32[]{:S(2)}) collective-permute-start(bf16[512,512]{1,0:T(8,128)(2,1)} %copy-done.10), channel_id=1, source_target_pairs={{0,32},{1,33},{2,34},{3,35},{4,36},{5,37},{6,38},{7,39},{8,40},{9,... | collective-permute-start | bytes 1572872 | tf_op jit(solution)/shard_map/ppermute | solution.py:34
  121.1 2.4 %collective-permute-start.11 = (bf16[128,512]{1,0:T(8,128)(2,1)S(1)}, bf16[128,512]{1,0:T(8,128)(2,1)S(1)}, u32[]{:S(2)}, u32[]{:S(2)}) collective-permute-start(bf16[128,512]{1,0:T(8,128)(2,1)S(1)} %bitcast.30), channel_id=1, source_target_pairs={{0,32},{1,33},{2,34},{3,35},{4,36},{5,37},{6,38},{7,39},{8,40},{9,... | collective-permute-start | bytes 393224 | tf_op jit(solution)/shard_map/ppermute | solution.py:34
  123.5 1.0 collective-permute-done.11.eo
  124.5 1.0 copy-done.6
  125.5 2.8 %read.1 = (bf16[512,1024]{1,0:T(8,128)(2,1)}, f32[128,1024]{1,0:T(8,128)}) custom-call(bf16[512,1024]{1,0:T(8,128)(2,1)S(1)} %bitcast.26, bf16[512,512]{1,0:T(8,128)(2,1)S(1)} %copy-done.6, bf16[512,512]{1,0:T(8,128)(2,1)S(1)} %collective-permute-done.10.qo, bf16[128,512]{1,0:T(8,128)(2,1)S(1)} %bitcast.31, bf16[128,512]{1,0:T(8,128)(2,1)S(1)} %collective-permute-done.11.eo, ...), custom_call_target="tpu_custom_call" | custom-call | tf_op jit(solution)/shard_map/read/pallas_call | solution.py:249
  (36 shorter events, 3.9 us)
Async XLA Ops:
  2.4 30.6 %all-to-all-start = ((bf16[16,128,128]{2,1,0:T(8,128)(2,1)}), bf16[16,128,128]{2,1,0:T(8,128)(2,1)S(1)}, u32[]{:S(2)}, u32[]{:S(2)}) async-start(bf16[16,128,128]{2,1,0:T(8,128)(2,1)} %bitcast.2), calls=%async_computation | async-start | bytes 1048576 | tf_op jit(solution)/shard_map/all_to_all | solution.py:179
  15.8 21.9 %collective-permute-start.1 = (bf16[512,1024]{1,0:T(8,128)(2,1)}, bf16[512,1024]{1,0:T(8,128)(2,1)}, u32[]{:S(2)}, u32[]{:S(2)}) collective-permute-start(bf16[512,1024]{1,0:T(8,128)(2,1)} %bitcast.22), channel_id=1, source_target_pairs={{0,32},{1,33},{2,34},{3,35},{4,36},{5,37},{6,38},{7,39},{8,40},{9,... | collective-permute-start | bytes 3145736 | tf_op jit(solution)/shard_map/ppermute | solution.py:34
  18.7 32.6 %collective-permute-start.6 = (bf16[512,1024]{1,0:T(8,128)(2,1)}, bf16[512,1024]{1,0:T(8,128)(2,1)}, u32[]{:S(2)}, u32[]{:S(2)}) collective-permute-start(bf16[512,1024]{1,0:T(8,128)(2,1)} %bitcast.23), channel_id=1, source_target_pairs={{0,1},{1,0},{2,3},{3,2},{4,5},{5,4},{6,7},{7,6},{8,9},{9,8},{10,11... | collective-permute-start | bytes 3145736 | tf_op jit(solution)/shard_map/ppermute | solution.py:34
  20.9 3.3 %collective-permute-start = (f32[1,1024]{1,0:T(1,128)}, f32[1,1024]{1,0:T(1,128)S(1)}, u32[]{:S(2)}, u32[]{:S(2)}) collective-permute-start(f32[1,1024]{1,0:T(1,128)} %bitcast.32), channel_id=1, source_target_pairs={{0,32},{1,33},{2,34},{3,35},{4,36},{5,37},{6,38},{7,39},{8,40},{9,... | collective-permute-start | bytes 12296 | tf_op jit(solution)/shard_map/ppermute | solution.py:34
  24.0 48.1 %copy-start = (bf16[1,512,1024]{2,1,0:T(8,128)(2,1)S(1)}, bf16[1,512,1024]{2,1,0:T(8,128)(2,1)}, u32[]{:S(2)}) copy-start(bf16[1,512,1024]{2,1,0:T(8,128)(2,1)} %param.6) | copy-start | bytes 3145732
  24.0 48.1 %copy-start.1 = (bf16[128,1024]{1,0:T(8,128)(2,1)S(1)}, bf16[128,1024]{1,0:T(8,128)(2,1)}, u32[]{:S(2)}) copy-start(bf16[128,1024]{1,0:T(8,128)(2,1)} %lat.3) | copy-start | bytes 786436
  32.9 49.3 %all-to-all-start.2 = ((bf16[16,128,256]{2,1,0:T(8,128)(2,1)}), bf16[16,128,256]{2,1,0:T(8,128)(2,1)S(1)}, u32[]{:S(2)}, u32[]{:S(2)}) async-start(bf16[16,128,256]{2,1,0:T(8,128)(2,1)} %bitcast.35), calls=%async_computation.2 | async-start | bytes 2097152 | tf_op jit(solution)/shard_map/all_to_all | solution.py:184
  37.7 31.0 %collective-permute-start.3 = (bf16[2048,128]{1,0:T(8,128)(2,1)S(1)}, bf16[2048,128]{1,0:T(8,128)(2,1)S(1)}, u32[]{:S(2)}, u32[]{:S(2)}) collective-permute-start(bf16[2048,128]{1,0:T(8,128)(2,1)S(1)} %bitcast.18), channel_id=1, source_target_pairs={{0,64},{1,65},{2,66},{3,67},{4,68},{5,69},{6,70},{7,71},{8,72},{9,... | collective-permute-start | bytes 1572872 | tf_op jit(solution)/shard_map/ppermute | solution.py:34
  41.0 27.8 %collective-permute-start.2 = (bf16[2048,128]{1,0:T(8,128)(2,1)S(1)}, bf16[2048,128]{1,0:T(8,128)(2,1)S(1)}, u32[]{:S(2)}, u32[]{:S(2)}) collective-permute-start(bf16[2048,128]{1,0:T(8,128)(2,1)S(1)} %bitcast.19), channel_id=1, source_target_pairs={{0,448},{1,449},{2,450},{3,451},{4,452},{5,453},{6,454},{7,455},{8... | collective-permute-start | bytes 1572872 | tf_op jit(solution)/shard_map/ppermute | solution.py:34
  44.8 22.8 %collective-permute-start.5 = (bf16[1024,128]{1,0:T(8,128)(2,1)S(1)}, bf16[1024,128]{1,0:T(8,128)(2,1)S(1)}, u32[]{:S(2)}, u32[]{:S(2)}) collective-permute-start(bf16[1024,128]{1,0:T(8,128)(2,1)S(1)} %get-tuple-element.52), channel_id=1, source_target_pairs={{0,28},{1,29},{2,30},{3,31},{4,0},{5,1},{6,2},{7,3},{8,4},{9,5},{1... | collective-permute-start | bytes 786440 | tf_op jit(solution)/shard_map/ppermute | solution.py:34
  49.3 27.3 %copy-start.9 = (f32[1,1,1024]{2,1,0:T(1,128)S(1)}, f32[1,1,1024]{2,1,0:T(1,128)}, u32[]{:S(2)}) copy-start(f32[1,1,1024]{2,1,0:T(1,128)} %param.11) | copy-start | bytes 12292
  49.3 19.4 %collective-permute-start.4 = (bf16[1024,128]{1,0:T(8,128)(2,1)S(1)}, bf16[1024,128]{1,0:T(8,128)(2,1)S(1)}, u32[]{:S(2)}, u32[]{:S(2)}) collective-permute-start(bf16[1024,128]{1,0:T(8,128)(2,1)S(1)} %get-tuple-element.53), channel_id=1, source_target_pairs={{0,4},{1,5},{2,6},{3,7},{4,8},{5,9},{6,10},{7,11},{8,12},{9,13},{1... | collective-permute-start | bytes 786440 | tf_op jit(solution)/shard_map/ppermute | solution.py:34
  68.8 7.8 %collective-permute-start.7 = (bf16[512,1024]{1,0:T(8,128)(2,1)}, bf16[512,1024]{1,0:T(8,128)(2,1)S(1)}, u32[]{:S(2)}, u32[]{:S(2)}) collective-permute-start(bf16[512,1024]{1,0:T(8,128)(2,1)} %collective-permute-done.6.b.mr), channel_id=1, source_target_pairs={{0,32},{1,33},{2,34},{3,35},{4,36},{5,37},{6,38},{7,39},{8,40},{9,... | collective-permute-start | bytes 3145736 | tf_op jit(solution)/shard_map/ppermute | solution.py:34
  80.6 1.0 copy-start.2
  81.6 0.7 copy-start.7
  82.2 21.3 %copy-start.4 = (f32[1,128,1024]{2,1,0:T(8,128)S(1)}, f32[1,128,1024]{2,1,0:T(8,128)}, u32[]{:S(2)}) copy-start(f32[1,128,1024]{2,1,0:T(8,128)} %param.10) | copy-start | bytes 1572868
  82.2 6.3 %copy-start.8 = (bf16[8,16,640]{2,1,0:T(8,128)(2,1)S(1)}, bf16[8,16,640]{2,1,0:T(8,128)(2,1)}, u32[]{:S(2)}) copy-start(bf16[8,16,640]{2,1,0:T(8,128)(2,1)} %copy-done.7) | copy-start | bytes 491524
  83.3 28.6 %collective-permute-start.9 = (bf16[1024,256]{1,0:T(8,128)(2,1)}, bf16[1024,256]{1,0:T(8,128)(2,1)}, u32[]{:S(2)}, u32[]{:S(2)}) collective-permute-start(bf16[1024,256]{1,0:T(8,128)(2,1)} %get-tuple-element.50), channel_id=1, source_target_pairs={{0,28},{1,29},{2,30},{3,31},{4,0},{5,1},{6,2},{7,3},{8,4},{9,5},{1... | collective-permute-start | bytes 1572872 | tf_op jit(solution)/shard_map/ppermute | solution.py:34
  86.4 25.5 %collective-permute-start.8 = (bf16[1024,256]{1,0:T(8,128)(2,1)}, bf16[1024,256]{1,0:T(8,128)(2,1)}, u32[]{:S(2)}, u32[]{:S(2)}) collective-permute-start(bf16[1024,256]{1,0:T(8,128)(2,1)} %get-tuple-element.51), channel_id=1, source_target_pairs={{0,4},{1,5},{2,6},{3,7},{4,8},{5,9},{6,10},{7,11},{8,12},{9,13},{1... | collective-permute-start | bytes 1572872 | tf_op jit(solution)/shard_map/ppermute | solution.py:34
  104.2 15.0 %all-to-all-start.3 = ((bf16[8,16,512]{2,1,0:T(8,128)(2,1)}), bf16[8,16,512]{2,1,0:T(8,128)(2,1)S(1)}, u32[]{:S(2)}, u32[]{:S(2)}) async-start(bf16[8,16,512]{2,1,0:T(8,128)(2,1)} %scan.1), calls=%async_computation.3 | async-start | bytes 262144 | tf_op jit(solution)/shard_map/all_to_all | solution.py:245
  107.5 16.0 %collective-permute-start.12 = (f32[2,128,512]{2,1,0:T(8,128)S(1)}, f32[2,128,512]{2,1,0:T(8,128)S(1)}, u32[]{:S(2)}, u32[]{:S(2)}) collective-permute-start(f32[2,128,512]{2,1,0:T(8,128)S(1)} %get-tuple-element.47.um), channel_id=1, source_target_pairs={{0,32},{1,33},{2,34},{3,35},{4,36},{5,37},{6,38},{7,39},{8,40},{9,... | collective-permute-start | bytes 1572872 | tf_op jit(solution)/shard_map/ppermute | solution.py:34
  111.9 1.2 copy-start.3
  117.6 0.8 copy-start.5
  118.4 0.8 copy-start.10
  119.2 5.3 %collective-permute-start.10 = (bf16[512,512]{1,0:T(8,128)(2,1)}, bf16[512,512]{1,0:T(8,128)(2,1)S(1)}, u32[]{:S(2)}, u32[]{:S(2)}) collective-permute-start(bf16[512,512]{1,0:T(8,128)(2,1)} %copy-done.10), channel_id=1, source_target_pairs={{0,32},{1,33},{2,34},{3,35},{4,36},{5,37},{6,38},{7,39},{8,40},{9,... | collective-permute-start | bytes 1572872 | tf_op jit(solution)/shard_map/ppermute | solution.py:34
  121.1 3.4 %collective-permute-start.11 = (bf16[128,512]{1,0:T(8,128)(2,1)S(1)}, bf16[128,512]{1,0:T(8,128)(2,1)S(1)}, u32[]{:S(2)}, u32[]{:S(2)}) collective-permute-start(bf16[128,512]{1,0:T(8,128)(2,1)S(1)} %bitcast.30), channel_id=1, source_target_pairs={{0,32},{1,33},{2,34},{3,35},{4,36},{5,37},{6,38},{7,39},{8,40},{9,... | collective-permute-start | bytes 393224 | tf_op jit(solution)/shard_map/ppermute | solution.py:34
  124.5 1.0 copy-start.6

commit v3 on v2

v3 whole, which is shorter than its diff:
```python
import jax
import jax.numpy as jnp
from jax import lax
from jax.experimental import pallas as pl
from jax.experimental.pallas import tpu as pltpu
from jax.sharding import Mesh, PartitionSpec as P

HEAD = 128
M = 128
TOK = 512
HALF = 1024
QUART = 512
Y, C, Z, H, L = 8, 2, 8, 2, 2
AXES = ("y", "c", "z", "h", "l")
BF = jnp.bfloat16
F32 = jnp.float32
SCALE = 128.0**-0.5
SCAN_COST = 1 << 20
KERNEL_COST = 1024
VMEM = pl.BlockSpec(memory_space=pltpu.VMEM)
ANY = pl.BlockSpec(memory_space=pltpu.HBM)
PARAMS = pltpu.CompilerParams(vmem_limit_bytes=24 * 1024 * 1024)


def rank(y, c, z, h, l):
    return (((y * C + c) * Z + z) * H + h) * L + l


def sent(x, move):
    pairs = []
    for y in range(Y):
        for c in range(C):
            for z in range(Z):
                for h in range(H):
                    for l in range(L):
                        pairs.append((rank(y, c, z, h, l), rank(*move(y, c, z, h, l))))
    return lax.ppermute(x, AXES, pairs)


def to_core(x):
    return sent(x, lambda y, c, z, h, l: (y, 1 - c, z, h, l))


def to_tp(x):
    return sent(x, lambda y, c, z, h, l: (y, c, z, h, 1 - l))


def to_h(x):
    return sent(x, lambda y, c, z, h, l: (y, c, z, 1 - h, l))


def to_y(x, d):
    return sent(x, lambda y, c, z, h, l: ((y + d) % Y, c, z, h, l))


def to_z(x, d):
    return sent(x, lambda y, c, z, h, l: (y, c, (z + d) % Z, h, l))


def softmax(s):
    top = jnp.max(s, axis=-1, keepdims=True)
    e = jnp.exp(s - top)
    return (e / jnp.sum(e, axis=-1, keepdims=True)).astype(BF)


def dot(a, b):
    return jnp.dot(a, b, preferred_element_type=F32)


def dot_t(a, b):
    return lax.dot_general(a, b, (((1,), (1,)), ((), ())), preferred_element_type=F32)


def lanes(block, width):
    return pl.ds(pl.multiple_of(block * width, width), width)


def fetch(pairs, sems):
    copies = [pltpu.make_async_copy(a, b, sems.at[i]) for i, (a, b) in enumerate(pairs)]
    for copy in copies:
        copy.start()
    return copies


def columns_of(w, slabs):
    k = lax.rem(lax.axis_index("y") + 2 * lax.axis_index("z"), 4)
    return [(s, w.at[:, lanes(lax.rem(k + i, 4), HEAD)]) for i, s in enumerate(slabs)]


def projected(a, b, w, later):
    l = lax.axis_index("l")
    left = dot(a[...], w[lanes(l, HALF), :])
    later.wait()
    return (left + dot(b[...], w[lanes(1 - l, HALF), :])).astype(BF)


def resample(a_in, b_in, s0, s1, s2, s3, lat, u_ref, w, a, b, sems):
    c = lax.axis_index("c")
    copies = fetch(columns_of(w, (s0, s1, s2, s3)) + [(a_in, a), (b_in, b)], sems)
    for copy in copies[:5]:
        copy.wait()
    keys = projected(a, b, w, copies[5])
    for h in range(4):
        cols = pl.ds(pl.multiple_of(c * QUART + h * HEAD, HEAD), HEAD)
        wts = softmax(dot_t(lat[:, cols], keys[:, h * HEAD : (h + 1) * HEAD]) * SCALE)
        u_ref[:, h * HEAD : (h + 1) * HEAD] = dot(wts, a[:, cols])


def second_kernel(
    a_in, b_in, s0, s1, s2, s3, lat, um, fm, fo, u_out, p_out, w, a, b, sems, u_ref, p_ref
):
    c = lax.axis_index("c")
    u_ref[0] = um[...]
    resample(a_in, b_in, s0, s1, s2, s3, lat, u_ref.at[1], w, a, b, sems)
    mine, other = fm[:, lanes(c, QUART)], fo[:, lanes(c, QUART)]
    first = c == 0
    f1 = jnp.where(first, other, mine)
    u0 = jnp.where(first, u_ref[0], u_ref[1])
    u1 = jnp.where(first, u_ref[1], u_ref[0])
    p_ref[:, :, 0:QUART] = (f1 * u0 + u1).astype(BF).reshape(Y, 16, QUART)
    f = mine * other
    hi = f.astype(BF)
    rest = f - hi.astype(F32)
    mid = rest.astype(BF)
    low = (rest - mid.astype(F32)).astype(BF)
    terms = [
        t.astype(F32)[:, i * HEAD : (i + 1) * HEAD] for t in (hi, mid, low) for i in range(4)
    ]
    rows = jnp.concatenate(terms + [jnp.zeros((4, HEAD), F32)], axis=0).astype(BF)
    p_ref[:, :, QUART:] = jnp.broadcast_to(rows[None], (Y, 16, HEAD))
    for copy in fetch([(p_ref, p_out), (u_ref, u_out)], sems):
        copy.wait()


def scan_kernel(p, init_in, e_ref, init, sem):
    y, c = lax.axis_index("y"), lax.axis_index("c")
    rows = pl.ds(pl.multiple_of(y * 16, 16), 16)
    (copy,) = fetch([(init_in.at[rows, lanes(c, QUART)], init)], sem)
    copy.wait()
    e = init[...]
    for s in range(Y):
        e_ref[s] = e.astype(BF)
        rows = p[s, :, QUART:].astype(F32)
        rows = rows[0:4] + rows[4:8] + rows[8:12]
        f = jnp.concatenate([rows[i : i + 1] for i in range(4)], axis=1)
        e = f * e + p[s, :, 0:QUART].astype(F32)


def query_kernel(
    ml_in, mr_in, ol_in, or_in, t0, t1, t2, t3, qm_out, qo_out, w, ml, mr, ol, orr, qm, qo, sems
):
    rest = [(ol_in, ol), (or_in, orr), (ml_in, ml), (mr_in, mr)]
    copies = fetch(columns_of(w, (t0, t1, t2, t3)) + rest, sems)
    for copy in copies[:5]:
        copy.wait()
    qo[...] = projected(ol, orr, w, copies[5])
    (out_o,) = fetch([(qo, qo_out)], sems)
    copies[6].wait()
    qm[...] = projected(ml, mr, w, copies[7])
    (out_m,) = fetch([(qm, qm_out)], sems.at[pl.ds(1, 1)])
    out_o.wait()
    out_m.wait()


def read_kernel(
    tok_in, qm_in, qo_in, um_in, uo_in, em, eo, fm, fo, mixed, mem, tok, qm, qo, um, uo, sems
):
    copies = fetch([(um_in, um), (qm_in, qm), (tok_in, tok), (uo_in, uo), (qo_in, qo)], sems)
    c = lax.axis_index("c")
    first = c == 0
    f0 = jnp.where(first, fm[...], fo[...])
    for half, (q, e, u) in enumerate(((qm, em, um), (qo, eo, uo))):
        part = c if half == 0 else 1 - c
        at = lanes(part, QUART)
        g = jnp.where(first, fm[:, at], fo[:, at])
        mine = fm[:, at]
        copies[3 * half].wait()
        own, oth = (u[0], u[1]) if half == 0 else (u[1], u[0])
        e0 = e[...].astype(F32)
        entering = jnp.where(first, e0, g * e0 + oth)
        mem[:, at] = mine * entering + own
        copies[3 * half + 1].wait()
        if half == 0:
            copies[2].wait()
        for h in range(4):
            lo = h * HEAD
            x = entering[:, lo : lo + HEAD]
            keys = (x * lax.rsqrt(jnp.mean(x * x, axis=-1, keepdims=True) + 1e-6)).astype(BF)
            wts = softmax(dot_t(q[:, lo : lo + HEAD], keys) * SCALE)
            r = dot(wts, x.astype(BF))
            cols = pl.ds(pl.multiple_of(part * QUART + lo, HEAD), HEAD)
            mixed[:, cols] = (tok[:, cols].astype(F32) + r).astype(BF)


def spread(pair):
    wide = jnp.stack(pair)[None, :, None]
    return jnp.broadcast_to(wide, (4, 2, 2, *pair[0].shape)).reshape(16, *pair[0].shape)


def split_kernel(both, k_out, q_out, sems):
    pairs = [(both.at[:, 0:HEAD], k_out), (both.at[:, HEAD : 2 * HEAD], q_out)]
    for copy in fetch(pairs, sems):
        copy.wait()


def head_columns(a, b, at):
    parts = [lax.dynamic_slice(x, (0, at), (128, HEAD)) for x in (a, b)]
    return jnp.concatenate(parts, axis=1)


def shards(tokens, key_weight, query_weight, latent_queries, init_memory, forget):
    y, c, z, h = (lax.axis_index(a) for a in ("y", "c", "z", "h"))
    tie = lax.optimization_barrier
    fm = forget[0]
    even = head_columns(key_weight, query_weight, c * QUART + (y % 4) * HEAD)
    odd = head_columns(key_weight, query_weight, c * QUART + ((y + 2) % 4) * HEAD)
    out, mine_l = tie((spread((even, odd)), tokens[0]))
    both = lax.all_to_all(out, ("z", "h"), 0, 0, tiled=True).reshape(2048, 2 * HEAD)
    mine_r = to_tp(mine_l)
    other_l = to_core(mine_l)
    fo = to_core(fm)
    both, fo, other_l = tie((both, fo, other_l))
    s0, t0 = pl.pallas_call(
        split_kernel,
        out_shape=(jax.ShapeDtypeStruct((2048, HEAD), BF),) * 2,
        in_specs=[ANY],
        out_specs=(ANY, ANY),
        scratch_shapes=[pltpu.SemaphoreType.DMA((2,))],
        compiler_params=PARAMS,
        name="split",
    )(both)
    s1 = to_y(s0, -1)
    s3 = to_y(s0, 1)
    s2 = to_z(s0, 1)
    t1 = to_y(t0, -1)
    t3 = to_y(t0, 1)
    t2 = to_z(t0, -1)
    other_r = to_core(mine_r)
    cost = pl.CostEstimate(
        flops=KERNEL_COST, bytes_accessed=KERNEL_COST, transcendentals=0
    )
    scratch = [
        pltpu.VMEM((2048, QUART), BF),
        pltpu.VMEM((TOK, HALF), BF),
        pltpu.VMEM((TOK, HALF), BF),
        pltpu.SemaphoreType.DMA((6,)),
    ]
    um = pl.pallas_call(
        resample,
        out_shape=jax.ShapeDtypeStruct((M, QUART), F32),
        in_specs=[ANY] * 6 + [VMEM],
        out_specs=VMEM,
        scratch_shapes=scratch,
        compiler_params=PARAMS,
        cost_estimate=cost,
        name="first",
    )(mine_l, mine_r, s0, s1, s2, s3, latent_queries)
    u, packed = pl.pallas_call(
        second_kernel,
        out_shape=(
            jax.ShapeDtypeStruct((2, M, QUART), F32),
            jax.ShapeDtypeStruct((Y, 16, QUART + HEAD), BF),
        ),
        in_specs=[ANY] * 6 + [VMEM] * 4,
        out_specs=(ANY, ANY),
        scratch_shapes=scratch
        + [
            pltpu.VMEM((2, M, QUART), F32),
            pltpu.VMEM((Y, 16, QUART + HEAD), BF),
        ],
        compiler_params=PARAMS,
        cost_estimate=cost,
        name="second",
    )(other_l, other_r, s0, s1, s2, s3, latent_queries, um, fm, fo)
    arrived = lax.all_to_all(packed, "y", 0, 0, tiled=True)
    swapped = to_core(u)
    entered = pl.pallas_call(
        scan_kernel,
        out_shape=jax.ShapeDtypeStruct((Y, 16, QUART), BF),
        in_specs=[VMEM, ANY],
        out_specs=VMEM,
        scratch_shapes=[pltpu.VMEM((16, QUART), F32), pltpu.SemaphoreType.DMA((1,))],
        compiler_params=PARAMS,
        cost_estimate=pl.CostEstimate(
            flops=SCAN_COST, bytes_accessed=1 << 20, transcendentals=0
        ),
        name="scan",
    )(arrived, init_memory[0])
    queries = pl.pallas_call(
        query_kernel,
        out_shape=(jax.ShapeDtypeStruct((TOK, QUART), BF),) * 2,
        in_specs=[ANY] * 8,
        out_specs=(ANY, ANY),
        scratch_shapes=[pltpu.VMEM((2048, QUART), BF)]
        + [pltpu.VMEM((TOK, HALF), BF)] * 4
        + [pltpu.VMEM((TOK, QUART), BF)] * 2
        + [pltpu.SemaphoreType.DMA((8,))],
        compiler_params=PARAMS,
        cost_estimate=pl.CostEstimate(
            flops=2 * 1024 * 2048 * 512, bytes_accessed=7 << 20, transcendentals=0
        ),
        name="query",
    )(mine_l, mine_r, other_l, other_r, t0, t1, t2, t3)
    e = lax.all_to_all(entered, "y", 0, 0, tiled=True).reshape(M, QUART)
    e_other = to_core(e)
    q_other = to_core(queries[1])
    mixed, mem = pl.pallas_call(
        read_kernel,
        out_shape=(
            jax.ShapeDtypeStruct((TOK, HALF), BF),
            jax.ShapeDtypeStruct((M, HALF), F32),
        ),
        in_specs=[ANY] * 5 + [VMEM] * 4,
        out_specs=(VMEM, VMEM),
        scratch_shapes=[
            pltpu.VMEM((TOK, HALF), BF),
            pltpu.VMEM((TOK, QUART), BF),
            pltpu.VMEM((TOK, QUART), BF),
            pltpu.VMEM((2, M, QUART), F32),
            pltpu.VMEM((2, M, QUART), F32),
            pltpu.SemaphoreType.DMA((5,)),
        ],
        compiler_params=PARAMS,
        name="read",
    )(mine_l, queries[0], q_other, u, swapped, e, e_other, fm, fo)
    return mixed[None], mem[None]


def solution(mesh):
    fine = Mesh(mesh.devices.reshape(Y, C, Z, H, L), AXES)
    seg, vid = ("y", "c"), ("z", "h")
    return jax.shard_map(
        shards,
        mesh=fine,
        in_specs=(
            P(vid, seg, "l"),
            P(vid, "l"),
            P(vid, "l"),
            P(None, "l"),
            P(vid, None, "l"),
            P(vid, seg, "l"),
        ),
        out_specs=(P(vid, seg, "l"), P(vid, seg, "l")),
        check_vma=False,
    )
```

time: 129 us -> 133 us (1.031)
  waiting for transfers between devices: 26.3 us -> 32 us
  local copies, waits for them, and re-layouts: 10.2 us -> 4.69 us
  Pallas kernels: 16.3 us -> 18.9 us
    ppermute x13, waiting for transfers between devices: 18.6 us -> 32 us  [sent(): return lax.ppermute(x, AXES, pairs)]
    all_to_all x3 -> x2, waiting for transfers between devices: 7.66 us -> 0.01 us  [the longest x1 0.01 us: shards(): lax.all_to_all(out, ('z', 'h'), 0, 0, tiled=True).reshape(2048, 2 * HEAD)]
    ppermute x13, starting transfers between devices: 38 us -> 42.4 us  [sent(): return lax.ppermute(x, AXES, pairs)]
    all_to_all x3 -> x2, starting transfers between devices: 21.6 us -> 18.3 us  [the longest x1 13.6 us: shards(): lax.all_to_all(out, ('z', 'h'), 0, 0, tiled=True).reshape(2048, 2 * HEAD)]
    unnamed x22 -> x16, local copies, waits for them, and re-layouts: 5.49 us -> 2.81 us
    another operation x2 -> x0, local copies, waits for them, and re-layouts: 1.67 us -> none  [spread(): wide = jnp.stack(pair)[None, :, None]]
    pallas_call x1, Pallas kernels: 2.79 us -> 4.43 us  [shards(): pl.pallas_call(read_kernel, out_shape=(jax.ShapeDtypeStruct((TOK, HALF),...]
    pallas_call x1, Pallas kernels: 4 us -> 5.38 us  [shards(): pl.pallas_call(second_kernel, out_shape=(jax.ShapeDtypeStruct((2, M, QUAR...]
  transfers between devices with their start and end apart: 16 -> 15, of which waited for: 5 -> 5; matrix products, arithmetic and copies ran while one was open for 2% -> 0% of each run, Pallas kernels for 11% -> 11%
where the time goes in v3:
time: 133 us; the launch traced here: 132 us
  starting transfers between devices  60.7 us (46%)
  waiting for transfers between devices  32 us (24%)
  Pallas kernels  18.9 us (14%)
  blocking collectives  14.6 us (11%)
  local copies, waits for them, and re-layouts  4.69 us (4%)
    ppermute x13, starting transfers between devices, sent(): return lax.ppermute(x, AXES, pairs)  42.4 us
    ppermute x13, waiting for transfers between devices, sent(): return lax.ppermute(x, AXES, pairs)  32 us
    all_to_all x1, blocking collectives, shards(): e = lax.all_to_all(entered, 'y', 0, 0, tiled=True).reshape(M, QUART)  14.6 us
    all_to_all x1, starting transfers between devices, shards(): lax.all_to_all(out, ('z', 'h'), 0, 0, tiled=True).reshape(2048, 2 * HEAD)  13.6 us
    pallas_call x1, Pallas kernels, shards(): pl.pallas_call(second_kernel, out_shape=(jax.ShapeDtypeStruct((2, M, QUAR...  5.38 us
    all_to_all x1, starting transfers between devices, shards(): arrived = lax.all_to_all(packed, 'y', 0, 0, tiled=True)  4.71 us
    pallas_call x1, Pallas kernels, shards(): pl.pallas_call(query_kernel, out_shape=(jax.ShapeDtypeStruct((TOK, QUART)...  4.7 us
    pallas_call x1, Pallas kernels, shards(): pl.pallas_call(read_kernel, out_shape=(jax.ShapeDtypeStruct((TOK, HALF),...  4.43 us
  transfers between devices with their start and end apart: 15, of which 5 were waited for; matrix products, arithmetic and copies ran while one was open for 0% of the time, Pallas kernels for 11%

profile of v3, /device:TPU:1, one launch (start us, length us, event | category | flops | bytes accessed | tf_op | source)
XLA Modules:
  0.0 132.0 jit_solution(15620834953031016846)
XLA Ops:
  0.7 0.8 constant_dynamic-slice_fusion.2
  1.6 1.1 broadcast_in_dim.12
  2.6 13.6 %all-to-all-start = ((bf16[16,128,256]{2,1,0:T(8,128)(2,1)}), bf16[16,128,256]{2,1,0:T(8,128)(2,1)S(1)}, u32[]{:S(2)}, u32[]{:S(2)}) async-start(bf16[16,128,256]{2,1,0:T(8,128)(2,1)} %bitcast.2), calls=%async_computation | async-start | bytes 2097152 | tf_op jit(solution)/shard_map/all_to_all | solution.py:218
  16.2 2.2 %collective-permute-start = (bf16[512,1024]{1,0:T(8,128)(2,1)S(1)}, bf16[512,1024]{1,0:T(8,128)(2,1)S(1)}, u32[]{:S(2)}, u32[]{:S(2)}) collective-permute-start(bf16[512,1024]{1,0:T(8,128)(2,1)S(1)} %bitcast.13), channel_id=1, source_target_pairs={{0,1},{1,0},{2,3},{3,2},{4,5},{5,4},{6,7},{7,6},{8,9},{9,8},{10,11... | collective-permute-start | bytes 3145736 | tf_op jit(solution)/shard_map/ppermute | solution.py:37
  18.4 3.1 %collective-permute-start.2 = (bf16[512,1024]{1,0:T(8,128)(2,1)S(1)}, bf16[512,1024]{1,0:T(8,128)(2,1)S(1)}, u32[]{:S(2)}, u32[]{:S(2)}) collective-permute-start(bf16[512,1024]{1,0:T(8,128)(2,1)S(1)} %bitcast.14), channel_id=1, source_target_pairs={{0,32},{1,33},{2,34},{3,35},{4,36},{5,37},{6,38},{7,39},{8,40},{9,... | collective-permute-start | bytes 3145736 | tf_op jit(solution)/shard_map/ppermute | solution.py:37
  21.6 1.9 %collective-permute-start.1 = (f32[1,1024]{1,0:T(1,128)S(1)}, f32[1,1024]{1,0:T(1,128)S(1)}, u32[]{:S(2)}, u32[]{:S(2)}) collective-permute-start(f32[1,1024]{1,0:T(1,128)S(1)} %bitcast.21), channel_id=1, source_target_pairs={{0,32},{1,33},{2,34},{3,35},{4,36},{5,37},{6,38},{7,39},{8,40},{9,... | collective-permute-start | bytes 12296 | tf_op jit(solution)/shard_map/ppermute | solution.py:37
  23.5 28.1 %collective-permute-done.mr_in.b_in = bf16[512,1024]{1,0:T(8,128)(2,1)S(1)} collective-permute-done((bf16[512,1024]{1,0:T(8,128)(2,1)S(1)}, bf16[512,1024]{1,0:T(8,128)(2,1)S(1)}, u32[]{:S(2)}, u32[]{:S(2)}) %collective-permute-start) | collective-permute-done | bytes 1048608 | tf_op jit(solution)/shard_map/ppermute | solution.py:37
  51.6 3.8 %collective-permute-start.3 = (bf16[512,1024]{1,0:T(8,128)(2,1)S(1)}, bf16[512,1024]{1,0:T(8,128)(2,1)}, u32[]{:S(2)}, u32[]{:S(2)}) collective-permute-start(bf16[512,1024]{1,0:T(8,128)(2,1)S(1)} %collective-permute-done.mr_in.b_in), channel_id=1, source_target_pairs={{0,32},{1,33},{2,34},{3,35},{4,36},{5,37},{6,38},{7,39},{8,40},{9,... | collective-permute-start | bytes 3145736 | tf_op jit(solution)/shard_map/ppermute | solution.py:37
  55.4 1.0 copy-done.2
  56.4 0.9 split.1
  57.3 5.1 %collective-permute-start.8 = (bf16[2048,128]{1,0:T(8,128)(2,1)S(1)}, bf16[2048,128]{1,0:T(8,128)(2,1)S(1)}, u32[]{:S(2)}, u32[]{:S(2)}) collective-permute-start(bf16[2048,128]{1,0:T(8,128)(2,1)S(1)} %get-tuple-element.22.s0), channel_id=1, source_target_pairs={{0,448},{1,449},{2,450},{3,451},{4,452},{5,453},{6,454},{7,455},{8... | collective-permute-start | bytes 1572872 | tf_op jit(solution)/shard_map/ppermute | solution.py:37
  62.4 3.3 %collective-permute-start.9 = (bf16[2048,128]{1,0:T(8,128)(2,1)S(1)}, bf16[2048,128]{1,0:T(8,128)(2,1)S(1)}, u32[]{:S(2)}, u32[]{:S(2)}) collective-permute-start(bf16[2048,128]{1,0:T(8,128)(2,1)S(1)} %get-tuple-element.22.s0), channel_id=1, source_target_pairs={{0,4},{1,5},{2,6},{3,7},{4,8},{5,9},{6,10},{7,11},{8,12},{9,13},{1... | collective-permute-start | bytes 1572872 | tf_op jit(solution)/shard_map/ppermute | solution.py:37
  65.7 1.9 %collective-permute-start.10 = (bf16[2048,128]{1,0:T(8,128)(2,1)S(1)}, bf16[2048,128]{1,0:T(8,128)(2,1)S(1)}, u32[]{:S(2)}, u32[]{:S(2)}) collective-permute-start(bf16[2048,128]{1,0:T(8,128)(2,1)S(1)} %get-tuple-element.22.s0), channel_id=1, source_target_pairs={{0,64},{1,65},{2,66},{3,67},{4,68},{5,69},{6,70},{7,71},{8,72},{9,... | collective-permute-start | bytes 1572872 | tf_op jit(solution)/shard_map/ppermute | solution.py:37
  67.6 4.7 %collective-permute-start.4 = (bf16[2048,128]{1,0:T(8,128)(2,1)}, bf16[2048,128]{1,0:T(8,128)(2,1)}, u32[]{:S(2)}, u32[]{:S(2)}) collective-permute-start(bf16[2048,128]{1,0:T(8,128)(2,1)} %get-tuple-element.19.t0), channel_id=1, source_target_pairs={{0,448},{1,449},{2,450},{3,451},{4,452},{5,453},{6,454},{7,455},{8... | collective-permute-start | bytes 1572872 | tf_op jit(solution)/shard_map/ppermute | solution.py:37
  72.3 1.4 %collective-permute-done.8.s1 = bf16[2048,128]{1,0:T(8,128)(2,1)S(1)} collective-permute-done((bf16[2048,128]{1,0:T(8,128)(2,1)S(1)}, bf16[2048,128]{1,0:T(8,128)(2,1)S(1)}, u32[]{:S(2)}, u32[]{:S(2)}) %collective-permute-start.8) | collective-permute-done | bytes 524320 | tf_op jit(solution)/shard_map/ppermute | solution.py:37
  73.7 4.5 %collective-permute-start.5 = (bf16[2048,128]{1,0:T(8,128)(2,1)}, bf16[2048,128]{1,0:T(8,128)(2,1)}, u32[]{:S(2)}, u32[]{:S(2)}) collective-permute-start(bf16[2048,128]{1,0:T(8,128)(2,1)} %get-tuple-element.19.t0), channel_id=1, source_target_pairs={{0,28},{1,29},{2,30},{3,31},{4,0},{5,1},{6,2},{7,3},{8,4},{9,5},{1... | collective-permute-start | bytes 1572872 | tf_op jit(solution)/shard_map/ppermute | solution.py:37
  78.2 0.5 collective-permute-done.9.s2
  78.7 1.9 %collective-permute-start.6 = (bf16[2048,128]{1,0:T(8,128)(2,1)}, bf16[2048,128]{1,0:T(8,128)(2,1)}, u32[]{:S(2)}, u32[]{:S(2)}) collective-permute-start(bf16[2048,128]{1,0:T(8,128)(2,1)} %get-tuple-element.19.t0), channel_id=1, source_target_pairs={{0,64},{1,65},{2,66},{3,67},{4,68},{5,69},{6,70},{7,71},{8,72},{9,... | collective-permute-start | bytes 1572872 | tf_op jit(solution)/shard_map/ppermute | solution.py:37
  80.7 1.0 collective-permute-done.10.s3
  81.7 3.5 %first.1.um = f32[128,512]{1,0:T(8,128)S(1)} custom-call(bf16[512,1024]{1,0:T(8,128)(2,1)S(1)} %bitcast.15, bf16[512,1024]{1,0:T(8,128)(2,1)S(1)} %collective-permute-done.mr_in.b_in, bf16[2048,128]{1,0:T(8,128)(2,1)S(1)} %get-tuple-element.22.s0, bf16[2048,128]{1,0:T(8,128)(2,1)S(1)} %collective-permute-done.8.s1, ...), custom_call_target="tpu_custom_call" | custom-call | flops 1024 | bytes 1024 | tf_op jit(solution)/shard_map/first/pallas_call | solution.py:248
  85.2 5.4 %second.1 = (f32[2,128,512]{2,1,0:T(8,128)}, bf16[8,16,640]{2,1,0:T(8,128)(2,1)}) custom-call(bf16[512,1024]{1,0:T(8,128)(2,1)S(1)} %copy-done.3, bf16[512,1024]{1,0:T(8,128)(2,1)} %collective-permute-done.3.or_in.b_in, bf16[2048,128]{1,0:T(8,128)(2,1)S(1)} %get-tuple-element.22.s0, bf16[2048,128]{1,0:T(8,128)(2,1)S(1)} %collective-permute-done.8.s1, ...), custom_call_target="tpu_custom_call" | custom-call | flops 1024 | bytes 1024 | tf_op jit(solution)/shard_map/second/pallas_call | solution.py:258
  90.6 4.7 %all-to-all-start.1 = ((bf16[8,16,640]{2,1,0:T(8,128)(2,1)}), bf16[8,16,640]{2,1,0:T(8,128)(2,1)S(1)}, u32[]{:S(2)}, u32[]{:S(2)}) async-start(bf16[8,16,640]{2,1,0:T(8,128)(2,1)} %get-tuple-element.25), calls=%async_computation.1 | async-start | bytes 327680 | tf_op jit(solution)/shard_map/all_to_all | solution.py:275
  95.3 4.7 %query.1 = (bf16[512,512]{1,0:T(8,128)(2,1)S(1)}, bf16[512,512]{1,0:T(8,128)(2,1)}) custom-call(bf16[512,1024]{1,0:T(8,128)(2,1)S(1)} %bitcast.16, bf16[512,1024]{1,0:T(8,128)(2,1)S(1)} %collective-permute-done.mr_in.b_in, bf16[512,1024]{1,0:T(8,128)(2,1)S(1)} %copy-done.3, bf16[512,1024]{1,0:T(8,128)(2,1)} %collective-permute-done.3.or_in.b_in, ...), custom_call_target="tpu_custom_call" | custom-call | flops 2147483648 | bytes 7340032 | tf_op jit(solution)/shard_map/query/pallas_call | solution.py:289
  100.0 0.8 copy-done.5
  100.8 3.9 %collective-permute-start.7 = (bf16[512,512]{1,0:T(8,128)(2,1)}, bf16[512,512]{1,0:T(8,128)(2,1)S(1)}, u32[]{:S(2)}, u32[]{:S(2)}) collective-permute-start(bf16[512,512]{1,0:T(8,128)(2,1)} %get-tuple-element.21), channel_id=1, source_target_pairs={{0,32},{1,33},{2,34},{3,35},{4,36},{5,37},{6,38},{7,39},{8,40},{9,... | collective-permute-start | bytes 1572872 | tf_op jit(solution)/shard_map/ppermute | solution.py:37
  104.7 1.9 %collective-permute-start.11 = (f32[2,128,512]{2,1,0:T(8,128)}, f32[2,128,512]{2,1,0:T(8,128)S(1)}, u32[]{:S(2)}, u32[]{:S(2)}) collective-permute-start(f32[2,128,512]{2,1,0:T(8,128)} %get-tuple-element.24.um_in), channel_id=1, source_target_pairs={{0,32},{1,33},{2,34},{3,35},{4,36},{5,37},{6,38},{7,39},{8,40},{9,... | collective-permute-start | bytes 1572872 | tf_op jit(solution)/shard_map/ppermute | solution.py:37
  106.7 1.0 copy-done.4
  107.7 0.1 scan.1
  107.8 14.6 %all_to_all.15 = bf16[8,16,512]{2,1,0:T(8,128)(2,1)S(1)} all-to-all(bf16[8,16,512]{2,1,0:T(8,128)(2,1)S(1)} %scan.1), channel_id=1, replica_groups=mesh['y'=8,'c'=2,'z'=8,'h'=2,'l'=2] {'y'}, dimensions={0} | all-to-all | bytes 262144 | tf_op jit(solution)/shard_map/all_to_all | solution.py:304
  122.4 4.2 %collective-permute-start.12 = (bf16[128,512]{1,0:T(8,128)(2,1)S(1)}, bf16[128,512]{1,0:T(8,128)(2,1)S(1)}, u32[]{:S(2)}, u32[]{:S(2)}) collective-permute-start(bf16[128,512]{1,0:T(8,128)(2,1)S(1)} %bitcast.19), channel_id=1, source_target_pairs={{0,32},{1,33},{2,34},{3,35},{4,36},{5,37},{6,38},{7,39},{8,40},{9,... | collective-permute-start | bytes 393224 | tf_op jit(solution)/shard_map/ppermute | solution.py:37
  126.6 0.9 collective-permute-done.12.eo
  127.6 4.4 %read.1 = (bf16[512,1024]{1,0:T(8,128)(2,1)}, f32[128,1024]{1,0:T(8,128)}) custom-call(bf16[512,1024]{1,0:T(8,128)(2,1)S(1)} %bitcast.17, bf16[512,512]{1,0:T(8,128)(2,1)S(1)} %copy-done.6, bf16[512,512]{1,0:T(8,128)(2,1)S(1)} %collective-permute-done.7.qo_in, f32[2,128,512]{2,1,0:T(8,128)} %get-tuple-element.24.um_in, ...), custom_call_target="tpu_custom_call" | custom-call | tf_op jit(solution)/shard_map/read/pallas_call | solution.py:307
  (26 shorter events, 0.1 us)
Async XLA Ops:
  2.6 13.6 %copy-start = (bf16[1,512,1024]{2,1,0:T(8,128)(2,1)S(1)}, bf16[1,512,1024]{2,1,0:T(8,128)(2,1)}, u32[]{:S(2)}) copy-start(bf16[1,512,1024]{2,1,0:T(8,128)(2,1)} %param.6) | copy-start | bytes 3145732
  2.6 19.0 %copy-start.7 = (f32[1,1,1024]{2,1,0:T(1,128)S(1)}, f32[1,1,1024]{2,1,0:T(1,128)}, u32[]{:S(2)}) copy-start(f32[1,1,1024]{2,1,0:T(1,128)} %param.11) | copy-start | bytes 12292
  2.6 53.8 %all-to-all-start = ((bf16[16,128,256]{2,1,0:T(8,128)(2,1)}), bf16[16,128,256]{2,1,0:T(8,128)(2,1)S(1)}, u32[]{:S(2)}, u32[]{:S(2)}) async-start(bf16[16,128,256]{2,1,0:T(8,128)(2,1)} %bitcast.2), calls=%async_computation | async-start | bytes 2097152 | tf_op jit(solution)/shard_map/all_to_all | solution.py:218
  16.2 35.4 %collective-permute-start = (bf16[512,1024]{1,0:T(8,128)(2,1)S(1)}, bf16[512,1024]{1,0:T(8,128)(2,1)S(1)}, u32[]{:S(2)}, u32[]{:S(2)}) collective-permute-start(bf16[512,1024]{1,0:T(8,128)(2,1)S(1)} %bitcast.13), channel_id=1, source_target_pairs={{0,1},{1,0},{2,3},{3,2},{4,5},{5,4},{6,7},{7,6},{8,9},{9,8},{10,11... | collective-permute-start | bytes 3145736 | tf_op jit(solution)/shard_map/ppermute | solution.py:37
  18.4 37.0 %collective-permute-start.2 = (bf16[512,1024]{1,0:T(8,128)(2,1)S(1)}, bf16[512,1024]{1,0:T(8,128)(2,1)S(1)}, u32[]{:S(2)}, u32[]{:S(2)}) collective-permute-start(bf16[512,1024]{1,0:T(8,128)(2,1)S(1)} %bitcast.14), channel_id=1, source_target_pairs={{0,32},{1,33},{2,34},{3,35},{4,36},{5,37},{6,38},{7,39},{8,40},{9,... | collective-permute-start | bytes 3145736 | tf_op jit(solution)/shard_map/ppermute | solution.py:37
  21.6 33.8 %collective-permute-start.1 = (f32[1,1024]{1,0:T(1,128)S(1)}, f32[1,1024]{1,0:T(1,128)S(1)}, u32[]{:S(2)}, u32[]{:S(2)}) collective-permute-start(f32[1,1024]{1,0:T(1,128)S(1)} %bitcast.21), channel_id=1, source_target_pairs={{0,32},{1,33},{2,34},{3,35},{4,36},{5,37},{6,38},{7,39},{8,40},{9,... | collective-permute-start | bytes 12296 | tf_op jit(solution)/shard_map/ppermute | solution.py:37
  51.6 33.6 %collective-permute-start.3 = (bf16[512,1024]{1,0:T(8,128)(2,1)S(1)}, bf16[512,1024]{1,0:T(8,128)(2,1)}, u32[]{:S(2)}, u32[]{:S(2)}) collective-permute-start(bf16[512,1024]{1,0:T(8,128)(2,1)S(1)} %collective-permute-done.mr_in.b_in), channel_id=1, source_target_pairs={{0,32},{1,33},{2,34},{3,35},{4,36},{5,37},{6,38},{7,39},{8,40},{9,... | collective-permute-start | bytes 3145736 | tf_op jit(solution)/shard_map/ppermute | solution.py:37
  55.4 1.0 copy-start.2
  56.4 25.3 %copy-start.1 = (bf16[128,1024]{1,0:T(8,128)(2,1)S(1)}, bf16[128,1024]{1,0:T(8,128)(2,1)}, u32[]{:S(2)}) copy-start(bf16[128,1024]{1,0:T(8,128)(2,1)} %lat.3) | copy-start | bytes 786436
  57.3 16.4 %collective-permute-start.8 = (bf16[2048,128]{1,0:T(8,128)(2,1)S(1)}, bf16[2048,128]{1,0:T(8,128)(2,1)S(1)}, u32[]{:S(2)}, u32[]{:S(2)}) collective-permute-start(bf16[2048,128]{1,0:T(8,128)(2,1)S(1)} %get-tuple-element.22.s0), channel_id=1, source_target_pairs={{0,448},{1,449},{2,450},{3,451},{4,452},{5,453},{6,454},{7,455},{8... | collective-permute-start | bytes 1572872 | tf_op jit(solution)/shard_map/ppermute | solution.py:37
  62.4 16.3 %collective-permute-start.9 = (bf16[2048,128]{1,0:T(8,128)(2,1)S(1)}, bf16[2048,128]{1,0:T(8,128)(2,1)S(1)}, u32[]{:S(2)}, u32[]{:S(2)}) collective-permute-start(bf16[2048,128]{1,0:T(8,128)(2,1)S(1)} %get-tuple-element.22.s0), channel_id=1, source_target_pairs={{0,4},{1,5},{2,6},{3,7},{4,8},{5,9},{6,10},{7,11},{8,12},{9,13},{1... | collective-permute-start | bytes 1572872 | tf_op jit(solution)/shard_map/ppermute | solution.py:37
  65.7 16.0 %collective-permute-start.10 = (bf16[2048,128]{1,0:T(8,128)(2,1)S(1)}, bf16[2048,128]{1,0:T(8,128)(2,1)S(1)}, u32[]{:S(2)}, u32[]{:S(2)}) collective-permute-start(bf16[2048,128]{1,0:T(8,128)(2,1)S(1)} %get-tuple-element.22.s0), channel_id=1, source_target_pairs={{0,64},{1,65},{2,66},{3,67},{4,68},{5,69},{6,70},{7,71},{8,72},{9,... | collective-permute-start | bytes 1572872 | tf_op jit(solution)/shard_map/ppermute | solution.py:37
  67.6 17.6 %copy-start.3 = (bf16[512,1024]{1,0:T(8,128)(2,1)S(1)}, bf16[512,1024]{1,0:T(8,128)(2,1)}, u32[]{:S(2)}) copy-start(bf16[512,1024]{1,0:T(8,128)(2,1)} %copy-done.2) | copy-start | bytes 3145732
  67.6 27.7 %collective-permute-start.4 = (bf16[2048,128]{1,0:T(8,128)(2,1)}, bf16[2048,128]{1,0:T(8,128)(2,1)}, u32[]{:S(2)}, u32[]{:S(2)}) collective-permute-start(bf16[2048,128]{1,0:T(8,128)(2,1)} %get-tuple-element.19.t0), channel_id=1, source_target_pairs={{0,448},{1,449},{2,450},{3,451},{4,452},{5,453},{6,454},{7,455},{8... | collective-permute-start | bytes 1572872 | tf_op jit(solution)/shard_map/ppermute | solution.py:37
  73.7 21.6 %collective-permute-start.5 = (bf16[2048,128]{1,0:T(8,128)(2,1)}, bf16[2048,128]{1,0:T(8,128)(2,1)}, u32[]{:S(2)}, u32[]{:S(2)}) collective-permute-start(bf16[2048,128]{1,0:T(8,128)(2,1)} %get-tuple-element.19.t0), channel_id=1, source_target_pairs={{0,28},{1,29},{2,30},{3,31},{4,0},{5,1},{6,2},{7,3},{8,4},{9,5},{1... | collective-permute-start | bytes 1572872 | tf_op jit(solution)/shard_map/ppermute | solution.py:37
  78.7 16.6 %collective-permute-start.6 = (bf16[2048,128]{1,0:T(8,128)(2,1)}, bf16[2048,128]{1,0:T(8,128)(2,1)}, u32[]{:S(2)}, u32[]{:S(2)}) collective-permute-start(bf16[2048,128]{1,0:T(8,128)(2,1)} %get-tuple-element.19.t0), channel_id=1, source_target_pairs={{0,64},{1,65},{2,66},{3,67},{4,68},{5,69},{6,70},{7,71},{8,72},{9,... | collective-permute-start | bytes 1572872 | tf_op jit(solution)/shard_map/ppermute | solution.py:37
  90.6 16.1 %all-to-all-start.1 = ((bf16[8,16,640]{2,1,0:T(8,128)(2,1)}), bf16[8,16,640]{2,1,0:T(8,128)(2,1)S(1)}, u32[]{:S(2)}, u32[]{:S(2)}) async-start(bf16[8,16,640]{2,1,0:T(8,128)(2,1)} %get-tuple-element.25), calls=%async_computation.1 | async-start | bytes 327680 | tf_op jit(solution)/shard_map/all_to_all | solution.py:275
  100.0 0.8 copy-start.5
  100.8 25.8 %collective-permute-start.7 = (bf16[512,512]{1,0:T(8,128)(2,1)}, bf16[512,512]{1,0:T(8,128)(2,1)S(1)}, u32[]{:S(2)}, u32[]{:S(2)}) collective-permute-start(bf16[512,512]{1,0:T(8,128)(2,1)} %get-tuple-element.21), channel_id=1, source_target_pairs={{0,32},{1,33},{2,34},{3,35},{4,36},{5,37},{6,38},{7,39},{8,40},{9,... | collective-permute-start | bytes 1572872 | tf_op jit(solution)/shard_map/ppermute | solution.py:37
  104.7 21.9 %collective-permute-start.11 = (f32[2,128,512]{2,1,0:T(8,128)}, f32[2,128,512]{2,1,0:T(8,128)S(1)}, u32[]{:S(2)}, u32[]{:S(2)}) collective-permute-start(f32[2,128,512]{2,1,0:T(8,128)} %get-tuple-element.24.um_in), channel_id=1, source_target_pairs={{0,32},{1,33},{2,34},{3,35},{4,36},{5,37},{6,38},{7,39},{8,40},{9,... | collective-permute-start | bytes 1572872 | tf_op jit(solution)/shard_map/ppermute | solution.py:37
  106.7 1.0 copy-start.4
  107.7 19.8 %copy-start.6 = (bf16[512,512]{1,0:T(8,128)(2,1)S(1)}, bf16[512,512]{1,0:T(8,128)(2,1)}, u32[]{:S(2)}) copy-start(bf16[512,512]{1,0:T(8,128)(2,1)} %copy-done.5) | copy-start | bytes 1572868
  122.4 5.1 %collective-permute-start.12 = (bf16[128,512]{1,0:T(8,128)(2,1)S(1)}, bf16[128,512]{1,0:T(8,128)(2,1)S(1)}, u32[]{:S(2)}, u32[]{:S(2)}) collective-permute-start(bf16[128,512]{1,0:T(8,128)(2,1)S(1)} %bitcast.19), channel_id=1, source_target_pairs={{0,32},{1,33},{2,34},{3,35},{4,36},{5,37},{6,38},{7,39},{8,40},{9,... | collective-permute-start | bytes 393224 | tf_op jit(solution)/shard_map/ppermute | solution.py:37

commit v4 on v3

--- a/solution.py
+++ b/solution.py
@@ -15,7 +15,7 @@
 BF = jnp.bfloat16
 F32 = jnp.float32
 SCALE = 128.0**-0.5
-SCAN_COST = 1 << 20
+SCAN_COST = 50 * 10**9
 KERNEL_COST = 1024
 VMEM = pl.BlockSpec(memory_space=pltpu.VMEM)
 ANY = pl.BlockSpec(memory_space=pltpu.HBM)
@@ -192,6 +192,10 @@
             mixed[:, cols] = (tok[:, cols].astype(F32) + r).astype(BF)
 
 
+def in_hbm(*arrays):
+    return [pltpu.with_memory_space_constraint(a, pltpu.HBM) for a in arrays]
+
+
 def spread(pair):
     wide = jnp.stack(pair)[None, :, None]
     return jnp.broadcast_to(wide, (4, 2, 2, *pair[0].shape)).reshape(16, *pair[0].shape)
@@ -218,8 +222,7 @@
     both = lax.all_to_all(out, ("z", "h"), 0, 0, tiled=True).reshape(2048, 2 * HEAD)
     mine_r = to_tp(mine_l)
     other_l = to_core(mine_l)
-    fo = to_core(fm)
-    both, fo, other_l = tie((both, fo, other_l))
+    both, other_l = tie((both, other_l))
     s0, t0 = pl.pallas_call(
         split_kernel,
         out_shape=(jax.ShapeDtypeStruct((2048, HEAD), BF),) * 2,
@@ -232,9 +235,9 @@
     s1 = to_y(s0, -1)
     s3 = to_y(s0, 1)
     s2 = to_z(s0, 1)
-    t1 = to_y(t0, -1)
-    t3 = to_y(t0, 1)
-    t2 = to_z(t0, -1)
+    fm, _ = tie((fm, s0))
+    fo = to_core(fm)
+    s1, s3, s2, fo, mine_r = tie((s1, s3, s2, fo, mine_r))
     other_r = to_core(mine_r)
     cost = pl.CostEstimate(
         flops=KERNEL_COST, bytes_accessed=KERNEL_COST, transcendentals=0
@@ -258,8 +261,8 @@
     u, packed = pl.pallas_call(
         second_kernel,
         out_shape=(
-            jax.ShapeDtypeStruct((2, M, QUART), F32),
-            jax.ShapeDtypeStruct((Y, 16, QUART + HEAD), BF),
+            pltpu.HBM((2, M, QUART), F32),
+            pltpu.HBM((Y, 16, QUART + HEAD), BF),
         ),
         in_specs=[ANY] * 6 + [VMEM] * 4,
         out_specs=(ANY, ANY),
@@ -273,6 +276,10 @@
         name="second",
     )(other_l, other_r, s0, s1, s2, s3, latent_queries, um, fm, fo)
     arrived = lax.all_to_all(packed, "y", 0, 0, tiled=True)
+    packed, t0 = tie((packed, t0))
+    t1 = to_y(t0, -1)
+    t3 = to_y(t0, 1)
+    t2 = to_z(t0, -1)
     swapped = to_core(u)
     entered = pl.pallas_call(
         scan_kernel,
@@ -285,10 +292,11 @@
             flops=SCAN_COST, bytes_accessed=1 << 20, transcendentals=0
         ),
         name="scan",
-    )(arrived, init_memory[0])
+    )(arrived, *in_hbm(init_memory[0]))
+    entered, t0 = tie((entered, t0))
     queries = pl.pallas_call(
         query_kernel,
-        out_shape=(jax.ShapeDtypeStruct((TOK, QUART), BF),) * 2,
+        out_shape=(pltpu.HBM((TOK, QUART), BF),) * 2,
         in_specs=[ANY] * 8,
         out_specs=(ANY, ANY),
         scratch_shapes=[pltpu.VMEM((2048, QUART), BF)]
@@ -300,10 +308,11 @@
             flops=2 * 1024 * 2048 * 512, bytes_accessed=7 << 20, transcendentals=0
         ),
         name="query",
-    )(mine_l, mine_r, other_l, other_r, t0, t1, t2, t3)
+    )(*in_hbm(mine_l, mine_r, other_l, other_r), t0, t1, t2, t3)
     e = lax.all_to_all(entered, "y", 0, 0, tiled=True).reshape(M, QUART)
     e_other = to_core(e)
-    q_other = to_core(queries[1])
+    q_late, e_late = tie((queries[1], e))
+    q_other = to_core(q_late)
     mixed, mem = pl.pallas_call(
         read_kernel,
         out_shape=(
@@ -322,7 +331,7 @@
         ],
         compiler_params=PARAMS,
         name="read",
-    )(mine_l, queries[0], q_other, u, swapped, e, e_other, fm, fo)
+    )(*in_hbm(mine_l, queries[0]), q_other, *in_hbm(u), swapped, e, e_other, fm, fo)
     return mixed[None], mem[None]
 
 

time: 133 us -> 128 us (0.962)
  blocking collectives: 14.6 us -> 0 us
  starting transfers between devices: 60.7 us -> 72.8 us
  waiting for transfers between devices: 32 us -> 29.6 us
  Pallas kernels: 18.9 us -> 20.9 us
  local copies, waits for them, and re-layouts: 4.69 us -> 2.71 us
    ppermute x13, waiting for transfers between devices: 32 us -> 7.93 us  [sent(): return lax.ppermute(x, AXES, pairs)]
    all_to_all x1, waiting for transfers between devices: 0.01 us -> 21.7 us  [shards(): lax.all_to_all(out, ('z', 'h'), 0, 0, tiled=True).reshape(2048, 2 * HEAD)]
    all_to_all x1 -> x0, blocking collectives: 14.6 us -> none  [shards(): e = lax.all_to_all(entered, 'y', 0, 0, tiled=True).reshape(M, QUART)]
    ppermute x13, starting transfers between devices: 42.4 us -> 48.7 us  [sent(): return lax.ppermute(x, AXES, pairs)]
    all_to_all x0 -> x1, starting transfers between devices: none -> 5.44 us  [shards(): e = lax.all_to_all(entered, 'y', 0, 0, tiled=True).reshape(M, QUART)]
    unnamed x16, local copies, waits for them, and re-layouts: 2.81 us -> 0.82 us
    pallas_call x1, Pallas kernels: 0.06 us -> 1.51 us  [shards(): pl.pallas_call(scan_kernel, out_shape=jax.ShapeDtypeStruct((Y, 16, QUART)...]
  transfers between devices with their start and end apart: 15 -> 16, of which waited for: 5 -> 6; matrix products, arithmetic and copies ran while one was open for 0% -> 0% of each run, Pallas kernels for 11% -> 9%
where the time goes in v4:
time: 128 us; the launch traced here: 127 us
  starting transfers between devices  72.8 us (57%)
  waiting for transfers between devices  29.6 us (23%)
  Pallas kernels  20.9 us (16%)
  local copies, waits for them, and re-layouts  2.71 us (2%)
    ppermute x13, starting transfers between devices, sent(): return lax.ppermute(x, AXES, pairs)  48.7 us
    all_to_all x1, waiting for transfers between devices, shards(): lax.all_to_all(out, ('z', 'h'), 0, 0, tiled=True).reshape(2048, 2 * HEAD)  21.7 us
    all_to_all x1, starting transfers between devices, shards(): lax.all_to_all(out, ('z', 'h'), 0, 0, tiled=True).reshape(2048, 2 * HEAD)  13.6 us
    ppermute x13, waiting for transfers between devices, sent(): return lax.ppermute(x, AXES, pairs)  7.93 us
    pallas_call x1, Pallas kernels, shards(): pl.pallas_call(query_kernel, out_shape=(pltpu.HBM((TOK, QUART), BF),) * 2...  5.45 us
    all_to_all x1, starting transfers between devices, shards(): e = lax.all_to_all(entered, 'y', 0, 0, tiled=True).reshape(M, QUART)  5.44 us
    all_to_all x1, starting transfers between devices, shards(): arrived = lax.all_to_all(packed, 'y', 0, 0, tiled=True)  5.11 us
    pallas_call x1, Pallas kernels, shards(): pl.pallas_call(read_kernel, out_shape=(jax.ShapeDtypeStruct((TOK, HALF),...  4.88 us
  transfers between devices with their start and end apart: 16, of which 6 were waited for; matrix products, arithmetic and copies ran while one was open for 0% of the time, Pallas kernels for 9%

profile of v4, /device:TPU:1, one launch (start us, length us, event | category | flops | bytes accessed | tf_op | source)
XLA Modules:
  0.0 127.0 jit_solution(2042341897895171239)
XLA Ops:
  0.7 0.8 constant_dynamic-slice_fusion.2
  1.6 1.1 broadcast_in_dim.12
  2.6 13.6 %all-to-all-start = ((bf16[16,128,256]{2,1,0:T(8,128)(2,1)}), bf16[16,128,256]{2,1,0:T(8,128)(2,1)S(1)}, u32[]{:S(2)}, u32[]{:S(2)}) async-start(bf16[16,128,256]{2,1,0:T(8,128)(2,1)} %bitcast.2), calls=%async_computation | async-start | bytes 2097152 | tf_op jit(solution)/shard_map/all_to_all | solution.py:222
  16.2 2.9 %collective-permute-start = (bf16[512,1024]{1,0:T(8,128)(2,1)S(1)}, bf16[512,1024]{1,0:T(8,128)(2,1)S(1)}, u32[]{:S(2)}, u32[]{:S(2)}) collective-permute-start(bf16[512,1024]{1,0:T(8,128)(2,1)S(1)} %bitcast.15), channel_id=1, source_target_pairs={{0,32},{1,33},{2,34},{3,35},{4,36},{5,37},{6,38},{7,39},{8,40},{9,... | collective-permute-start | bytes 3145736 | tf_op jit(solution)/shard_map/ppermute | solution.py:37
  19.1 2.2 %collective-permute-start.5 = (bf16[512,1024]{1,0:T(8,128)(2,1)S(1)}, bf16[512,1024]{1,0:T(8,128)(2,1)}, u32[]{:S(2)}, u32[]{:S(2)}) collective-permute-start(bf16[512,1024]{1,0:T(8,128)(2,1)S(1)} %bitcast.16), channel_id=1, source_target_pairs={{0,1},{1,0},{2,3},{3,2},{4,5},{5,4},{6,7},{7,6},{8,9},{9,8},{10,11... | collective-permute-start | bytes 3145736 | tf_op jit(solution)/shard_map/ppermute | solution.py:37
  21.3 0.0 collective-permute-done.a_in.ol_in
  21.3 21.7 %all-to-all-done = bf16[16,128,256]{2,1,0:T(8,128)(2,1)S(1)} async-done(((bf16[16,128,256]{2,1,0:T(8,128)(2,1)}), bf16[16,128,256]{2,1,0:T(8,128)(2,1)S(1)}, u32[]{:S(2)}, u32[]{:S(2)}) %all-to-all-start) | async-done | bytes 1048608 | tf_op jit(solution)/shard_map/all_to_all | solution.py:222
  43.0 0.2 split.1
  43.2 0.8 copy-done.5
  44.0 5.1 %collective-permute-start.1 = (bf16[2048,128]{1,0:T(8,128)(2,1)S(1)}, bf16[2048,128]{1,0:T(8,128)(2,1)S(1)}, u32[]{:S(2)}, u32[]{:S(2)}) collective-permute-start(bf16[2048,128]{1,0:T(8,128)(2,1)S(1)} %get-tuple-element.27.s0), channel_id=1, source_target_pairs={{0,448},{1,449},{2,450},{3,451},{4,452},{5,453},{6,454},{7,455},{8... | collective-permute-start | bytes 1572872 | tf_op jit(solution)/shard_map/ppermute | solution.py:37
  49.1 1.9 %collective-permute-start.2 = (bf16[2048,128]{1,0:T(8,128)(2,1)S(1)}, bf16[2048,128]{1,0:T(8,128)(2,1)S(1)}, u32[]{:S(2)}, u32[]{:S(2)}) collective-permute-start(bf16[2048,128]{1,0:T(8,128)(2,1)S(1)} %get-tuple-element.27.s0), channel_id=1, source_target_pairs={{0,64},{1,65},{2,66},{3,67},{4,68},{5,69},{6,70},{7,71},{8,72},{9,... | collective-permute-start | bytes 1572872 | tf_op jit(solution)/shard_map/ppermute | solution.py:37
  51.0 3.0 %collective-permute-start.3 = (bf16[2048,128]{1,0:T(8,128)(2,1)S(1)}, bf16[2048,128]{1,0:T(8,128)(2,1)S(1)}, u32[]{:S(2)}, u32[]{:S(2)}) collective-permute-start(bf16[2048,128]{1,0:T(8,128)(2,1)S(1)} %get-tuple-element.27.s0), channel_id=1, source_target_pairs={{0,4},{1,5},{2,6},{3,7},{4,8},{5,9},{6,10},{7,11},{8,12},{9,13},{1... | collective-permute-start | bytes 1572872 | tf_op jit(solution)/shard_map/ppermute | solution.py:37
  54.1 5.4 %collective-permute-start.4 = (f32[1,1024]{1,0:T(1,128)S(1)}, f32[1,1024]{1,0:T(1,128)S(1)}, u32[]{:S(2)}, u32[]{:S(2)}) collective-permute-start(f32[1,1024]{1,0:T(1,128)S(1)} %bitcast.20), channel_id=1, source_target_pairs={{0,32},{1,33},{2,34},{3,35},{4,36},{5,37},{6,38},{7,39},{8,40},{9,... | collective-permute-start | bytes 12296 | tf_op jit(solution)/shard_map/ppermute | solution.py:37
  59.5 0.8 collective-permute-done.4.fo
  60.3 0.7 collective-permute-done.2.s3
  61.0 1.9 %collective-permute-done.3.s2 = bf16[2048,128]{1,0:T(8,128)(2,1)S(1)} collective-permute-done((bf16[2048,128]{1,0:T(8,128)(2,1)S(1)}, bf16[2048,128]{1,0:T(8,128)(2,1)S(1)}, u32[]{:S(2)}, u32[]{:S(2)}) %collective-permute-start.3) | collective-permute-done | bytes 524320 | tf_op jit(solution)/shard_map/ppermute | solution.py:37
  63.0 7.4 %collective-permute-start.6 = (bf16[512,1024]{1,0:T(8,128)(2,1)}, bf16[512,1024]{1,0:T(8,128)(2,1)S(1)}, u32[]{:S(2)}, u32[]{:S(2)}) collective-permute-start(bf16[512,1024]{1,0:T(8,128)(2,1)} %collective-permute-done.5.b_in.mr_in), channel_id=1, source_target_pairs={{0,32},{1,33},{2,34},{3,35},{4,36},{5,37},{6,38},{7,39},{8,40},{9,... | collective-permute-start | bytes 3145736 | tf_op jit(solution)/shard_map/ppermute | solution.py:37
  70.4 4.5 %first.1.um = f32[128,512]{1,0:T(8,128)S(1)} custom-call(bf16[512,1024]{1,0:T(8,128)(2,1)S(1)} %bitcast.17, bf16[512,1024]{1,0:T(8,128)(2,1)} %collective-permute-done.5.b_in.mr_in, bf16[2048,128]{1,0:T(8,128)(2,1)S(1)} %get-tuple-element.27.s0, bf16[2048,128]{1,0:T(8,128)(2,1)S(1)} %collective-permute-done.1.s1, ...), custom_call_target="tpu_custom_call" | custom-call | flops 1024 | bytes 1024 | tf_op jit(solution)/shard_map/first/pallas_call | solution.py:251
  74.9 4.4 %second.1 = (f32[2,128,512]{2,1,0:T(8,128)}, bf16[8,16,640]{2,1,0:T(8,128)(2,1)}) custom-call(bf16[512,1024]{1,0:T(8,128)(2,1)S(1)} %collective-permute-done.a_in.ol_in, bf16[512,1024]{1,0:T(8,128)(2,1)S(1)} %collective-permute-done.6.b_in.or_in, bf16[2048,128]{1,0:T(8,128)(2,1)S(1)} %get-tuple-element.27.s0, ...), custom_call_target="tpu_custom_call" | custom-call | flops 1024 | bytes 1024 | tf_op jit(solution)/shard_map/second/pallas_call | solution.py:261
  79.3 5.1 %all-to-all-start.1 = ((bf16[8,16,640]{2,1,0:T(8,128)(2,1)}), bf16[8,16,640]{2,1,0:T(8,128)(2,1)S(1)}, u32[]{:S(2)}, u32[]{:S(2)}) async-start(bf16[8,16,640]{2,1,0:T(8,128)(2,1)} %get-tuple-element.35), calls=%async_computation.1 | async-start | bytes 327680 | tf_op jit(solution)/shard_map/all_to_all | solution.py:278
  84.4 4.6 %collective-permute-start.7 = (bf16[2048,128]{1,0:T(8,128)(2,1)S(1)}, bf16[2048,128]{1,0:T(8,128)(2,1)S(1)}, u32[]{:S(2)}, u32[]{:S(2)}) collective-permute-start(bf16[2048,128]{1,0:T(8,128)(2,1)S(1)} %copy-done.6), channel_id=1, source_target_pairs={{0,448},{1,449},{2,450},{3,451},{4,452},{5,453},{6,454},{7,455},{8... | collective-permute-start | bytes 1572872 | tf_op jit(solution)/shard_map/ppermute | solution.py:37
  89.0 3.1 %collective-permute-start.8 = (bf16[2048,128]{1,0:T(8,128)(2,1)S(1)}, bf16[2048,128]{1,0:T(8,128)(2,1)S(1)}, u32[]{:S(2)}, u32[]{:S(2)}) collective-permute-start(bf16[2048,128]{1,0:T(8,128)(2,1)S(1)} %copy-done.6), channel_id=1, source_target_pairs={{0,28},{1,29},{2,30},{3,31},{4,0},{5,1},{6,2},{7,3},{8,4},{9,5},{1... | collective-permute-start | bytes 1572872 | tf_op jit(solution)/shard_map/ppermute | solution.py:37
  92.1 1.9 %collective-permute-start.9 = (bf16[2048,128]{1,0:T(8,128)(2,1)S(1)}, bf16[2048,128]{1,0:T(8,128)(2,1)S(1)}, u32[]{:S(2)}, u32[]{:S(2)}) collective-permute-start(bf16[2048,128]{1,0:T(8,128)(2,1)S(1)} %copy-done.6), channel_id=1, source_target_pairs={{0,64},{1,65},{2,66},{3,67},{4,68},{5,69},{6,70},{7,71},{8,72},{9,... | collective-permute-start | bytes 1572872 | tf_op jit(solution)/shard_map/ppermute | solution.py:37
  94.1 1.5 %scan.1 = bf16[8,16,512]{2,1,0:T(8,128)(2,1)} custom-call(bf16[8,16,640]{2,1,0:T(8,128)(2,1)S(1)} %all-to-all-done.1.p, f32[128,1024]{1,0:T(8,128)} %bitcast.24), custom_call_target="tpu_custom_call" | custom-call | flops 49999998976 | bytes 1048576 | tf_op jit(solution)/shard_map/scan/pallas_call | solution.py:284
  95.6 5.4 %all-to-all-start.2 = ((bf16[8,16,512]{2,1,0:T(8,128)(2,1)}), bf16[8,16,512]{2,1,0:T(8,128)(2,1)S(1)}, u32[]{:S(2)}, u32[]{:S(2)}) async-start(bf16[8,16,512]{2,1,0:T(8,128)(2,1)} %scan.1), calls=%async_computation.2 | async-start | bytes 262144 | tf_op jit(solution)/shard_map/all_to_all | solution.py:312
  101.0 3.6 %collective-permute-start.11 = (f32[2,128,512]{2,1,0:T(8,128)S(1)}, f32[2,128,512]{2,1,0:T(8,128)S(1)}, u32[]{:S(2)}, u32[]{:S(2)}) collective-permute-start(f32[2,128,512]{2,1,0:T(8,128)S(1)} %copy-done.7), channel_id=1, source_target_pairs={{0,32},{1,33},{2,34},{3,35},{4,36},{5,37},{6,38},{7,39},{8,40},{9,... | collective-permute-start | bytes 1572872 | tf_op jit(solution)/shard_map/ppermute | solution.py:37
  104.7 3.1 %collective-permute-done.9.t3 = bf16[2048,128]{1,0:T(8,128)(2,1)S(1)} collective-permute-done((bf16[2048,128]{1,0:T(8,128)(2,1)S(1)}, bf16[2048,128]{1,0:T(8,128)(2,1)S(1)}, u32[]{:S(2)}, u32[]{:S(2)}) %collective-permute-start.9) | collective-permute-done | bytes 524320 | tf_op jit(solution)/shard_map/ppermute | solution.py:37
  107.8 5.5 %query.1 = (bf16[512,512]{1,0:T(8,128)(2,1)}, bf16[512,512]{1,0:T(8,128)(2,1)}) custom-call(bf16[512,1024]{1,0:T(8,128)(2,1)} %bitcast.13, bf16[512,1024]{1,0:T(8,128)(2,1)} %collective-permute-done.5.b_in.mr_in, bf16[512,1024]{1,0:T(8,128)(2,1)} %copy-done.2, bf16[512,1024]{1,0:T(8,128)(2,1)} %copy-done.3, bf16[2048,128]{1,0:T(8,128)(2,1)S(1)} %copy-done.6, ...), custom_call_target="tpu_custom_call" | custom-call | flops 2147483648 | bytes 7340032 | tf_op jit(solution)/shard_map/query/pallas_call | solution.py:297
  113.3 5.6 %collective-permute-start.10 = (bf16[512,512]{1,0:T(8,128)(2,1)}, bf16[512,512]{1,0:T(8,128)(2,1)S(1)}, u32[]{:S(2)}, u32[]{:S(2)}) collective-permute-start(bf16[512,512]{1,0:T(8,128)(2,1)} %get-tuple-element.42), channel_id=1, source_target_pairs={{0,32},{1,33},{2,34},{3,35},{4,36},{5,37},{6,38},{7,39},{8,40},{9,... | collective-permute-start | bytes 1572872 | tf_op jit(solution)/shard_map/ppermute | solution.py:37
  118.9 1.9 %collective-permute-start.12 = (bf16[128,512]{1,0:T(8,128)(2,1)S(1)}, bf16[128,512]{1,0:T(8,128)(2,1)S(1)}, u32[]{:S(2)}, u32[]{:S(2)}) collective-permute-start(bf16[128,512]{1,0:T(8,128)(2,1)S(1)} %bitcast.18), channel_id=1, source_target_pairs={{0,32},{1,33},{2,34},{3,35},{4,36},{5,37},{6,38},{7,39},{8,40},{9,... | collective-permute-start | bytes 393224 | tf_op jit(solution)/shard_map/ppermute | solution.py:37
  120.9 1.3 %collective-permute-done.12.eo = bf16[128,512]{1,0:T(8,128)(2,1)S(1)} collective-permute-done((bf16[128,512]{1,0:T(8,128)(2,1)S(1)}, bf16[128,512]{1,0:T(8,128)(2,1)S(1)}, u32[]{:S(2)}, u32[]{:S(2)}) %collective-permute-start.12) | collective-permute-done | bytes 131104 | tf_op jit(solution)/shard_map/ppermute | solution.py:37
  122.2 4.9 %read.1 = (bf16[512,1024]{1,0:T(8,128)(2,1)}, f32[128,1024]{1,0:T(8,128)}) custom-call(bf16[512,1024]{1,0:T(8,128)(2,1)} %bitcast.14, bf16[512,512]{1,0:T(8,128)(2,1)} %get-tuple-element.39.qm_in, bf16[512,512]{1,0:T(8,128)(2,1)S(1)} %collective-permute-done.10.qo_in, f32[2,128,512]{2,1,0:T(8,128)} %get-tuple-element.43.um_in, ...), custom_call_target="tpu_custom_call" | custom-call | tf_op jit(solution)/shard_map/read/pallas_call | solution.py:316
  (27 shorter events, 0.1 us)
Async XLA Ops:
  2.6 13.6 %copy-start = (bf16[1,512,1024]{2,1,0:T(8,128)(2,1)S(1)}, bf16[1,512,1024]{2,1,0:T(8,128)(2,1)}, u32[]{:S(2)}) copy-start(bf16[1,512,1024]{2,1,0:T(8,128)(2,1)} %param.6) | copy-start | bytes 3145732
  2.6 40.4 %all-to-all-start = ((bf16[16,128,256]{2,1,0:T(8,128)(2,1)}), bf16[16,128,256]{2,1,0:T(8,128)(2,1)S(1)}, u32[]{:S(2)}, u32[]{:S(2)}) async-start(bf16[16,128,256]{2,1,0:T(8,128)(2,1)} %bitcast.2), calls=%async_computation | async-start | bytes 2097152 | tf_op jit(solution)/shard_map/all_to_all | solution.py:222
  16.2 5.1 %collective-permute-start = (bf16[512,1024]{1,0:T(8,128)(2,1)S(1)}, bf16[512,1024]{1,0:T(8,128)(2,1)S(1)}, u32[]{:S(2)}, u32[]{:S(2)}) collective-permute-start(bf16[512,1024]{1,0:T(8,128)(2,1)S(1)} %bitcast.15), channel_id=1, source_target_pairs={{0,32},{1,33},{2,34},{3,35},{4,36},{5,37},{6,38},{7,39},{8,40},{9,... | collective-permute-start | bytes 3145736 | tf_op jit(solution)/shard_map/ppermute | solution.py:37
  19.1 40.4 %collective-permute-start.5 = (bf16[512,1024]{1,0:T(8,128)(2,1)S(1)}, bf16[512,1024]{1,0:T(8,128)(2,1)}, u32[]{:S(2)}, u32[]{:S(2)}) collective-permute-start(bf16[512,1024]{1,0:T(8,128)(2,1)S(1)} %bitcast.16), channel_id=1, source_target_pairs={{0,1},{1,0},{2,3},{3,2},{4,5},{5,4},{6,7},{7,6},{8,9},{9,8},{10,11... | collective-permute-start | bytes 3145736 | tf_op jit(solution)/shard_map/ppermute | solution.py:37
  21.3 53.6 %copy-start.2 = (bf16[512,1024]{1,0:T(8,128)(2,1)}, bf16[512,1024]{1,0:T(8,128)(2,1)S(1)}, u32[]{:S(2)}) copy-start(bf16[512,1024]{1,0:T(8,128)(2,1)S(1)} %collective-permute-done.a_in.ol_in) | copy-start | bytes 3145732
  43.0 11.0 %copy-start.4 = (f32[1,1,1024]{2,1,0:T(1,128)S(1)}, f32[1,1,1024]{2,1,0:T(1,128)}, u32[]{:S(2)}) copy-start(f32[1,1,1024]{2,1,0:T(1,128)} %param.11) | copy-start | bytes 12292
  43.0 27.4 %copy-start.1 = (bf16[128,1024]{1,0:T(8,128)(2,1)S(1)}, bf16[128,1024]{1,0:T(8,128)(2,1)}, u32[]{:S(2)}) copy-start(bf16[128,1024]{1,0:T(8,128)(2,1)} %lat.3) | copy-start | bytes 786436
  43.2 0.8 copy-start.5
  44.0 16.3 %collective-permute-start.1 = (bf16[2048,128]{1,0:T(8,128)(2,1)S(1)}, bf16[2048,128]{1,0:T(8,128)(2,1)S(1)}, u32[]{:S(2)}, u32[]{:S(2)}) collective-permute-start(bf16[2048,128]{1,0:T(8,128)(2,1)S(1)} %get-tuple-element.27.s0), channel_id=1, source_target_pairs={{0,448},{1,449},{2,450},{3,451},{4,452},{5,453},{6,454},{7,455},{8... | collective-permute-start | bytes 1572872 | tf_op jit(solution)/shard_map/ppermute | solution.py:37
  49.1 11.9 %collective-permute-start.2 = (bf16[2048,128]{1,0:T(8,128)(2,1)S(1)}, bf16[2048,128]{1,0:T(8,128)(2,1)S(1)}, u32[]{:S(2)}, u32[]{:S(2)}) collective-permute-start(bf16[2048,128]{1,0:T(8,128)(2,1)S(1)} %get-tuple-element.27.s0), channel_id=1, source_target_pairs={{0,64},{1,65},{2,66},{3,67},{4,68},{5,69},{6,70},{7,71},{8,72},{9,... | collective-permute-start | bytes 1572872 | tf_op jit(solution)/shard_map/ppermute | solution.py:37
  51.0 11.9 %collective-permute-start.3 = (bf16[2048,128]{1,0:T(8,128)(2,1)S(1)}, bf16[2048,128]{1,0:T(8,128)(2,1)S(1)}, u32[]{:S(2)}, u32[]{:S(2)}) collective-permute-start(bf16[2048,128]{1,0:T(8,128)(2,1)S(1)} %get-tuple-element.27.s0), channel_id=1, source_target_pairs={{0,4},{1,5},{2,6},{3,7},{4,8},{5,9},{6,10},{7,11},{8,12},{9,13},{1... | collective-permute-start | bytes 1572872 | tf_op jit(solution)/shard_map/ppermute | solution.py:37
  54.1 6.2 %collective-permute-start.4 = (f32[1,1024]{1,0:T(1,128)S(1)}, f32[1,1024]{1,0:T(1,128)S(1)}, u32[]{:S(2)}, u32[]{:S(2)}) collective-permute-start(f32[1,1024]{1,0:T(1,128)S(1)} %bitcast.20), channel_id=1, source_target_pairs={{0,32},{1,33},{2,34},{3,35},{4,36},{5,37},{6,38},{7,39},{8,40},{9,... | collective-permute-start | bytes 12296 | tf_op jit(solution)/shard_map/ppermute | solution.py:37
  63.0 12.0 %collective-permute-start.6 = (bf16[512,1024]{1,0:T(8,128)(2,1)}, bf16[512,1024]{1,0:T(8,128)(2,1)S(1)}, u32[]{:S(2)}, u32[]{:S(2)}) collective-permute-start(bf16[512,1024]{1,0:T(8,128)(2,1)} %collective-permute-done.5.b_in.mr_in), channel_id=1, source_target_pairs={{0,32},{1,33},{2,34},{3,35},{4,36},{5,37},{6,38},{7,39},{8,40},{9,... | collective-permute-start | bytes 3145736 | tf_op jit(solution)/shard_map/ppermute | solution.py:37
  74.9 9.5 %copy-start.6 = (bf16[2048,128]{1,0:T(8,128)(2,1)S(1)}, bf16[2048,128]{1,0:T(8,128)(2,1)}, u32[]{:S(2)}) copy-start(bf16[2048,128]{1,0:T(8,128)(2,1)} %copy-done.5) | copy-start | bytes 1572868
  74.9 4.4 %copy-start.3 = (bf16[512,1024]{1,0:T(8,128)(2,1)}, bf16[512,1024]{1,0:T(8,128)(2,1)S(1)}, u32[]{:S(2)}) copy-start(bf16[512,1024]{1,0:T(8,128)(2,1)S(1)} %collective-permute-done.6.b_in.or_in) | copy-start | bytes 3145732
  79.3 14.7 %all-to-all-start.1 = ((bf16[8,16,640]{2,1,0:T(8,128)(2,1)}), bf16[8,16,640]{2,1,0:T(8,128)(2,1)S(1)}, u32[]{:S(2)}, u32[]{:S(2)}) async-start(bf16[8,16,640]{2,1,0:T(8,128)(2,1)} %get-tuple-element.35), calls=%async_computation.1 | async-start | bytes 327680 | tf_op jit(solution)/shard_map/all_to_all | solution.py:278
  84.4 20.2 %collective-permute-start.7 = (bf16[2048,128]{1,0:T(8,128)(2,1)S(1)}, bf16[2048,128]{1,0:T(8,128)(2,1)S(1)}, u32[]{:S(2)}, u32[]{:S(2)}) collective-permute-start(bf16[2048,128]{1,0:T(8,128)(2,1)S(1)} %copy-done.6), channel_id=1, source_target_pairs={{0,448},{1,449},{2,450},{3,451},{4,452},{5,453},{6,454},{7,455},{8... | collective-permute-start | bytes 1572872 | tf_op jit(solution)/shard_map/ppermute | solution.py:37
  89.0 15.7 %collective-permute-start.8 = (bf16[2048,128]{1,0:T(8,128)(2,1)S(1)}, bf16[2048,128]{1,0:T(8,128)(2,1)S(1)}, u32[]{:S(2)}, u32[]{:S(2)}) collective-permute-start(bf16[2048,128]{1,0:T(8,128)(2,1)S(1)} %copy-done.6), channel_id=1, source_target_pairs={{0,28},{1,29},{2,30},{3,31},{4,0},{5,1},{6,2},{7,3},{8,4},{9,5},{1... | collective-permute-start | bytes 1572872 | tf_op jit(solution)/shard_map/ppermute | solution.py:37
  92.1 15.7 %collective-permute-start.9 = (bf16[2048,128]{1,0:T(8,128)(2,1)S(1)}, bf16[2048,128]{1,0:T(8,128)(2,1)S(1)}, u32[]{:S(2)}, u32[]{:S(2)}) collective-permute-start(bf16[2048,128]{1,0:T(8,128)(2,1)S(1)} %copy-done.6), channel_id=1, source_target_pairs={{0,64},{1,65},{2,66},{3,67},{4,68},{5,69},{6,70},{7,71},{8,72},{9,... | collective-permute-start | bytes 1572872 | tf_op jit(solution)/shard_map/ppermute | solution.py:37
  94.1 7.0 %copy-start.7 = (f32[2,128,512]{2,1,0:T(8,128)S(1)}, f32[2,128,512]{2,1,0:T(8,128)}, u32[]{:S(2)}) copy-start(f32[2,128,512]{2,1,0:T(8,128)} %get-tuple-element.43.um_in) | copy-start | bytes 1572868
  95.6 17.7 %all-to-all-start.2 = ((bf16[8,16,512]{2,1,0:T(8,128)(2,1)}), bf16[8,16,512]{2,1,0:T(8,128)(2,1)S(1)}, u32[]{:S(2)}, u32[]{:S(2)}) async-start(bf16[8,16,512]{2,1,0:T(8,128)(2,1)} %scan.1), calls=%async_computation.2 | async-start | bytes 262144 | tf_op jit(solution)/shard_map/all_to_all | solution.py:312
  101.0 19.8 %collective-permute-start.11 = (f32[2,128,512]{2,1,0:T(8,128)S(1)}, f32[2,128,512]{2,1,0:T(8,128)S(1)}, u32[]{:S(2)}, u32[]{:S(2)}) collective-permute-start(f32[2,128,512]{2,1,0:T(8,128)S(1)} %copy-done.7), channel_id=1, source_target_pairs={{0,32},{1,33},{2,34},{3,35},{4,36},{5,37},{6,38},{7,39},{8,40},{9,... | collective-permute-start | bytes 1572872 | tf_op jit(solution)/shard_map/ppermute | solution.py:37
  113.3 8.9 %collective-permute-start.10 = (bf16[512,512]{1,0:T(8,128)(2,1)}, bf16[512,512]{1,0:T(8,128)(2,1)S(1)}, u32[]{:S(2)}, u32[]{:S(2)}) collective-permute-start(bf16[512,512]{1,0:T(8,128)(2,1)} %get-tuple-element.42), channel_id=1, source_target_pairs={{0,32},{1,33},{2,34},{3,35},{4,36},{5,37},{6,38},{7,39},{8,40},{9,... | collective-permute-start | bytes 1572872 | tf_op jit(solution)/shard_map/ppermute | solution.py:37
  118.9 3.2 %collective-permute-start.12 = (bf16[128,512]{1,0:T(8,128)(2,1)S(1)}, bf16[128,512]{1,0:T(8,128)(2,1)S(1)}, u32[]{:S(2)}, u32[]{:S(2)}) collective-permute-start(bf16[128,512]{1,0:T(8,128)(2,1)S(1)} %bitcast.18), channel_id=1, source_target_pairs={{0,32},{1,33},{2,34},{3,35},{4,36},{5,37},{6,38},{7,39},{8,40},{9,... | collective-permute-start | bytes 393224 | tf_op jit(solution)/shard_map/ppermute | solution.py:37

commit v5 on v4

--- a/solution.py
+++ b/solution.py
@@ -147,7 +147,7 @@
 
 
 def query_kernel(
-    ml_in, mr_in, ol_in, or_in, t0, t1, t2, t3, qm_out, qo_out, w, ml, mr, ol, orr, qm, qo, sems
+    ml_in, mr_in, ol_in, or_in, t0, t1, t3, t2, qm_out, qo_out, w, ml, mr, ol, orr, qm, qo, sems
 ):
     rest = [(ol_in, ol), (or_in, orr), (ml_in, ml), (mr_in, mr)]
     copies = fetch(columns_of(w, (t0, t1, t2, t3)) + rest, sems)
@@ -308,7 +308,7 @@
             flops=2 * 1024 * 2048 * 512, bytes_accessed=7 << 20, transcendentals=0
         ),
         name="query",
-    )(*in_hbm(mine_l, mine_r, other_l, other_r), t0, t1, t2, t3)
+    )(*in_hbm(mine_l, mine_r, other_l, other_r), t0, t1, t3, t2)
     e = lax.all_to_all(entered, "y", 0, 0, tiled=True).reshape(M, QUART)
     e_other = to_core(e)
     q_late, e_late = tie((queries[1], e))

time: 128 us -> 124 us (0.969)
  waiting for transfers between devices: 29.6 us -> 27.2 us
  starting transfers between devices: 72.8 us -> 71.4 us
    ppermute x13, waiting for transfers between devices: 7.93 us -> 5.57 us  [sent(): return lax.ppermute(x, AXES, pairs)]
    ppermute x13, starting transfers between devices: 48.7 us -> 47.3 us  [sent(): return lax.ppermute(x, AXES, pairs)]
  transfers between devices with their start and end apart: 16 -> 16, of which waited for: 6 -> 7; matrix products, arithmetic and copies ran while one was open for 0% -> 0% of each run, Pallas kernels for 9% -> 9%
where the time goes in v5:
time: 124 us; the launch traced here: 123 us
  starting transfers between devices  71.4 us (58%)
  waiting for transfers between devices  27.2 us (22%)
  Pallas kernels  20.9 us (17%)
  local copies, waits for them, and re-layouts  2.71 us (2%)
    ppermute x13, starting transfers between devices, sent(): return lax.ppermute(x, AXES, pairs)  47.3 us
    all_to_all x1, waiting for transfers between devices, shards(): lax.all_to_all(out, ('z', 'h'), 0, 0, tiled=True).reshape(2048, 2 * HEAD)  21.7 us
    all_to_all x1, starting transfers between devices, shards(): lax.all_to_all(out, ('z', 'h'), 0, 0, tiled=True).reshape(2048, 2 * HEAD)  13.6 us
    ppermute x13, waiting for transfers between devices, sent(): return lax.ppermute(x, AXES, pairs)  5.57 us
    pallas_call x1, Pallas kernels, shards(): pl.pallas_call(query_kernel, out_shape=(pltpu.HBM((TOK, QUART), BF),) * 2...  5.45 us
    all_to_all x1, starting transfers between devices, shards(): e = lax.all_to_all(entered, 'y', 0, 0, tiled=True).reshape(M, QUART)  5.44 us
    all_to_all x1, starting transfers between devices, shards(): arrived = lax.all_to_all(packed, 'y', 0, 0, tiled=True)  5.11 us
    pallas_call x1, Pallas kernels, shards(): pl.pallas_call(read_kernel, out_shape=(jax.ShapeDtypeStruct((TOK, HALF),...  4.88 us
  transfers between devices with their start and end apart: 16, of which 7 were waited for; matrix products, arithmetic and copies ran while one was open for 0% of the time, Pallas kernels for 9%

profile of v5, /device:TPU:1, one launch (start us, length us, event | category | flops | bytes accessed | tf_op | source)
XLA Modules:
  0.0 123.2 jit_solution(4923722151330260713)
XLA Ops:
  0.7 0.8 constant_dynamic-slice_fusion.2
  1.6 1.1 broadcast_in_dim.12
  2.6 13.6 %all-to-all-start = ((bf16[16,128,256]{2,1,0:T(8,128)(2,1)}), bf16[16,128,256]{2,1,0:T(8,128)(2,1)S(1)}, u32[]{:S(2)}, u32[]{:S(2)}) async-start(bf16[16,128,256]{2,1,0:T(8,128)(2,1)} %bitcast.2), calls=%async_computation | async-start | bytes 2097152 | tf_op jit(solution)/shard_map/all_to_all | solution.py:222
  16.2 2.9 %collective-permute-start = (bf16[512,1024]{1,0:T(8,128)(2,1)S(1)}, bf16[512,1024]{1,0:T(8,128)(2,1)S(1)}, u32[]{:S(2)}, u32[]{:S(2)}) collective-permute-start(bf16[512,1024]{1,0:T(8,128)(2,1)S(1)} %bitcast.15), channel_id=1, source_target_pairs={{0,32},{1,33},{2,34},{3,35},{4,36},{5,37},{6,38},{7,39},{8,40},{9,... | collective-permute-start | bytes 3145736 | tf_op jit(solution)/shard_map/ppermute | solution.py:37
  19.1 2.2 %collective-permute-start.5 = (bf16[512,1024]{1,0:T(8,128)(2,1)S(1)}, bf16[512,1024]{1,0:T(8,128)(2,1)}, u32[]{:S(2)}, u32[]{:S(2)}) collective-permute-start(bf16[512,1024]{1,0:T(8,128)(2,1)S(1)} %bitcast.16), channel_id=1, source_target_pairs={{0,1},{1,0},{2,3},{3,2},{4,5},{5,4},{6,7},{7,6},{8,9},{9,8},{10,11... | collective-permute-start | bytes 3145736 | tf_op jit(solution)/shard_map/ppermute | solution.py:37
  21.3 21.7 %all-to-all-done = bf16[16,128,256]{2,1,0:T(8,128)(2,1)S(1)} async-done(((bf16[16,128,256]{2,1,0:T(8,128)(2,1)}), bf16[16,128,256]{2,1,0:T(8,128)(2,1)S(1)}, u32[]{:S(2)}, u32[]{:S(2)}) %all-to-all-start) | async-done | bytes 1048608 | tf_op jit(solution)/shard_map/all_to_all | solution.py:222
  43.0 0.2 split.1
  43.2 0.8 copy-done.5
  44.0 5.1 %collective-permute-start.1 = (bf16[2048,128]{1,0:T(8,128)(2,1)S(1)}, bf16[2048,128]{1,0:T(8,128)(2,1)S(1)}, u32[]{:S(2)}, u32[]{:S(2)}) collective-permute-start(bf16[2048,128]{1,0:T(8,128)(2,1)S(1)} %get-tuple-element.27.s0), channel_id=1, source_target_pairs={{0,448},{1,449},{2,450},{3,451},{4,452},{5,453},{6,454},{7,455},{8... | collective-permute-start | bytes 1572872 | tf_op jit(solution)/shard_map/ppermute | solution.py:37
  49.1 1.9 %collective-permute-start.2 = (bf16[2048,128]{1,0:T(8,128)(2,1)S(1)}, bf16[2048,128]{1,0:T(8,128)(2,1)S(1)}, u32[]{:S(2)}, u32[]{:S(2)}) collective-permute-start(bf16[2048,128]{1,0:T(8,128)(2,1)S(1)} %get-tuple-element.27.s0), channel_id=1, source_target_pairs={{0,64},{1,65},{2,66},{3,67},{4,68},{5,69},{6,70},{7,71},{8,72},{9,... | collective-permute-start | bytes 1572872 | tf_op jit(solution)/shard_map/ppermute | solution.py:37
  51.0 3.0 %collective-permute-start.3 = (bf16[2048,128]{1,0:T(8,128)(2,1)S(1)}, bf16[2048,128]{1,0:T(8,128)(2,1)S(1)}, u32[]{:S(2)}, u32[]{:S(2)}) collective-permute-start(bf16[2048,128]{1,0:T(8,128)(2,1)S(1)} %get-tuple-element.27.s0), channel_id=1, source_target_pairs={{0,4},{1,5},{2,6},{3,7},{4,8},{5,9},{6,10},{7,11},{8,12},{9,13},{1... | collective-permute-start | bytes 1572872 | tf_op jit(solution)/shard_map/ppermute | solution.py:37
  54.1 5.4 %collective-permute-start.4 = (f32[1,1024]{1,0:T(1,128)S(1)}, f32[1,1024]{1,0:T(1,128)S(1)}, u32[]{:S(2)}, u32[]{:S(2)}) collective-permute-start(f32[1,1024]{1,0:T(1,128)S(1)} %bitcast.20), channel_id=1, source_target_pairs={{0,32},{1,33},{2,34},{3,35},{4,36},{5,37},{6,38},{7,39},{8,40},{9,... | collective-permute-start | bytes 12296 | tf_op jit(solution)/shard_map/ppermute | solution.py:37
  59.5 0.8 collective-permute-done.4.fo
  60.3 0.7 collective-permute-done.2.s3
  61.0 1.9 %collective-permute-done.3.s2 = bf16[2048,128]{1,0:T(8,128)(2,1)S(1)} collective-permute-done((bf16[2048,128]{1,0:T(8,128)(2,1)S(1)}, bf16[2048,128]{1,0:T(8,128)(2,1)S(1)}, u32[]{:S(2)}, u32[]{:S(2)}) %collective-permute-start.3) | collective-permute-done | bytes 524320 | tf_op jit(solution)/shard_map/ppermute | solution.py:37
  63.0 7.4 %collective-permute-start.6 = (bf16[512,1024]{1,0:T(8,128)(2,1)}, bf16[512,1024]{1,0:T(8,128)(2,1)S(1)}, u32[]{:S(2)}, u32[]{:S(2)}) collective-permute-start(bf16[512,1024]{1,0:T(8,128)(2,1)} %collective-permute-done.5.b_in.mr_in), channel_id=1, source_target_pairs={{0,32},{1,33},{2,34},{3,35},{4,36},{5,37},{6,38},{7,39},{8,40},{9,... | collective-permute-start | bytes 3145736 | tf_op jit(solution)/shard_map/ppermute | solution.py:37
  70.4 4.5 %first.1.um = f32[128,512]{1,0:T(8,128)S(1)} custom-call(bf16[512,1024]{1,0:T(8,128)(2,1)S(1)} %bitcast.17, bf16[512,1024]{1,0:T(8,128)(2,1)} %collective-permute-done.5.b_in.mr_in, bf16[2048,128]{1,0:T(8,128)(2,1)S(1)} %get-tuple-element.27.s0, bf16[2048,128]{1,0:T(8,128)(2,1)S(1)} %collective-permute-done.1.s1, ...), custom_call_target="tpu_custom_call" | custom-call | flops 1024 | bytes 1024 | tf_op jit(solution)/shard_map/first/pallas_call | solution.py:251
  74.9 4.4 %second.1 = (f32[2,128,512]{2,1,0:T(8,128)}, bf16[8,16,640]{2,1,0:T(8,128)(2,1)}) custom-call(bf16[512,1024]{1,0:T(8,128)(2,1)S(1)} %collective-permute-done.a_in.ol_in, bf16[512,1024]{1,0:T(8,128)(2,1)S(1)} %collective-permute-done.6.b_in.or_in, bf16[2048,128]{1,0:T(8,128)(2,1)S(1)} %get-tuple-element.27.s0, ...), custom_call_target="tpu_custom_call" | custom-call | flops 1024 | bytes 1024 | tf_op jit(solution)/shard_map/second/pallas_call | solution.py:261
  79.3 5.1 %all-to-all-start.1 = ((bf16[8,16,640]{2,1,0:T(8,128)(2,1)}), bf16[8,16,640]{2,1,0:T(8,128)(2,1)S(1)}, u32[]{:S(2)}, u32[]{:S(2)}) async-start(bf16[8,16,640]{2,1,0:T(8,128)(2,1)} %get-tuple-element.35), calls=%async_computation.1 | async-start | bytes 327680 | tf_op jit(solution)/shard_map/all_to_all | solution.py:278
  84.4 4.6 %collective-permute-start.7 = (bf16[2048,128]{1,0:T(8,128)(2,1)S(1)}, bf16[2048,128]{1,0:T(8,128)(2,1)S(1)}, u32[]{:S(2)}, u32[]{:S(2)}) collective-permute-start(bf16[2048,128]{1,0:T(8,128)(2,1)S(1)} %copy-done.6), channel_id=1, source_target_pairs={{0,448},{1,449},{2,450},{3,451},{4,452},{5,453},{6,454},{7,455},{8... | collective-permute-start | bytes 1572872 | tf_op jit(solution)/shard_map/ppermute | solution.py:37
  89.0 1.9 %collective-permute-start.8 = (bf16[2048,128]{1,0:T(8,128)(2,1)S(1)}, bf16[2048,128]{1,0:T(8,128)(2,1)S(1)}, u32[]{:S(2)}, u32[]{:S(2)}) collective-permute-start(bf16[2048,128]{1,0:T(8,128)(2,1)S(1)} %copy-done.6), channel_id=1, source_target_pairs={{0,64},{1,65},{2,66},{3,67},{4,68},{5,69},{6,70},{7,71},{8,72},{9,... | collective-permute-start | bytes 1572872 | tf_op jit(solution)/shard_map/ppermute | solution.py:37
  91.0 3.1 %collective-permute-start.9 = (bf16[2048,128]{1,0:T(8,128)(2,1)S(1)}, bf16[2048,128]{1,0:T(8,128)(2,1)S(1)}, u32[]{:S(2)}, u32[]{:S(2)}) collective-permute-start(bf16[2048,128]{1,0:T(8,128)(2,1)S(1)} %copy-done.6), channel_id=1, source_target_pairs={{0,28},{1,29},{2,30},{3,31},{4,0},{5,1},{6,2},{7,3},{8,4},{9,5},{1... | collective-permute-start | bytes 1572872 | tf_op jit(solution)/shard_map/ppermute | solution.py:37
  94.1 1.5 %scan.1 = bf16[8,16,512]{2,1,0:T(8,128)(2,1)} custom-call(bf16[8,16,640]{2,1,0:T(8,128)(2,1)S(1)} %all-to-all-done.1.p, f32[128,1024]{1,0:T(8,128)} %bitcast.24), custom_call_target="tpu_custom_call" | custom-call | flops 49999998976 | bytes 1048576 | tf_op jit(solution)/shard_map/scan/pallas_call | solution.py:284
  95.6 5.4 %all-to-all-start.2 = ((bf16[8,16,512]{2,1,0:T(8,128)(2,1)}), bf16[8,16,512]{2,1,0:T(8,128)(2,1)S(1)}, u32[]{:S(2)}, u32[]{:S(2)}) async-start(bf16[8,16,512]{2,1,0:T(8,128)(2,1)} %scan.1), calls=%async_computation.2 | async-start | bytes 262144 | tf_op jit(solution)/shard_map/all_to_all | solution.py:312
  101.0 3.6 %collective-permute-start.11 = (f32[2,128,512]{2,1,0:T(8,128)S(1)}, f32[2,128,512]{2,1,0:T(8,128)S(1)}, u32[]{:S(2)}, u32[]{:S(2)}) collective-permute-start(f32[2,128,512]{2,1,0:T(8,128)S(1)} %copy-done.7), channel_id=1, source_target_pairs={{0,32},{1,33},{2,34},{3,35},{4,36},{5,37},{6,38},{7,39},{8,40},{9,... | collective-permute-start | bytes 1572872 | tf_op jit(solution)/shard_map/ppermute | solution.py:37
  104.7 0.1 collective-permute-done.8.t3
  104.8 0.6 collective-permute-done.9.t2
  105.4 5.5 %query.1 = (bf16[512,512]{1,0:T(8,128)(2,1)}, bf16[512,512]{1,0:T(8,128)(2,1)}) custom-call(bf16[512,1024]{1,0:T(8,128)(2,1)} %bitcast.13, bf16[512,1024]{1,0:T(8,128)(2,1)} %collective-permute-done.5.b_in.mr_in, bf16[512,1024]{1,0:T(8,128)(2,1)} %copy-done.2, bf16[512,1024]{1,0:T(8,128)(2,1)} %copy-done.3, bf16[2048,128]{1,0:T(8,128)(2,1)S(1)} %copy-done.6, ...), custom_call_target="tpu_custom_call" | custom-call | flops 2147483648 | bytes 7340032 | tf_op jit(solution)/shard_map/query/pallas_call | solution.py:297
  110.9 4.2 %collective-permute-start.10 = (bf16[512,512]{1,0:T(8,128)(2,1)}, bf16[512,512]{1,0:T(8,128)(2,1)S(1)}, u32[]{:S(2)}, u32[]{:S(2)}) collective-permute-start(bf16[512,512]{1,0:T(8,128)(2,1)} %get-tuple-element.42), channel_id=1, source_target_pairs={{0,32},{1,33},{2,34},{3,35},{4,36},{5,37},{6,38},{7,39},{8,40},{9,... | collective-permute-start | bytes 1572872 | tf_op jit(solution)/shard_map/ppermute | solution.py:37
  115.1 1.9 %collective-permute-start.12 = (bf16[128,512]{1,0:T(8,128)(2,1)S(1)}, bf16[128,512]{1,0:T(8,128)(2,1)S(1)}, u32[]{:S(2)}, u32[]{:S(2)}) collective-permute-start(bf16[128,512]{1,0:T(8,128)(2,1)S(1)} %bitcast.18), channel_id=1, source_target_pairs={{0,32},{1,33},{2,34},{3,35},{4,36},{5,37},{6,38},{7,39},{8,40},{9,... | collective-permute-start | bytes 393224 | tf_op jit(solution)/shard_map/ppermute | solution.py:37
  117.1 1.3 %collective-permute-done.12.eo = bf16[128,512]{1,0:T(8,128)(2,1)S(1)} collective-permute-done((bf16[128,512]{1,0:T(8,128)(2,1)S(1)}, bf16[128,512]{1,0:T(8,128)(2,1)S(1)}, u32[]{:S(2)}, u32[]{:S(2)}) %collective-permute-start.12) | collective-permute-done | bytes 131104 | tf_op jit(solution)/shard_map/ppermute | solution.py:37
  118.4 4.9 %read.1 = (bf16[512,1024]{1,0:T(8,128)(2,1)}, f32[128,1024]{1,0:T(8,128)}) custom-call(bf16[512,1024]{1,0:T(8,128)(2,1)} %bitcast.14, bf16[512,512]{1,0:T(8,128)(2,1)} %get-tuple-element.39.qm_in, bf16[512,512]{1,0:T(8,128)(2,1)S(1)} %collective-permute-done.10.qo_in, f32[2,128,512]{2,1,0:T(8,128)} %get-tuple-element.43.um_in, ...), custom_call_target="tpu_custom_call" | custom-call | tf_op jit(solution)/shard_map/read/pallas_call | solution.py:316
  (27 shorter events, 0.1 us)
Async XLA Ops:
  2.6 13.6 %copy-start = (bf16[1,512,1024]{2,1,0:T(8,128)(2,1)S(1)}, bf16[1,512,1024]{2,1,0:T(8,128)(2,1)}, u32[]{:S(2)}) copy-start(bf16[1,512,1024]{2,1,0:T(8,128)(2,1)} %param.6) | copy-start | bytes 3145732
  2.6 40.4 %all-to-all-start = ((bf16[16,128,256]{2,1,0:T(8,128)(2,1)}), bf16[16,128,256]{2,1,0:T(8,128)(2,1)S(1)}, u32[]{:S(2)}, u32[]{:S(2)}) async-start(bf16[16,128,256]{2,1,0:T(8,128)(2,1)} %bitcast.2), calls=%async_computation | async-start | bytes 2097152 | tf_op jit(solution)/shard_map/all_to_all | solution.py:222
  16.2 5.1 %collective-permute-start = (bf16[512,1024]{1,0:T(8,128)(2,1)S(1)}, bf16[512,1024]{1,0:T(8,128)(2,1)S(1)}, u32[]{:S(2)}, u32[]{:S(2)}) collective-permute-start(bf16[512,1024]{1,0:T(8,128)(2,1)S(1)} %bitcast.15), channel_id=1, source_target_pairs={{0,32},{1,33},{2,34},{3,35},{4,36},{5,37},{6,38},{7,39},{8,40},{9,... | collective-permute-start | bytes 3145736 | tf_op jit(solution)/shard_map/ppermute | solution.py:37
  19.1 40.4 %collective-permute-start.5 = (bf16[512,1024]{1,0:T(8,128)(2,1)S(1)}, bf16[512,1024]{1,0:T(8,128)(2,1)}, u32[]{:S(2)}, u32[]{:S(2)}) collective-permute-start(bf16[512,1024]{1,0:T(8,128)(2,1)S(1)} %bitcast.16), channel_id=1, source_target_pairs={{0,1},{1,0},{2,3},{3,2},{4,5},{5,4},{6,7},{7,6},{8,9},{9,8},{10,11... | collective-permute-start | bytes 3145736 | tf_op jit(solution)/shard_map/ppermute | solution.py:37
  21.3 53.6 %copy-start.2 = (bf16[512,1024]{1,0:T(8,128)(2,1)}, bf16[512,1024]{1,0:T(8,128)(2,1)S(1)}, u32[]{:S(2)}) copy-start(bf16[512,1024]{1,0:T(8,128)(2,1)S(1)} %collective-permute-done.a_in.ol_in) | copy-start | bytes 3145732
  43.0 11.0 %copy-start.4 = (f32[1,1,1024]{2,1,0:T(1,128)S(1)}, f32[1,1,1024]{2,1,0:T(1,128)}, u32[]{:S(2)}) copy-start(f32[1,1,1024]{2,1,0:T(1,128)} %param.11) | copy-start | bytes 12292
  43.0 27.4 %copy-start.1 = (bf16[128,1024]{1,0:T(8,128)(2,1)S(1)}, bf16[128,1024]{1,0:T(8,128)(2,1)}, u32[]{:S(2)}) copy-start(bf16[128,1024]{1,0:T(8,128)(2,1)} %lat.3) | copy-start | bytes 786436
  43.2 0.8 copy-start.5
  44.0 16.3 %collective-permute-start.1 = (bf16[2048,128]{1,0:T(8,128)(2,1)S(1)}, bf16[2048,128]{1,0:T(8,128)(2,1)S(1)}, u32[]{:S(2)}, u32[]{:S(2)}) collective-permute-start(bf16[2048,128]{1,0:T(8,128)(2,1)S(1)} %get-tuple-element.27.s0), channel_id=1, source_target_pairs={{0,448},{1,449},{2,450},{3,451},{4,452},{5,453},{6,454},{7,455},{8... | collective-permute-start | bytes 1572872 | tf_op jit(solution)/shard_map/ppermute | solution.py:37
  49.1 11.9 %collective-permute-start.2 = (bf16[2048,128]{1,0:T(8,128)(2,1)S(1)}, bf16[2048,128]{1,0:T(8,128)(2,1)S(1)}, u32[]{:S(2)}, u32[]{:S(2)}) collective-permute-start(bf16[2048,128]{1,0:T(8,128)(2,1)S(1)} %get-tuple-element.27.s0), channel_id=1, source_target_pairs={{0,64},{1,65},{2,66},{3,67},{4,68},{5,69},{6,70},{7,71},{8,72},{9,... | collective-permute-start | bytes 1572872 | tf_op jit(solution)/shard_map/ppermute | solution.py:37
  51.0 11.9 %collective-permute-start.3 = (bf16[2048,128]{1,0:T(8,128)(2,1)S(1)}, bf16[2048,128]{1,0:T(8,128)(2,1)S(1)}, u32[]{:S(2)}, u32[]{:S(2)}) collective-permute-start(bf16[2048,128]{1,0:T(8,128)(2,1)S(1)} %get-tuple-element.27.s0), channel_id=1, source_target_pairs={{0,4},{1,5},{2,6},{3,7},{4,8},{5,9},{6,10},{7,11},{8,12},{9,13},{1... | collective-permute-start | bytes 1572872 | tf_op jit(solution)/shard_map/ppermute | solution.py:37
  54.1 6.2 %collective-permute-start.4 = (f32[1,1024]{1,0:T(1,128)S(1)}, f32[1,1024]{1,0:T(1,128)S(1)}, u32[]{:S(2)}, u32[]{:S(2)}) collective-permute-start(f32[1,1024]{1,0:T(1,128)S(1)} %bitcast.20), channel_id=1, source_target_pairs={{0,32},{1,33},{2,34},{3,35},{4,36},{5,37},{6,38},{7,39},{8,40},{9,... | collective-permute-start | bytes 12296 | tf_op jit(solution)/shard_map/ppermute | solution.py:37
  63.0 12.0 %collective-permute-start.6 = (bf16[512,1024]{1,0:T(8,128)(2,1)}, bf16[512,1024]{1,0:T(8,128)(2,1)S(1)}, u32[]{:S(2)}, u32[]{:S(2)}) collective-permute-start(bf16[512,1024]{1,0:T(8,128)(2,1)} %collective-permute-done.5.b_in.mr_in), channel_id=1, source_target_pairs={{0,32},{1,33},{2,34},{3,35},{4,36},{5,37},{6,38},{7,39},{8,40},{9,... | collective-permute-start | bytes 3145736 | tf_op jit(solution)/shard_map/ppermute | solution.py:37
  74.9 9.5 %copy-start.6 = (bf16[2048,128]{1,0:T(8,128)(2,1)S(1)}, bf16[2048,128]{1,0:T(8,128)(2,1)}, u32[]{:S(2)}) copy-start(bf16[2048,128]{1,0:T(8,128)(2,1)} %copy-done.5) | copy-start | bytes 1572868
  74.9 4.4 %copy-start.3 = (bf16[512,1024]{1,0:T(8,128)(2,1)}, bf16[512,1024]{1,0:T(8,128)(2,1)S(1)}, u32[]{:S(2)}) copy-start(bf16[512,1024]{1,0:T(8,128)(2,1)S(1)} %collective-permute-done.6.b_in.or_in) | copy-start | bytes 3145732
  79.3 14.7 %all-to-all-start.1 = ((bf16[8,16,640]{2,1,0:T(8,128)(2,1)}), bf16[8,16,640]{2,1,0:T(8,128)(2,1)S(1)}, u32[]{:S(2)}, u32[]{:S(2)}) async-start(bf16[8,16,640]{2,1,0:T(8,128)(2,1)} %get-tuple-element.35), calls=%async_computation.1 | async-start | bytes 327680 | tf_op jit(solution)/shard_map/all_to_all | solution.py:278
  84.4 20.2 %collective-permute-start.7 = (bf16[2048,128]{1,0:T(8,128)(2,1)S(1)}, bf16[2048,128]{1,0:T(8,128)(2,1)S(1)}, u32[]{:S(2)}, u32[]{:S(2)}) collective-permute-start(bf16[2048,128]{1,0:T(8,128)(2,1)S(1)} %copy-done.6), channel_id=1, source_target_pairs={{0,448},{1,449},{2,450},{3,451},{4,452},{5,453},{6,454},{7,455},{8... | collective-permute-start | bytes 1572872 | tf_op jit(solution)/shard_map/ppermute | solution.py:37
  89.0 15.8 %collective-permute-start.8 = (bf16[2048,128]{1,0:T(8,128)(2,1)S(1)}, bf16[2048,128]{1,0:T(8,128)(2,1)S(1)}, u32[]{:S(2)}, u32[]{:S(2)}) collective-permute-start(bf16[2048,128]{1,0:T(8,128)(2,1)S(1)} %copy-done.6), channel_id=1, source_target_pairs={{0,64},{1,65},{2,66},{3,67},{4,68},{5,69},{6,70},{7,71},{8,72},{9,... | collective-permute-start | bytes 1572872 | tf_op jit(solution)/shard_map/ppermute | solution.py:37
  91.0 14.5 %collective-permute-start.9 = (bf16[2048,128]{1,0:T(8,128)(2,1)S(1)}, bf16[2048,128]{1,0:T(8,128)(2,1)S(1)}, u32[]{:S(2)}, u32[]{:S(2)}) collective-permute-start(bf16[2048,128]{1,0:T(8,128)(2,1)S(1)} %copy-done.6), channel_id=1, source_target_pairs={{0,28},{1,29},{2,30},{3,31},{4,0},{5,1},{6,2},{7,3},{8,4},{9,5},{1... | collective-permute-start | bytes 1572872 | tf_op jit(solution)/shard_map/ppermute | solution.py:37
  94.1 7.0 %copy-start.7 = (f32[2,128,512]{2,1,0:T(8,128)S(1)}, f32[2,128,512]{2,1,0:T(8,128)}, u32[]{:S(2)}) copy-start(f32[2,128,512]{2,1,0:T(8,128)} %get-tuple-element.43.um_in) | copy-start | bytes 1572868
  95.6 15.3 %all-to-all-start.2 = ((bf16[8,16,512]{2,1,0:T(8,128)(2,1)}), bf16[8,16,512]{2,1,0:T(8,128)(2,1)S(1)}, u32[]{:S(2)}, u32[]{:S(2)}) async-start(bf16[8,16,512]{2,1,0:T(8,128)(2,1)} %scan.1), calls=%async_computation.2 | async-start | bytes 262144 | tf_op jit(solution)/shard_map/all_to_all | solution.py:312
  101.0 16.0 %collective-permute-start.11 = (f32[2,128,512]{2,1,0:T(8,128)S(1)}, f32[2,128,512]{2,1,0:T(8,128)S(1)}, u32[]{:S(2)}, u32[]{:S(2)}) collective-permute-start(f32[2,128,512]{2,1,0:T(8,128)S(1)} %copy-done.7), channel_id=1, source_target_pairs={{0,32},{1,33},{2,34},{3,35},{4,36},{5,37},{6,38},{7,39},{8,40},{9,... | collective-permute-start | bytes 1572872 | tf_op jit(solution)/shard_map/ppermute | solution.py:37
  110.9 7.5 %collective-permute-start.10 = (bf16[512,512]{1,0:T(8,128)(2,1)}, bf16[512,512]{1,0:T(8,128)(2,1)S(1)}, u32[]{:S(2)}, u32[]{:S(2)}) collective-permute-start(bf16[512,512]{1,0:T(8,128)(2,1)} %get-tuple-element.42), channel_id=1, source_target_pairs={{0,32},{1,33},{2,34},{3,35},{4,36},{5,37},{6,38},{7,39},{8,40},{9,... | collective-permute-start | bytes 1572872 | tf_op jit(solution)/shard_map/ppermute | solution.py:37
  115.1 3.2 %collective-permute-start.12 = (bf16[128,512]{1,0:T(8,128)(2,1)S(1)}, bf16[128,512]{1,0:T(8,128)(2,1)S(1)}, u32[]{:S(2)}, u32[]{:S(2)}) collective-permute-start(bf16[128,512]{1,0:T(8,128)(2,1)S(1)} %bitcast.18), channel_id=1, source_target_pairs={{0,32},{1,33},{2,34},{3,35},{4,36},{5,37},{6,38},{7,39},{8,40},{9,... | collective-permute-start | bytes 393224 | tf_op jit(solution)/shard_map/ppermute | solution.py:37
